TPU v7x, 32 devices: a whole 2x2x4 slice. The times are simulated.
32 devices in a mesh: parts: 2 (over y), space: 16 (over z, x, core).
Axes of the slice: x: 2, y: 2, z: 4, core: 2. Of those that a mesh axis runs over, the one named last changes fastest.
Arguments:
- outer_grad: bfloat16 [32, 4, 128, 1024], P(('parts', 'space')), parts along dimension 0, may hold values from -6 to 6
- block_input: bfloat16 [32, 4, 128, 1024], P(('parts', 'space')), parts along dimension 0, may hold values from -6 to 6
- third_input: bfloat16 [32, 4, 128, 1024], P(('parts', 'space')), parts along dimension 0, as said below
- second_input: bfloat16 [32, 8, 256, 256], P(('parts', 'space')), parts along dimension 0, as said below
- third_weight: bfloat16 [1024, 1024], replicated, may hold values from -0.1875 to 0.1875
- group_weight: bfloat16 [1024, 288], replicated, may hold values from -0.375 to 0.375
- first_weight: bfloat16 [1024, 1024], replicated, may hold values from -0.1875 to 0.1875
Outputs:
- input_grad: bfloat16 [32, 4, 128, 1024], P(('parts', 'space')), parts along dimension 0
- third_wgrad: float32 [2048, 1024], P(('parts', 'space')), parts along dimension 0
- group_wgrad: float32 [2048, 288], P(('parts', 'space')), parts along dimension 0
- first_wgrad: float32 [2048, 1024], P(('parts', 'space')), parts along dimension 0
There are 2 independent parts, one for each index of `parts`. A program takes and returns all parts, laid end to end along the dimension named above; an argument that names none is the same for every part. Nothing has to cross between parts.
Inputs may be any that keep to these rules, and one draw needn't show every extreme that they name: `third_input`: rectified values: zero or positive, about half of them zero. `second_input`: rectified values: zero or positive, about half of them zero.
All inputs are finite; a program needn't handle non-finite values.
Results may differ from a plain program's by a relative error of at most 0.0049.
Values may be sent and summed in bfloat16 or wider, within the bound.
No kernel may reach another device: no remote copies, remote signals or barrier semaphores. Data moves between devices by JAX's collectives and lax.ppermute only.
A program may use at most 128 MiB of HBM per device.

v0:
```python
import math

import jax
import jax.numpy as jnp
from jax import lax
from jax.sharding import PartitionSpec as P


def partner(block, axis, distance):
    count = lax.axis_size(axis)
    route = []
    for low in range(count):
        high = low | 1 << distance
        if high != low and high < count:
            route += [(low, high), (high, low)]
    return lax.ppermute(block, axis, route)


def from_behind(array, axis, by):
    count = lax.axis_size(axis)
    pairs = [(i, i + by) for i in range(count) if 0 <= i + by < count]
    return lax.ppermute(array, axis, pairs)


def to_groups(tile, col_parity, row_parity, row_bit):
    tile_rows, tile_width, channels = tile.shape
    shard_width = channels // 4
    split = tile.reshape(tile_rows, tile_width, 2, 2, shard_width)
    kept_part = lax.dynamic_index_in_dim(split, col_parity, 3, keepdims=False)
    sent_part = lax.dynamic_index_in_dim(split, 1 - col_parity, 3, keepdims=False)
    received = partner(sent_part, "space", 0)
    joined = jnp.where(
        col_parity == 0, jnp.stack([kept_part, received], 1), jnp.stack([received, kept_part], 1)
    )
    joined = joined.reshape(tile_rows, 2 * tile_width, 2, shard_width)
    kept_rows = lax.dynamic_index_in_dim(joined, row_parity, 2, keepdims=False)
    sent_rows = lax.dynamic_index_in_dim(joined, 1 - row_parity, 2, keepdims=False)
    received_rows = partner(sent_rows, "space", row_bit)
    stacked = jnp.where(
        row_parity == 0,
        jnp.stack([kept_rows, received_rows], 0),
        jnp.stack([received_rows, kept_rows], 0),
    )
    return stacked.reshape(2 * tile_rows, 2 * tile_width, shard_width)


def to_tiles(block, col_parity, row_parity, row_bit):
    double_rows, double_cols, shard_width = block.shape
    tile_rows = double_rows // 2
    tile_width = double_cols // 2
    split = block.reshape(2, tile_rows, double_cols, shard_width)
    kept_part = lax.dynamic_index_in_dim(split, row_parity, 0, keepdims=False)
    sent_part = lax.dynamic_index_in_dim(split, 1 - row_parity, 0, keepdims=False)
    received = partner(sent_part, "space", row_bit)
    joined = jnp.where(
        row_parity == 0, jnp.stack([kept_part, received], 2), jnp.stack([received, kept_part], 2)
    )
    joined = joined.reshape(tile_rows, 2, tile_width, 2, shard_width)
    kept_cols = lax.dynamic_index_in_dim(joined, col_parity, 1, keepdims=False)
    sent_cols = lax.dynamic_index_in_dim(joined, 1 - col_parity, 1, keepdims=False)
    received_cols = partner(sent_cols, "space", 0)
    stacked = jnp.where(
        col_parity == 0,
        jnp.stack([kept_cols, received_cols], 3),
        jnp.stack([received_cols, kept_cols], 3),
    )
    return stacked.reshape(tile_rows, tile_width, 4 * shard_width)


def with_rims(block, row_step):
    top = from_behind(block[-1:], "space", row_step)
    bottom = from_behind(block[:1], "space", -row_step)
    tall = jnp.concatenate([top, block, bottom], 0)
    empty = jnp.zeros_like(tall[:, :1])
    return jnp.concatenate([empty, tall, empty], 1)


def group_backward(padded, second_block, kernel, normalizer):
    tile_rows, tile_width, channels = second_block.shape
    group_width = kernel.shape[3]
    groups = channels // group_width
    second_groups = second_block.reshape(tile_rows, tile_width, groups, group_width)
    back_second = jnp.zeros((tile_rows, tile_width, groups, group_width), jnp.float32)
    tap_terms = []
    for tap_row in range(3):
        for tap_col in range(3):
            window = padded[
                2 - tap_row : 2 - tap_row + tile_rows, 2 - tap_col : 2 - tap_col + tile_width
            ]
            window = window.reshape(tile_rows, tile_width, groups, group_width)
            back_second = back_second + jnp.einsum(
                "hwgo,goi->hwgi",
                window,
                kernel[:, :, 3 * tap_row + tap_col, :],
                preferred_element_type=jnp.float32,
            )
            tap_terms.append(
                jnp.einsum(
                    "hwgi,hwgo->goi", second_groups, window, preferred_element_type=jnp.float32
                )
            )
    local_term = jnp.stack(tap_terms, 2).reshape(channels, 9 * group_width) * normalizer
    return (back_second.reshape(tile_rows, tile_width, channels), local_term)


def per_device(
    outer_grad, block_input, third_input, second_input, third_weight, group_weight, first_weight
):
    devices = lax.axis_size("space")
    position = lax.axis_index("space")
    row_bit = 1
    col_parity = position % 2
    row_parity = position // 2 % 2
    tile_rows = outer_grad.shape[1]
    tile_width = outer_grad.shape[2]
    channels = outer_grad.shape[3]
    shard_width = channels // 4
    group_width = group_weight.shape[1] // 9
    normalizer = 1.0 / math.sqrt(tile_rows * tile_width * devices)
    grad_rows = outer_grad.reshape(tile_rows * tile_width, channels)
    third_rows = third_input.reshape(tile_rows * tile_width, channels)
    input_rows = block_input.reshape(tile_rows * tile_width, channels)
    back_third = lax.dot_general(
        grad_rows, third_weight, (((1,), (1,)), ((), ())), preferred_element_type=jnp.float32
    )
    inner_grad = jnp.where(third_rows > 0, back_third, 0.0).astype(jnp.bfloat16)
    left_cols = third_rows
    third_wgrad = lax.psum_scatter(
        lax.dot_general(
            left_cols, grad_rows, (((0,), (0,)), ((), ())), preferred_element_type=jnp.float32
        )
        * normalizer,
        "space",
        scatter_dimension=0,
        tiled=True,
    )
    inner_block = to_groups(
        inner_grad.reshape(tile_rows, tile_width, channels), col_parity, row_parity, row_bit
    )
    second_block = second_input[0]
    row_step = 4
    offset = (2 * row_parity + col_parity) * shard_width
    padded = with_rims(inner_block, row_step)
    kernel = lax.dynamic_slice_in_dim(group_weight, offset, shard_width, 0)
    kernel = kernel.reshape(shard_width // group_width, group_width, 9, group_width)
    back_second, local_term = group_backward(padded, second_block, kernel, normalizer)
    full_term = lax.dynamic_update_slice_in_dim(
        jnp.zeros((channels, 9 * group_width), jnp.float32), local_term, offset, 0
    )
    group_wgrad = lax.psum_scatter(full_term, "space", scatter_dimension=0, tiled=True)
    first_block = jnp.where(second_block > 0, back_second, 0.0).astype(jnp.bfloat16)
    first_tile = to_tiles(first_block, col_parity, row_parity, row_bit)
    first_rows = first_tile.reshape(tile_rows * tile_width, channels)
    summed = lax.dot_general(
        first_rows, first_weight, (((1,), (1,)), ((), ())), preferred_element_type=jnp.float32
    )
    input_grad = (
        (summed + grad_rows.astype(jnp.float32))
        .astype(jnp.bfloat16)
        .reshape(1, tile_rows, tile_width, channels)
    )
    left_cols = input_rows
    first_wgrad = lax.psum_scatter(
        lax.dot_general(
            left_cols, first_rows, (((0,), (0,)), ((), ())), preferred_element_type=jnp.float32
        )
        * normalizer,
        "space",
        scatter_dimension=0,
        tiled=True,
    )
    return (input_grad, third_wgrad, group_wgrad, first_wgrad)


def solution(mesh):
    in_specs = (
        P(("parts", "space"), None, None, None),
        P(("parts", "space"), None, None, None),
        P(("parts", "space"), None, None, None),
        P(("parts", "space"), None, None, None),
        P(),
        P(),
        P(),
    )
    out_specs = (
        P(("parts", "space"), None, None, None),
        P(("parts", "space"), None),
        P(("parts", "space"), None),
        P(("parts", "space"), None),
    )
    return jax.shard_map(
        per_device, mesh=mesh, in_specs=in_specs, out_specs=out_specs, check_vma=False
    )
```

profile of v0, /device:TPU:0, one launch (start us, length us, event | category | flops | bytes accessed | tf_op | source)
XLA Modules:
  0.0 278.1 jit_solution(1105585685217040148)
XLA Ops:
  7.2 1.6 broadcast_compare_fusion
  9.1 2.5 select_convert_fusion.1
  12.4 2.2 constant_dynamic-slice_fusion.5
  15.3 1.4 collective-permute-done
  17.0 2.9 %collective-permute-start.1 = (bf16[4,256,256]{2,1,0:T(8,128)(2,1)S(1)}, bf16[4,256,256]{2,1,0:T(8,128)(2,1)S(1)}, u32[]{:S(2)}, u32[]{:S(2)}) collective-permute-start(bf16[4,256,256]{2,1,0:T(8,128)(2,1)S(1)} %get-tuple-element.39), channel_id=1, source_target_pairs={{0,2},{2,0},{1,3},{3,1},{4,6},{6,4},{5,7},{7,5},{8,10},{10,8},{9,1... | collective-permute-start | bytes 1572872 | tf_op jit(solution)/shard_map/ppermute | solution.py:16
  19.9 12.2 %collective-permute-done.1 = bf16[4,256,256]{2,1,0:T(8,128)(2,1)S(1)} collective-permute-done((bf16[4,256,256]{2,1,0:T(8,128)(2,1)S(1)}, bf16[4,256,256]{2,1,0:T(8,128)(2,1)S(1)}, u32[]{:S(2)}, u32[]{:S(2)}) %collective-permute-start.1) | collective-permute-done | bytes 524320 | tf_op jit(solution)/shard_map/ppermute | solution.py:16
  33.5 3.7 %collective-permute-start.2 = (bf16[1,256,256]{1,2,0:T(8,128)(2,1)}, bf16[1,256,256]{1,2,0:T(8,128)(2,1)S(1)}, u32[]{:S(2)}, u32[]{:S(2)}) collective-permute-start(bf16[1,256,256]{1,2,0:T(8,128)(2,1)} %get-tuple-element.36), channel_id=1, source_target_pairs={{0,4},{1,5},{2,6},{3,7},{4,8},{5,9},{6,10},{7,11},{8,12},{9,13},{1... | collective-permute-start | bytes 393224 | tf_op jit(solution)/shard_map/ppermute | solution.py:22
  37.3 1.3 collective-permute-start.3
  38.6 1.5 copy.179
  40.1 1.3 copy.161
  41.4 2.7 collective-permute-done.3
  44.3 2.4 pad_slice_fusion.5
  52.4 1.4 copy.180
  53.8 1.6 mul.29
  55.6 1.2 broadcast_in_dim.14
  57.9 4.5 %bitcast_multiply_fusion = f32[1024,1024]{1,0:T(8,128)} fusion(bf16[1,4,128,1024]{3,2,1,0:T(8,128)(2,1)} %param.7, bf16[1,4,128,1024]{3,2,1,0:T(8,128)(2,1)S(1)} %copy-done.17), kind=kOutput, calls=%fused_computation | convolution fusion | flops 1074790400 | bytes 6291456 | tf_op jit(solution)/shard_map/dot_general | solution.py:129
  62.5 1.0 constant_dynamic-slice_fusion.6
  63.5 1.1 reshape.105
  64.6 1.1 broadcast_compare_fusion.1
  65.7 1.9 copy.144
  67.5 1.2 fusion.29
  74.9 1.1 add_bitcast_fusion
  76.7 1.5 collective-permute-start.4
  78.4 13.0 %collective-permute-done.4 = bf16[4,256,256]{2,1,0:T(8,128)(2,1)S(1)} collective-permute-done((bf16[4,256,256]{2,1,0:T(8,128)(2,1)S(1)}, bf16[4,256,256]{2,1,0:T(8,128)(2,1)S(1)}, u32[]{:S(2)}, u32[]{:S(2)}) %collective-permute-start.4) | collective-permute-done | bytes 524320 | tf_op jit(solution)/shard_map/ppermute | solution.py:16
  91.8 1.9 collective-permute-done.5
  93.8 1.1 copy.177
  96.1 3.3 %multiply_bitcast_fusion = f32[1024,1024]{0,1:T(8,128)} fusion(bf16[512,1024]{1,0:T(8,128)(2,1)S(1)} %select_n.125, bf16[512,1024]{1,0:T(8,128)(2,1)S(1)} %bitcast.217), kind=kOutput, calls=%fused_computation.1 | convolution fusion | flops 1074790400 | bytes 6291456 | tf_op jit(solution)/shard_map/dot_general | solution.py:164
  99.4 5.5 %copy.193 = f32[1024,1024]{1,0:T(8,128)} copy(f32[1024,1024]{0,1:T(8,128)} %multiply_bitcast_fusion) | data formatting | bytes 8388608
  104.9 4.3 %add_convert_fusion = bf16[512,1024]{1,0:T(8,128)(2,1)} fusion(bf16[512,1024]{1,0:T(8,128)(2,1)} %bitcast.219, bf16[512,1024]{1,0:T(8,128)(2,1)S(1)} %select_n.125, bf16[1024,1024]{1,0:T(8,128)(2,1)} %param.13), kind=kOutput, calls=%fused_computation.9 | convolution fusion | flops 1075314688 | bytes 5242880 | tf_op jit(solution)/shard_map/dot_general | solution.py:154
  109.2 9.7 %reduce-scatter.8.cloned.1.call-done = f32[64,288]{1,0:T(8,128)} async-done(((f32[1024,288]{1,0:T(8,128)}), f32[64,288]{1,0:T(8,128)}) %reduce-scatter.8.cloned.1.call-update) | async-done | bytes 73744 | tf_op jit(solution)/shard_map/reduce_scatter | solution.py:150
  118.9 76.6 %reduce-scatter.6.cloned.1.call-done = f32[64,1024]{1,0:T(8,128)} async-done(((f32[1024,1024]{1,0:T(8,128)}), f32[64,1024]{1,0:T(8,128)}) %reduce-scatter.6.cloned.1.call-update) | async-done | bytes 262160 | tf_op jit(solution)/shard_map/reduce_scatter | solution.py:128
  195.5 76.0 %reduce-scatter.10.cloned.1.call-done = f32[64,1024]{1,0:T(8,128)} async-done(((f32[1024,1024]{1,0:T(8,128)}), f32[64,1024]{1,0:T(8,128)}) %reduce-scatter.10.cloned.1.call-update) | async-done | bytes 262160
  (91 shorter events, 19.0 us)
Async XLA Ops:
  7.2 1.9 copy-start
  7.2 111.7 %reduce-scatter.8.cloned.1.call-start = ((), (), s32[]{:S(2)}) async-start(), calls=%async_computation.4 | async-start | bytes 1671168 | tf_op jit(solution)/shard_map/reduce_scatter | solution.py:150
  14.7 2.1 collective-permute-start
  17.0 15.2 %collective-permute-start.1 = (bf16[4,256,256]{2,1,0:T(8,128)(2,1)S(1)}, bf16[4,256,256]{2,1,0:T(8,128)(2,1)S(1)}, u32[]{:S(2)}, u32[]{:S(2)}) collective-permute-start(bf16[4,256,256]{2,1,0:T(8,128)(2,1)S(1)} %get-tuple-element.39), channel_id=1, source_target_pairs={{0,2},{2,0},{1,3},{3,1},{4,6},{6,4},{5,7},{7,5},{8,10},{10,8},{9,1... | collective-permute-start | bytes 1572872 | tf_op jit(solution)/shard_map/ppermute | solution.py:16
  33.5 7.8 %collective-permute-start.2 = (bf16[1,256,256]{1,2,0:T(8,128)(2,1)}, bf16[1,256,256]{1,2,0:T(8,128)(2,1)S(1)}, u32[]{:S(2)}, u32[]{:S(2)}) collective-permute-start(bf16[1,256,256]{1,2,0:T(8,128)(2,1)} %get-tuple-element.36), channel_id=1, source_target_pairs={{0,4},{1,5},{2,6},{3,7},{4,8},{5,9},{6,10},{7,11},{8,12},{9,13},{1... | collective-permute-start | bytes 393224 | tf_op jit(solution)/shard_map/ppermute | solution.py:22
  37.3 6.9 %collective-permute-start.3 = (bf16[1,256,256]{1,2,0:T(8,128)(2,1)S(1)}, bf16[1,256,256]{1,2,0:T(8,128)(2,1)S(1)}, u32[]{:S(2)}, u32[]{:S(2)}) collective-permute-start(bf16[1,256,256]{1,2,0:T(8,128)(2,1)S(1)} %get-tuple-element.37), channel_id=1, source_target_pairs={{4,0},{5,1},{6,2},{7,3},{8,4},{9,5},{10,6},{11,7},{12,8},{13,9},{1... | collective-permute-start | bytes 393224 | tf_op jit(solution)/shard_map/ppermute | solution.py:22
  46.7 1.0 copy-start.11
  46.7 1.4 copy-start.13
  46.7 2.6 copy-start.15
  46.7 3.8 %copy-start.9 = (bf16[8,256,256]{1,2,0:T(8,128)(2,1)}, bf16[8,256,256]{1,2,0:T(8,128)(2,1)S(1)}, u32[]{:S(2)}) copy-start(bf16[8,256,256]{1,2,0:T(8,128)(2,1)S(1)} %get-tuple-element.27) | copy-start | bytes 3145732
  46.7 4.2 %copy-start.7 = (bf16[8,256,256]{1,2,0:T(8,128)(2,1)}, bf16[8,256,256]{1,2,0:T(8,128)(2,1)S(1)}, u32[]{:S(2)}) copy-start(bf16[8,256,256]{1,2,0:T(8,128)(2,1)S(1)} %get-tuple-element.26) | copy-start | bytes 3145732
  46.7 5.1 %copy-start.5 = (bf16[8,256,256]{1,2,0:T(8,128)(2,1)}, bf16[8,256,256]{1,2,0:T(8,128)(2,1)S(1)}, u32[]{:S(2)}) copy-start(bf16[8,256,256]{1,2,0:T(8,128)(2,1)S(1)} %get-tuple-element.28) | copy-start | bytes 3145732
  47.7 1.6 copy-start.3
  48.1 2.0 copy-start.2
  55.6 2.3 copy-start.17
  57.7 137.8 %reduce-scatter.6.cloned.1.call-start = ((), (), s32[]{:S(2)}) async-start(), calls=%async_computation.3 | async-start | bytes 4456448 | tf_op jit(solution)/shard_map/reduce_scatter | solution.py:128
  62.4 2.2 copy-start.18
  62.4 209.1 %reduce-scatter.10.cloned.1.call-start = ((), (), s32[]{:S(2)}) async-start(), calls=%async_computation.5 | async-start | bytes 4456448
  67.5 1.7 copy-start.4
  69.2 1.3 copy-start.16
  69.6 1.3 copy-start.14
  70.9 1.3 copy-start.12
  71.4 1.3 copy-start.10
  72.5 1.3 copy-start.8
  73.1 1.3 copy-start.6
  76.7 14.7 %collective-permute-start.4 = (bf16[4,256,256]{2,1,0:T(8,128)(2,1)S(1)}, bf16[4,256,256]{2,1,0:T(8,128)(2,1)S(1)}, u32[]{:S(2)}, u32[]{:S(2)}) collective-permute-start(bf16[4,256,256]{2,1,0:T(8,128)(2,1)S(1)} %bitcast.225), channel_id=1, source_target_pairs={{0,2},{2,0},{1,3},{3,1},{4,6},{6,4},{5,7},{7,5},{8,10},{10,8},{9,1... | collective-permute-start | bytes 1572872 | tf_op jit(solution)/shard_map/ppermute | solution.py:16
  91.7 2.0 collective-permute-start.5
  94.9 1.2 copy-start.19
  104.9 166.7 %copy-start.1 = (bf16[1024,1024]{1,0:T(8,128)(2,1)S(1)}, bf16[1024,1024]{1,0:T(8,128)(2,1)}, u32[]{:S(2)}) copy-start(bf16[1024,1024]{1,0:T(8,128)(2,1)} %param.11) | copy-start | bytes 6291460
Sparse Core Ops, SparseCore 0:
  57.8 61.0 reduce-scatter.7
  123.8 71.6 reduce-scatter.5
  200.0 71.5 reduce-scatter.9
where the time goes:
time: 279 us; the launch traced here: 278 us
  waiting for transfers between devices  194 us (70%)
  local copies, waits for them, and re-layouts  33.1 us (12%)
  matrix products  22.7 us (8%)
  between operations  14.2 us (5%)
  starting transfers between devices  10.4 us (4%)
  other arithmetic  4.05 us (1%)
    reduce_scatter x1, waiting for transfers between devices, per_device(): lax.psum_scatter(lax.dot_general(left_cols, grad_rows, (((0,), (0,)), (()...  76.6 us
    unnamed x4, waiting for transfers between devices  76.1 us
    ppermute x4, waiting for transfers between devices, partner(): return lax.ppermute(block, axis, route)  28.5 us
    unnamed x44, local copies, waits for them, and re-layouts  12.1 us
    reduce_scatter x1, waiting for transfers between devices, per_device(): lax.psum_scatter(full_term, 'space', scatter_dimension=0, tiled=True)  9.7 us
  transfers between devices with their start and end apart: 9, of which 8 were waited for; matrix products, arithmetic and copies ran while one was open for 12% of the time, Pallas kernels for 0%

commit v1 on v0

v1 whole, which is shorter than its diff:
```python
import math

import jax
import jax.numpy as jnp
from jax import lax
from jax.experimental import pallas as pl
from jax.experimental.pallas import tpu as pltpu
from jax.sharding import PartitionSpec as P

BF = jnp.bfloat16
F32 = jnp.float32
VMEM_LIMIT = 48 * 1024 * 1024


def exchange(array, bit):
    count = lax.axis_size("space")
    return lax.ppermute(array, "space", [(i, i ^ (1 << bit)) for i in range(count)])


def exchange_across(array):
    count = lax.axis_size("space")
    route = []
    for low in range(count):
        high = low + 2
        if low & 2 and high < count:
            route += [(low, high), (high, low)]
    return lax.ppermute(array, "space", route)


def pick(array, index, axis):
    return lax.dynamic_index_in_dim(array, index, axis, keepdims=False)


def scatter_sum(total, bits, order, left):
    left = list(left)
    for bit in order:
        at = left.index(bit)
        left.pop(at)
        received = exchange(pick(total, 1 - bits[bit], at).astype(BF), bit)
        total = pick(total, bits[bit], at) + received.astype(F32)
    return total


def nt_dot(a, b):
    return lax.dot_general(a, b, (((1,), (1,)), ((), ())), preferred_element_type=F32)


def inner_kernel(grad_ref, weight_ref, mask_ref, out_ref):
    back = nt_dot(grad_ref[...], weight_ref[...])
    out_ref[...] = jnp.where(mask_ref[...] > 0, back, 0.0).astype(BF)


def inner_of(grad_rows, third_weight, third_rows):
    rows, channels = grad_rows.shape
    step = 256
    return pl.pallas_call(
        inner_kernel,
        grid=(channels // step,),
        in_specs=[
            pl.BlockSpec((rows, channels), lambda j: (0, 0)),
            pl.BlockSpec((step, channels), lambda j: (j, 0)),
            pl.BlockSpec((rows, step), lambda j: (0, j)),
        ],
        out_specs=pl.BlockSpec((rows, step), lambda j: (0, j)),
        out_shape=jax.ShapeDtypeStruct((rows, channels), BF),
        compiler_params=pltpu.CompilerParams(vmem_limit_bytes=VMEM_LIMIT),
        cost_estimate=pl.CostEstimate(
            flops=2 * rows * channels * channels, bytes_accessed=5 << 20, transcendentals=0
        ),
        name="inner",
    )(grad_rows, third_weight, third_rows)


def result_kernel(first_ref, weight_ref, grad_ref, out_ref):
    summed = nt_dot(first_ref[...], weight_ref[...])
    out_ref[...] = (summed + grad_ref[...].astype(F32)).astype(BF)


def result_of(first_rows, first_weight, grad_rows):
    rows, channels = grad_rows.shape
    step = 256
    return pl.pallas_call(
        result_kernel,
        grid=(channels // step,),
        in_specs=[
            pl.BlockSpec((rows, channels), lambda j: (0, 0)),
            pl.BlockSpec((step, channels), lambda j: (j, 0)),
            pl.BlockSpec((rows, step), lambda j: (0, j)),
        ],
        out_specs=pl.BlockSpec((rows, step), lambda j: (0, j)),
        out_shape=jax.ShapeDtypeStruct((rows, channels), BF),
        compiler_params=pltpu.CompilerParams(vmem_limit_bytes=VMEM_LIMIT),
        cost_estimate=pl.CostEstimate(
            flops=2 * rows * channels * channels, bytes_accessed=5 << 20, transcendentals=0
        ),
        name="result",
    )(first_rows, first_weight, grad_rows)


def spread_kernel(gw, taps, weight_ref, out_ref):
    step = weight_ref.shape[0]
    weight = weight_ref[...]
    source = lax.broadcasted_iota(jnp.int32, (taps * gw, step), 0)
    column = lax.broadcasted_iota(jnp.int32, (taps * gw, step), 1) % gw
    row_group = lax.broadcasted_iota(jnp.int32, (step, step), 0) // gw
    column_group = lax.broadcasted_iota(jnp.int32, (step, step), 1) // gw
    for tap in range(taps):
        chooser = jnp.where(source == tap * gw + column, 1.0, 0.0).astype(BF)
        copies = jnp.dot(weight, chooser, preferred_element_type=F32)
        out_ref[0, tap] = jnp.where(row_group == column_group, copies, 0.0).astype(BF)


def spread_of(group_weight, step):
    channels, width = group_weight.shape
    taps = 9
    gw = width // taps
    return pl.pallas_call(
        lambda w, o: spread_kernel(gw, taps, w, o),
        grid=(channels // step,),
        in_specs=[pl.BlockSpec((step, width), lambda j: (j, 0))],
        out_specs=pl.BlockSpec((1, taps, step, step), lambda j: (j, 0, 0, 0)),
        out_shape=jax.ShapeDtypeStruct((channels // step, taps, step, step), BF),
        compiler_params=pltpu.CompilerParams(vmem_limit_bytes=VMEM_LIMIT),
        name="spread",
    )(group_weight)


def conv_kernel(
    gw,
    piece,
    where_ref,
    inner_ref,
    top_ref,
    bottom_ref,
    edge_ref,
    second_ref,
    spread_ref,
    keep_in_ref,
    send_in_ref,
    first_ref,
    keep_ref,
    send_ref,
    group_keep_ref,
    group_send_ref,
    window_ref,
    term_ref,
):
    tile_rows, width, step = inner_ref.shape
    positions = tile_rows * width
    taps = spread_ref.shape[1]
    core = where_ref[0]
    at = lax.broadcasted_iota(jnp.int32, (width, step), 0)
    for row in range(tile_rows + 2):
        if row == 0:
            line = top_ref[...]
        elif row == tile_rows + 1:
            line = bottom_ref[...]
        else:
            line = inner_ref[row - 1]
        here = pl.ds(row * width, width)
        wide = line.astype(F32)
        edge = edge_ref[row : row + 1, :]
        left = jnp.where(core == 1, edge, 0.0)
        right = jnp.where(core == 0, edge, 0.0)
        window_ref[1, here, :] = line
        window_ref[2, here, :] = jnp.where(at == 0, left, pltpu.roll(wide, 1, 0)).astype(BF)
        window_ref[0, here, :] = jnp.where(
            at == width - 1, right, pltpu.roll(wide, width - 1, 0)
        ).astype(BF)
    second = second_ref[0]
    flipped = second.T
    lane_group = lax.broadcasted_iota(jnp.int32, (gw, step), 1) // gw
    back = jnp.zeros((positions, step), F32)
    for tap in range(taps):
        window = window_ref[tap % 3, pl.ds((2 - tap // 3) * width, positions), :]
        back = back + jnp.dot(window, spread_ref[0, tap], preferred_element_type=F32)
        term = jnp.dot(flipped, window, preferred_element_type=F32)
        mine = jnp.zeros((gw, step), F32)
        for group in range(step // gw):
            mine = jnp.where(lane_group == group, term[group * gw : (group + 1) * gw], mine)
        term_ref[tap * gw : (tap + 1) * gw, :] = mine
    first = jnp.where(second > 0, back, 0.0).astype(BF)
    first_ref[...] = first
    keep_ref[...] = jnp.dot(keep_in_ref[...], first, preferred_element_type=F32)
    send_ref[...] = jnp.dot(send_in_ref[...], first, preferred_element_type=F32).astype(BF)
    turned = term_ref[...].T.reshape(step // (2 * piece), 2, piece, taps * gw)
    low = turned[:, 0].reshape(step // 2, taps * gw)
    high = turned[:, 1].reshape(step // 2, taps * gw)
    group_keep_ref[...] = jnp.where(core == 0, low, high)
    group_send_ref[...] = jnp.where(core == 0, high, low).astype(BF)


def conv_of(where, inner, top, bottom, edge, second, spread, keep_in, send_in, gw, piece):
    tile_rows, width, channels = inner.shape
    slots, positions, step = second.shape
    taps = spread.shape[1]
    rows = keep_in.shape[0]
    grid_spec = pltpu.PrefetchScalarGridSpec(
        num_scalar_prefetch=1,
        grid=(slots,),
        in_specs=[
            pl.BlockSpec((tile_rows, width, step), lambda q, w: (0, 0, w[q + 1])),
            pl.BlockSpec((width, step), lambda q, w: (0, w[q + 1])),
            pl.BlockSpec((width, step), lambda q, w: (0, w[q + 1])),
            pl.BlockSpec((edge.shape[0], step), lambda q, w: (0, w[q + 1])),
            pl.BlockSpec((1, positions, step), lambda q, w: (q, 0, 0)),
            pl.BlockSpec((1, taps, step, step), lambda q, w: (w[q + 1], 0, 0, 0)),
            pl.BlockSpec((rows, positions), lambda q, w: (0, 0)),
            pl.BlockSpec((rows, positions), lambda q, w: (0, 0)),
        ],
        out_specs=[
            pl.BlockSpec((positions, step), lambda q, w: (0, w[q + 1])),
            pl.BlockSpec((rows, step), lambda q, w: (0, w[q + 1])),
            pl.BlockSpec((rows, step), lambda q, w: (0, w[q + 1])),
            pl.BlockSpec((step // 2, taps * gw), lambda q, w: (w[q + 1], 0)),
            pl.BlockSpec((step // 2, taps * gw), lambda q, w: (w[q + 1], 0)),
        ],
        scratch_shapes=[
            pltpu.VMEM((3, (tile_rows + 2) * width, step), BF),
            pltpu.VMEM((taps * gw, step), F32),
        ],
    )
    flops = 2 * slots * positions * step * (2 * taps * step + 2 * rows)
    return pl.pallas_call(
        lambda *refs: conv_kernel(gw, piece, *refs),
        grid_spec=grid_spec,
        out_shape=[
            jax.ShapeDtypeStruct((positions, channels), BF),
            jax.ShapeDtypeStruct((rows, channels), F32),
            jax.ShapeDtypeStruct((rows, channels), BF),
            jax.ShapeDtypeStruct((channels // 2, taps * gw), F32),
            jax.ShapeDtypeStruct((channels // 2, taps * gw), BF),
        ],
        compiler_params=pltpu.CompilerParams(vmem_limit_bytes=VMEM_LIMIT),
        cost_estimate=pl.CostEstimate(flops=flops, bytes_accessed=16 << 20, transcendentals=0),
        name="conv",
    )(where, inner, top, bottom, edge, second, spread, keep_in, send_in)


def per_device(
    outer_grad, block_input, third_input, second_input, third_weight, group_weight, first_weight
):
    devices = lax.axis_size("space")
    position = lax.axis_index("space")
    n_bits = devices.bit_length() - 1
    bits = [(position >> b) & 1 for b in range(n_bits)]
    core, half = bits[0], bits[1]
    _, tile_rows, width, channels = outer_grad.shape
    positions = tile_rows * width
    shard = channels // 4
    gw = group_weight.shape[1] // 9
    piece = channels // devices
    normalizer = 1.0 / math.sqrt(positions * devices)
    grad_rows = outer_grad.reshape(positions, channels)
    third_rows = third_input.reshape(positions, channels)
    input_rows = block_input.reshape(positions, channels)
    high_to_low = list(range(n_bits - 1, -1, -1))
    z_first = [*range(2, n_bits), 1]
    x_first = [*range(1, n_bits)]

    block = second_input[0].reshape(2, tile_rows, 2 * width, shard)
    far_sent = pick(block, 1 - half, 0)
    near = pick(block, half, 0).reshape(tile_rows, 2, width, shard)
    far = exchange(far_sent, 1).reshape(tile_rows, 2, width, shard)
    near_other = exchange(pick(near, 1 - core, 1), 0)
    far_other = exchange(pick(far, 1 - core, 1), 0)
    second = jnp.stack([pick(near, core, 1), near_other, pick(far, core, 1), far_other])
    second = second.reshape(4, positions, shard)
    where = jnp.stack(
        [
            core,
            2 * half + core,
            2 * half + 1 - core,
            2 * (1 - half) + core,
            2 * (1 - half) + 1 - core,
        ]
    ).astype(jnp.int32)

    by_core = third_rows.reshape(positions, channels // (2 * piece), 2, piece)
    third_keep = pick(by_core, core, 2).reshape(positions, channels // 2)
    third_send = pick(by_core, 1 - core, 2).reshape(positions, channels // 2)
    tn = (((0,), (0,)), ((), ()))
    sent = lax.dot_general(third_send, grad_rows, tn, preferred_element_type=F32).astype(BF)
    kept = lax.dot_general(third_keep, grad_rows, tn, preferred_element_type=F32)
    third_total = kept + exchange(sent, 0).astype(F32)
    third_total = third_total.reshape([2] * (n_bits - 1) + [piece, channels])
    third_wgrad = scatter_sum(third_total, bits, z_first, high_to_low[:-1]) * normalizer

    inner = inner_of(grad_rows, third_weight, third_rows).reshape(tile_rows, width, channels)
    inside = exchange(jnp.where(half == 0, inner[-1], inner[0]), 1)
    outside = exchange_across(jnp.where(half == 0, inner[0], inner[-1]))
    top = jnp.where(half == 0, outside, inside)
    bottom = jnp.where(half == 0, inside, outside)
    column = (1 - core) * (width - 1)
    edge = jnp.concatenate(
        [
            lax.dynamic_slice_in_dim(top, column, 1, 0),
            lax.dynamic_slice_in_dim(inner, column, 1, 1)[:, 0],
            lax.dynamic_slice_in_dim(bottom, column, 1, 0),
        ]
    )
    edge = exchange(edge, 0).astype(F32)

    spread = spread_of(group_weight, shard)
    turned = input_rows.T.reshape(channels // (2 * piece), 2, piece, positions)
    keep_in = pick(turned, core, 1).reshape(channels // 2, positions)
    send_in = pick(turned, 1 - core, 1).reshape(channels // 2, positions)
    first, kept, sent, group_kept, group_sent = conv_of(
        where, inner, top, bottom, edge, second, spread, keep_in, send_in, gw, piece
    )
    cut = 3 * channels // 8
    received = exchange(jnp.concatenate([group_sent, sent], 1), 0).astype(F32)
    total = jnp.concatenate([group_kept, kept], 1) + received
    cut += group_kept.shape[1]
    shape = [2] * (n_bits - 1) + [piece]
    one = scatter_sum(total[:, :cut].reshape([*shape, -1]), bits, z_first, high_to_low[:-1])
    two = scatter_sum(total[:, cut:].reshape([*shape, -1]), bits, x_first, high_to_low[:-1])
    total = jnp.concatenate([one, two], 1) * normalizer
    group_wgrad = total[:, : 9 * gw]
    first_wgrad = total[:, 9 * gw :]
    input_grad = result_of(first, first_weight, grad_rows).reshape(outer_grad.shape)
    return (input_grad, third_wgrad, group_wgrad, first_wgrad)


def solution(mesh):
    tiles = P(("parts", "space"), None, None, None)
    rows = P(("parts", "space"), None)
    return jax.shard_map(
        per_device,
        mesh=mesh,
        in_specs=(tiles, tiles, tiles, tiles, P(), P(), P()),
        out_specs=(tiles, rows, rows, rows),
        check_vma=False,
    )
```

time: 279 us -> 132 us (0.47)
  waiting for transfers between devices: 194 us -> 44.9 us
  matrix products: 22.7 us -> 4.28 us
  Pallas kernels: 0 us -> 18 us
  between operations: 14.2 us -> 0.99 us
  starting transfers between devices: 10.4 us -> 23 us
  other arithmetic: 4.05 us -> 9.65 us
  local copies, waits for them, and re-layouts: 33.1 us -> 30.2 us
    reduce_scatter x2 -> x0, waiting for transfers between devices: 86.3 us -> none  [the longest x1 76.6 us: per_device(): lax.psum_scatter(lax.dot_general(left_cols, grad_rows, (((0,), (0,)), (()...]
    unnamed x4 -> x0, waiting for transfers between devices: 76.1 us -> none
    dot_general x22 -> x2, matrix products: 22.7 us -> 4.28 us  [the longest x1 2.6 us: per_device(): lax.dot_general(third_keep, grad_rows, tn, preferred_element_type=F32)]
    pallas_call x0 -> x4, Pallas kernels: none -> 18 us  [the longest x1 10.3 us: conv_of(): pl.pallas_call(lambda *refs: conv_kernel(gw, piece, *refs), grid_spec=gri...]
    ppermute x6 -> x17, waiting for transfers between devices: 31.2 us -> 44.9 us  [the longest x16 44.9 us: exchange(): lax.ppermute(array, 'space', [(i, i ^ 1 << bit) for i in range(count)])]
    ppermute x6 -> x17, starting transfers between devices: 10.1 us -> 23 us  [the longest x16 21.7 us: exchange(): lax.ppermute(array, 'space', [(i, i ^ 1 << bit) for i in range(count)])]
    add x0 -> x9, other arithmetic: none -> 4.08 us  [the longest x1 2.27 us: per_device(): total = jnp.concatenate([group_kept, kept], 1) + received]
    select_n x5 -> x0, local copies, waits for them, and re-layouts: 3.77 us -> none  [the longest x2 1.84 us: to_tiles(): jnp.where(col_parity == 0, jnp.stack([kept_cols, received_cols], 3), jnp....]
  transfers between devices with their start and end apart: 9 -> 17, of which waited for: 8 -> 9; matrix products, arithmetic and copies ran while one was open for 12% -> 20% of each run, Pallas kernels for 0% -> 14%
where the time goes in v1:
time: 132 us; the launch traced here: 131 us
  waiting for transfers between devices  44.9 us (34%)
  local copies, waits for them, and re-layouts  30.2 us (23%)
  starting transfers between devices  23 us (17%)
  Pallas kernels  18 us (14%)
  other arithmetic  9.65 us (7%)
  matrix products  4.28 us (3%)
    ppermute x16, waiting for transfers between devices, exchange(): lax.ppermute(array, 'space', [(i, i ^ 1 << bit) for i in range(count)])  44.9 us
    ppermute x16, starting transfers between devices, exchange(): lax.ppermute(array, 'space', [(i, i ^ 1 << bit) for i in range(count)])  21.7 us
    unnamed x41, local copies, waits for them, and re-layouts  13.3 us
    pallas_call x1, Pallas kernels, conv_of(): pl.pallas_call(lambda *refs: conv_kernel(gw, piece, *refs), grid_spec=gri...  10.3 us
    dynamic_slice x5, local copies, waits for them, and re-layouts, pick(): return lax.dynamic_index_in_dim(array, index, axis, keepdims=False)  6.9 us
    pallas_call x1, Pallas kernels, result_of(): pl.pallas_call(result_kernel, grid=(channels // step,), in_specs=[pl.Bloc...  2.98 us
  transfers between devices with their start and end apart: 17, of which 9 were waited for; matrix products, arithmetic and copies ran while one was open for 20% of the time, Pallas kernels for 14%

profile of v1, /device:TPU:0, one launch (start us, length us, event | category | flops | bytes accessed | tf_op | source)
XLA Modules:
  0.0 131.0 jit_solution(10753065929125068381)
XLA Ops:
  0.7 2.2 %constant_dynamic-slice_fusion.8 = (bf16[1,4,256,256]{3,2,1,0:T(8,128)(2,1)S(1)}, bf16[4,256,256]{2,1,0:T(8,128)(2,1)}) fusion(bf16[2,4,256,256]{3,2,1,0:T(8,128)(2,1)} %bitcast.108, s32[]{:T(128)S(6)} %select_n.88, s32[]{:T(128)S(6)} %select_n.91), kind=kLoop, calls=%fused_computation.51 | loop fusion | bytes 2097160 | tf_op jit(solution)/shard_map/jit(dynamic_index_in_dim)/dynamic_slice | solution.py:31
  2.9 2.9 %collective-permute-start.4 = (bf16[4,256,256]{2,1,0:T(8,128)(2,1)}, bf16[4,256,256]{2,1,0:T(8,128)(2,1)}, u32[]{:S(2)}, u32[]{:S(2)}) collective-permute-start(bf16[4,256,256]{2,1,0:T(8,128)(2,1)} %get-tuple-element.19), channel_id=1, source_target_pairs={{0,2},{1,3},{2,0},{3,1},{4,6},{5,7},{6,4},{7,5},{8,10},{9,11},{10,... | collective-permute-start | bytes 1572872 | tf_op jit(solution)/shard_map/ppermute | solution.py:17
  6.6 1.6 %copy-done.3 = bf16[1024,1024]{1,0:T(8,128)(2,1)S(1)} copy-done((bf16[1024,1024]{1,0:T(8,128)(2,1)S(1)}, bf16[1024,1024]{1,0:T(8,128)(2,1)}, u32[]{:S(2)}) %copy-start.3) | copy-done | bytes 2097176
  8.2 2.2 %inner.1 = bf16[512,1024]{1,0:T(8,128)(2,1)S(1)} custom-call(bf16[512,1024]{1,0:T(8,128)(2,1)S(1)} %bitcast.88, bf16[1024,1024]{1,0:T(8,128)(2,1)S(1)} %copy-done.3, bf16[512,1024]{1,0:T(8,128)(2,1)S(1)} %bitcast.92), custom_call_target="tpu_custom_call" | custom-call | flops 1073741824 | bytes 5242880 | tf_op jit(solution)/shard_map/inner/pallas_call | solution.py:56
  12.5 3.7 %collective-permute-start.1 = (bf16[128,1024]{1,0:T(8,128)(2,1)}, bf16[128,1024]{1,0:T(8,128)(2,1)}, u32[]{:S(2)}, u32[]{:S(2)}) collective-permute-start(bf16[128,1024]{1,0:T(8,128)(2,1)} %get-tuple-element.20), channel_id=1, source_target_pairs={{0,2},{1,3},{2,0},{3,1},{4,6},{5,7},{6,4},{7,5},{8,10},{9,11},{10,... | collective-permute-start | bytes 786440 | tf_op jit(solution)/shard_map/ppermute | solution.py:17
  16.2 1.4 %copy.25 = bf16[1,4,128,1024]{2,1,3,0:T(4,128)(2,1)} copy(bf16[1,4,128,1024]{3,2,1,0:T(8,128)(2,1)S(1)} %copy-done.2) | data formatting | bytes 2097152 | tf_op args[2]
  17.6 1.5 %reshape_reshape.3 = bf16[512,8,2,64]{0,3,2,1:T(8,128)(2,1)S(1)} reshape(bf16[1,4,128,1024]{2,1,3,0:T(4,128)(2,1)} %copy.25) | data formatting | bytes 2097152 | tf_op jit(solution)/shard_map/reshape;reshape | solution.py:279
  20.0 1.7 %convolution_convert_fusion = bf16[512,1024]{1,0:T(8,128)(2,1)} fusion(bf16[512,512]{0,1:T(8,128)(2,1)S(1)} %bitcast.111, bf16[512,1024]{1,0:T(8,128)(2,1)S(1)} %bitcast.89), kind=kOutput, calls=%fused_computation.2 | convolution fusion | flops 537395200 | bytes 2621440 | tf_op jit(solution)/shard_map/dot_general | solution.py:283
  23.1 5.5 %collective-permute-done.1 = bf16[128,1024]{1,0:T(8,128)(2,1)} collective-permute-done((bf16[128,1024]{1,0:T(8,128)(2,1)}, bf16[128,1024]{1,0:T(8,128)(2,1)}, u32[]{:S(2)}, u32[]{:S(2)}) %collective-permute-start.1) | collective-permute-done | bytes 262176 | tf_op jit(solution)/shard_map/ppermute | solution.py:17
  29.6 2.0 %constant_dynamic-slice_fusion.6 = (bf16[4,1,128,256]{3,2,1,0:T(8,128)(2,1)}, bf16[4,128,256]{2,1,0:T(8,128)(2,1)}) fusion(bf16[4,2,128,256]{3,2,1,0:T(8,128)(2,1)} %bitcast.14, s32[]{:T(128)S(6)} %select_n.89, s32[]{:T(128)S(6)} %select_n.90), kind=kLoop, calls=%fused_computation.49 | loop fusion | bytes 1048584 | tf_op jit(solution)/shard_map/jit(dynamic_index_in_dim)/dynamic_slice | solution.py:31
  33.3 1.4 %copy.23.w = bf16[1024,288]{1,0:T(8,128)(2,1)S(1)} copy(bf16[1024,288]{0,1:T(8,128)(2,1)} %param.12) | data formatting | bytes 1179648 | tf_op args[5]
  34.7 2.5 %spread.1.refs_6_ = bf16[4,9,256,256]{3,2,1,0:T(8,128)(2,1)S(1)} custom-call(bf16[1024,288]{1,0:T(8,128)(2,1)S(1)} %copy.23.w), custom_call_target="tpu_custom_call" | custom-call | tf_op jit(solution)/shard_map/spread/pallas_call | solution.py:117
  37.2 2.1 %copy-done.1 = bf16[4,9,256,256]{3,2,1,0:T(8,128)(2,1)} copy-done((bf16[4,9,256,256]{3,2,1,0:T(8,128)(2,1)}, bf16[4,9,256,256]{3,2,1,0:T(8,128)(2,1)S(1)}, u32[]{:S(2)}) %copy-start.1) | copy-done | bytes 4718616
  39.5 2.2 %pad_maximum_fusion.1.refs_5_ = bf16[4,512,256]{2,1,0:T(8,128)(2,1)} fusion(bf16[1,512,256]{2,1,0:T(8,128)(2,1)} %bitcast.17, bf16[1,512,256]{2,1,0:T(8,128)(2,1)} %bitcast.110, bf16[1,512,256]{2,1,0:T(8,128)(2,1)} %bitcast.12, bf16[1,512,256]{2,1,0:T(8,128)(2,1)S(1)} %bitcast.109), kind=kLoop, calls=%fused_computation.4 | loop fusion | flops 1572864 | bytes 2097152 | tf_op jit(solution)/shard_map/stack | solution.py:267
  44.7 10.3 %conv.1 = (bf16[512,1024]{1,0:T(8,128)(2,1)S(1)}, f32[512,1024]{1,0:T(8,128)}, bf16[512,1024]{1,0:T(8,128)(2,1)S(1)}, f32[512,288]{1,0:T(8,128)S(1)}, bf16[512,288]{1,0:T(8,128)(2,1)S(1)}) custom-call(s32[5]{0:T(128)S(1)} %stack.38.refs_0_, bf16[4,128,1024]{2,1,0:T(8,128)(2,1)S(1)} %bitcast.94, bf16[128,1024]{1,0:T(8,128)(2,1)S(1)} %copy-done.12, ...), custom_call_target="tpu_custom_call" | custom-call | flops 5905580032 | bytes 16777216 | tf_op jit(solution)/shard_map/conv/pallas_call | solution.py:224
  55.1 2.6 %convert_add_fusion = f32[512,1024]{1,0:T(8,128)S(1)} fusion(bf16[512,1024]{1,0:T(8,128)(2,1)} %collective-permute-done.6, bf16[512,512]{0,1:T(8,128)(2,1)S(1)} %bitcast.104, bf16[512,1024]{1,0:T(8,128)(2,1)S(1)} %bitcast.90), kind=kOutput, calls=%fused_computation.1 | convolution fusion | flops 537919488 | bytes 4718592 | tf_op jit(solution)/shard_map/dot_general | solution.py:284
  57.7 1.4 %copy-done.13 = f32[512,1024]{1,0:T(8,128)} copy-done((f32[512,1024]{1,0:T(8,128)}, f32[512,1024]{1,0:T(8,128)S(1)}, u32[]{:S(2)}) %copy-start.13) | copy-done | bytes 2097176
  60.0 2.6 %collective-permute-start.7 = (bf16[2,2,64,1024]{3,2,1,0:T(8,128)(2,1)}, bf16[2,2,64,1024]{3,2,1,0:T(8,128)(2,1)}, u32[]{:S(2)}, u32[]{:S(2)}) collective-permute-start(bf16[2,2,64,1024]{3,2,1,0:T(8,128)(2,1)} %fusion), channel_id=1, source_target_pairs={{0,4},{1,5},{2,6},{3,7},{4,0},{5,1},{6,2},{7,3},{8,12},{9,13},{10,... | collective-permute-start | bytes 1572872 | tf_op jit(solution)/shard_map/ppermute | solution.py:17
  63.2 1.5 %copy.27 = bf16[512,1312]{0,1:T(8,128)(2,1)} copy(bf16[512,1312]{1,0:T(8,128)(2,1)S(1)} %pad_maximum_fusion) | data formatting | bytes 2686976 | tf_op jit(solution)/shard_map/concatenate | solution.py:312
  64.7 10.4 %collective-permute-done.7 = bf16[2,2,64,1024]{3,2,1,0:T(8,128)(2,1)} collective-permute-done((bf16[2,2,64,1024]{3,2,1,0:T(8,128)(2,1)}, bf16[2,2,64,1024]{3,2,1,0:T(8,128)(2,1)}, u32[]{:S(2)}, u32[]{:S(2)}) %collective-permute-start.7) | collective-permute-done | bytes 524320 | tf_op jit(solution)/shard_map/ppermute | solution.py:17
  75.0 1.5 %bitcast_add_fusion = f32[2,2,64,1024]{3,2,1,0:T(8,128)S(1)} fusion(bf16[2,2,64,1024]{3,2,1,0:T(8,128)(2,1)} %collective-permute-done.7, f32[2,2,2,64,1024]{4,3,2,1,0:T(8,128)} %bitcast.98, s32[]{:T(128)S(6)} %select_n.92), kind=kLoop, calls=%fused_computation.6 | loop fusion | flops 524288 | bytes 2621444 | tf_op jit(solution)/shard_map/add | solution.py:40
  78.3 2.8 %collective-permute-start.8 = (bf16[2,64,1024]{2,1,0:T(8,128)(2,1)}, bf16[2,64,1024]{2,1,0:T(8,128)(2,1)S(1)}, u32[]{:S(2)}, u32[]{:S(2)}) collective-permute-start(bf16[2,64,1024]{2,1,0:T(8,128)(2,1)} %fusion.3), channel_id=1, source_target_pairs={{0,8},{1,9},{2,10},{3,11},{4,12},{5,13},{6,14},{7,15},{8,0},{9,1},... | collective-permute-start | bytes 786440 | tf_op jit(solution)/shard_map/ppermute | solution.py:17
  82.3 3.0 %result.1 = bf16[512,1024]{1,0:T(8,128)(2,1)} custom-call(bf16[512,1024]{1,0:T(8,128)(2,1)S(1)} %copy-done.6, bf16[1024,1024]{1,0:T(8,128)(2,1)S(1)} %copy-done.4, bf16[512,1024]{1,0:T(8,128)(2,1)S(1)} %bitcast.91), custom_call_target="tpu_custom_call" | custom-call | flops 1073741824 | bytes 5242880 | tf_op jit(solution)/shard_map/result/pallas_call | solution.py:82
  85.3 7.5 %collective-permute-done.8 = bf16[2,64,1024]{2,1,0:T(8,128)(2,1)S(1)} collective-permute-done((bf16[2,64,1024]{2,1,0:T(8,128)(2,1)}, bf16[2,64,1024]{2,1,0:T(8,128)(2,1)S(1)}, u32[]{:S(2)}, u32[]{:S(2)}) %collective-permute-start.8) | collective-permute-done | bytes 262176 | tf_op jit(solution)/shard_map/ppermute | solution.py:17
  94.2 1.8 %copy.28 = bf16[512,1312]{1,0:T(8,128)(2,1)S(1)} copy(bf16[512,1312]{0,1:T(8,128)(2,1)} %collective-permute-done.10) | data formatting | bytes 2686976 | tf_op jit(solution)/shard_map/ppermute | solution.py:17
  96.0 2.3 %maximum_add_fusion = f32[512,1312]{1,0:T(8,128)S(1)} fusion(f32[512,1024]{1,0:T(8,128)} %get-tuple-element.11, f32[512,288]{1,0:T(8,128)S(1)} %copy-done.8, bf16[512,1312]{1,0:T(8,128)(2,1)S(1)} %copy.28), kind=kLoop, calls=%fused_computation | loop fusion | flops 2015232 | bytes 6717440 | tf_op jit(solution)/shard_map/add | solution.py:313
  101.2 5.9 %collective-permute-done.14 = bf16[2,2,64,640]{3,2,0,1:T(8,128)(2,1)S(1)} collective-permute-done((bf16[2,2,64,640]{3,2,0,1:T(8,128)(2,1)S(1)}, bf16[2,2,64,640]{3,2,0,1:T(8,128)(2,1)S(1)}, u32[]{:S(2)}, u32[]{:S(2)}) %collective-permute-start.14) | collective-permute-done | bytes 327712 | tf_op jit(solution)/shard_map/ppermute | solution.py:17
  108.0 3.9 %collective-permute-done.11 = bf16[2,2,64,672]{3,2,1,0:T(8,128)(2,1)S(1)} collective-permute-done((bf16[2,2,64,672]{3,2,1,0:T(8,128)(2,1)S(1)}, bf16[2,2,64,672]{3,2,1,0:T(8,128)(2,1)S(1)}, u32[]{:S(2)}, u32[]{:S(2)}) %collective-permute-start.11) | collective-permute-done | bytes 344096 | tf_op jit(solution)/shard_map/ppermute | solution.py:17
  112.0 2.7 %collective-permute-start.12 = (bf16[2,64,672]{2,1,0:T(8,128)(2,1)S(1)}, bf16[2,64,672]{2,1,0:T(8,128)(2,1)S(1)}, u32[]{:S(2)}, u32[]{:S(2)}) collective-permute-start(bf16[2,64,672]{2,1,0:T(8,128)(2,1)S(1)} %fusion.5), channel_id=1, source_target_pairs={{0,8},{1,9},{2,10},{3,11},{4,12},{5,13},{6,14},{7,15},{8,0},{9,1},... | collective-permute-start | bytes 516104 | tf_op jit(solution)/shard_map/ppermute | solution.py:17
  115.8 2.3 %collective-permute-start.16 = (bf16[64,640]{1,0:T(8,128)(2,1)S(1)}, bf16[64,640]{1,0:T(8,128)(2,1)S(1)}, u32[]{:S(2)}, u32[]{:S(2)}) collective-permute-start(bf16[64,640]{1,0:T(8,128)(2,1)S(1)} %fusion.9), channel_id=1, source_target_pairs={{0,8},{1,9},{2,10},{3,11},{4,12},{5,13},{6,14},{7,15},{8,0},{9,1},... | collective-permute-start | bytes 245768 | tf_op jit(solution)/shard_map/ppermute | solution.py:17
  118.1 6.5 %collective-permute-done.12 = bf16[2,64,672]{2,1,0:T(8,128)(2,1)S(1)} collective-permute-done((bf16[2,64,672]{2,1,0:T(8,128)(2,1)S(1)}, bf16[2,64,672]{2,1,0:T(8,128)(2,1)S(1)}, u32[]{:S(2)}, u32[]{:S(2)}) %collective-permute-start.12) | collective-permute-done | bytes 172064 | tf_op jit(solution)/shard_map/ppermute | solution.py:17
  125.5 3.9 %collective-permute-done.13 = bf16[64,672]{1,0:T(8,128)(2,1)S(1)} collective-permute-done((bf16[64,672]{1,0:T(8,128)(2,1)S(1)}, bf16[64,672]{1,0:T(8,128)(2,1)S(1)}, u32[]{:S(2)}, u32[]{:S(2)}) %collective-permute-start.13) | collective-permute-done | bytes 86048 | tf_op jit(solution)/shard_map/ppermute | solution.py:17
  (91 shorter events, 24.5 us)
Async XLA Ops:
  0.6 5.9 %copy-start = (bf16[1,4,128,1024]{3,2,1,0:T(8,128)(2,1)S(1)}, bf16[1,4,128,1024]{3,2,1,0:T(8,128)(2,1)}, u32[]{:S(2)}) copy-start(bf16[1,4,128,1024]{3,2,1,0:T(8,128)(2,1)} %param.7) | copy-start | bytes 3145732
  0.6 5.9 %copy-start.2 = (bf16[1,4,128,1024]{3,2,1,0:T(8,128)(2,1)S(1)}, bf16[1,4,128,1024]{3,2,1,0:T(8,128)(2,1)}, u32[]{:S(2)}) copy-start(bf16[1,4,128,1024]{3,2,1,0:T(8,128)(2,1)} %param.9) | copy-start | bytes 3145732
  2.9 26.8 %collective-permute-start.4 = (bf16[4,256,256]{2,1,0:T(8,128)(2,1)}, bf16[4,256,256]{2,1,0:T(8,128)(2,1)}, u32[]{:S(2)}, u32[]{:S(2)}) collective-permute-start(bf16[4,256,256]{2,1,0:T(8,128)(2,1)} %get-tuple-element.19), channel_id=1, source_target_pairs={{0,2},{1,3},{2,0},{3,1},{4,6},{5,7},{6,4},{7,5},{8,10},{9,11},{10,... | collective-permute-start | bytes 1572872 | tf_op jit(solution)/shard_map/ppermute | solution.py:17
  6.6 32.9 %collective-permute-start.3 = (bf16[4,128,256]{2,1,0:T(8,128)(2,1)}, bf16[4,128,256]{2,1,0:T(8,128)(2,1)}, u32[]{:S(2)}, u32[]{:S(2)}) collective-permute-start(bf16[4,128,256]{2,1,0:T(8,128)(2,1)} %get-tuple-element.23), channel_id=1, source_target_pairs={{0,1},{1,0},{2,3},{3,2},{4,5},{5,4},{6,7},{7,6},{8,9},{9,8},{10,11... | collective-permute-start | bytes 786440 | tf_op jit(solution)/shard_map/ppermute | solution.py:17
  6.6 1.6 %copy-start.3 = (bf16[1024,1024]{1,0:T(8,128)(2,1)S(1)}, bf16[1024,1024]{1,0:T(8,128)(2,1)}, u32[]{:S(2)}) copy-start(bf16[1024,1024]{1,0:T(8,128)(2,1)} %weight_ref.2) | copy-start | bytes 6291460
  11.2 11.9 %collective-permute-start = (bf16[128,1024]{1,0:T(8,128)(2,1)}, bf16[128,1024]{1,0:T(8,128)(2,1)}, u32[]{:S(2)}, u32[]{:S(2)}) collective-permute-start(bf16[128,1024]{1,0:T(8,128)(2,1)} %get-tuple-element.21), channel_id=1, source_target_pairs={{2,4},{4,2},{3,5},{5,3},{6,8},{8,6},{7,9},{9,7},{10,12},{12,10},{1... | collective-permute-start | bytes 786440 | tf_op jit(solution)/shard_map/ppermute | solution.py:27
  12.5 16.0 %collective-permute-start.1 = (bf16[128,1024]{1,0:T(8,128)(2,1)}, bf16[128,1024]{1,0:T(8,128)(2,1)}, u32[]{:S(2)}, u32[]{:S(2)}) collective-permute-start(bf16[128,1024]{1,0:T(8,128)(2,1)} %get-tuple-element.20), channel_id=1, source_target_pairs={{0,2},{1,3},{2,0},{3,1},{4,6},{5,7},{6,4},{7,5},{8,10},{9,11},{10,... | collective-permute-start | bytes 786440 | tf_op jit(solution)/shard_map/ppermute | solution.py:17
  20.0 1.7 %copy-start.18 = (bf16[1,4,128,1024]{3,2,1,0:T(8,128)(2,1)S(1)}, bf16[1,4,128,1024]{3,2,1,0:T(8,128)(2,1)}, u32[]{:S(2)}) copy-start(bf16[1,4,128,1024]{3,2,1,0:T(8,128)(2,1)} %param.8) | copy-start | bytes 3145732
  21.7 33.4 %collective-permute-start.6 = (bf16[512,1024]{1,0:T(8,128)(2,1)}, bf16[512,1024]{1,0:T(8,128)(2,1)}, u32[]{:S(2)}, u32[]{:S(2)}) collective-permute-start(bf16[512,1024]{1,0:T(8,128)(2,1)} %convolution_convert_fusion), channel_id=1, source_target_pairs={{0,1},{1,0},{2,3},{3,2},{4,5},{5,4},{6,7},{7,6},{8,9},{9,8},{10,11... | collective-permute-start | bytes 3145736 | tf_op jit(solution)/shard_map/ppermute | solution.py:17
  23.1 9.2 %copy-start.14 = (bf16[512,1024]{0,1:T(8,128)(2,1)S(1)}, bf16[512,1024]{0,1:T(8,128)(2,1)}, u32[]{:S(2)}) copy-start(bf16[512,1024]{0,1:T(8,128)(2,1)} %copy.32) | copy-start | bytes 3145732
  29.6 3.7 %copy-start.11 = (bf16[128,1024]{1,0:T(8,128)(2,1)}, bf16[128,1024]{1,0:T(8,128)(2,1)S(1)}, u32[]{:S(2)}) copy-start(bf16[128,1024]{1,0:T(8,128)(2,1)S(1)} %get-tuple-element.27.refs_2_) | copy-start | bytes 786436
  31.6 7.9 %collective-permute-start.5 = (bf16[4,128,256]{2,1,0:T(8,128)(2,1)}, bf16[4,128,256]{2,1,0:T(8,128)(2,1)}, u32[]{:S(2)}, u32[]{:S(2)}) collective-permute-start(bf16[4,128,256]{2,1,0:T(8,128)(2,1)} %get-tuple-element.25), channel_id=1, source_target_pairs={{0,1},{1,0},{2,3},{3,2},{4,5},{5,4},{6,7},{7,6},{8,9},{9,8},{10,11... | collective-permute-start | bytes 786440 | tf_op jit(solution)/shard_map/ppermute | solution.py:17
  31.7 7.8 %collective-permute-start.2 = (bf16[6,1024]{1,0:T(8,128)(2,1)S(1)}, bf16[6,1024]{1,0:T(8,128)(2,1)S(1)}, u32[]{:S(2)}, u32[]{:S(2)}) collective-permute-start(bf16[6,1024]{1,0:T(8,128)(2,1)S(1)} %pad_maximum_fusion.2), channel_id=1, source_target_pairs={{0,1},{1,0},{2,3},{3,2},{4,5},{5,4},{6,7},{7,6},{8,9},{9,8},{10,11... | collective-permute-start | bytes 36872 | tf_op jit(solution)/shard_map/ppermute | solution.py:17
  37.2 2.1 %copy-start.1 = (bf16[4,9,256,256]{3,2,1,0:T(8,128)(2,1)}, bf16[4,9,256,256]{3,2,1,0:T(8,128)(2,1)S(1)}, u32[]{:S(2)}) copy-start(bf16[4,9,256,256]{3,2,1,0:T(8,128)(2,1)S(1)} %spread.1.refs_6_) | copy-start | bytes 14155780
  44.7 10.3 %copy-start.17 = (bf16[512,8,1,64]{0,3,2,1:T(8,128)(2,1)S(1)}, bf16[512,8,1,64]{0,3,2,1:T(8,128)(2,1)}, u32[]{:S(2)}) copy-start(bf16[512,8,1,64]{0,3,2,1:T(8,128)(2,1)} %get-tuple-element.15) | copy-start | bytes 1572868
  55.1 2.6 %copy-start.5 = (bf16[512,1024]{1,0:T(8,128)(2,1)}, bf16[512,1024]{1,0:T(8,128)(2,1)S(1)}, u32[]{:S(2)}) copy-start(bf16[512,1024]{1,0:T(8,128)(2,1)S(1)} %get-tuple-element.9.first_ref) | copy-start | bytes 3145732
  55.1 2.6 %copy-start.7 = (f32[512,288]{1,0:T(8,128)}, f32[512,288]{1,0:T(8,128)S(1)}, u32[]{:S(2)}) copy-start(f32[512,288]{1,0:T(8,128)S(1)} %get-tuple-element.10) | copy-start | bytes 1769476
  57.7 1.4 %copy-start.13 = (f32[512,1024]{1,0:T(8,128)}, f32[512,1024]{1,0:T(8,128)S(1)}, u32[]{:S(2)}) copy-start(f32[512,1024]{1,0:T(8,128)S(1)} %convert_add_fusion) | copy-start | bytes 6291460
  60.0 15.0 %collective-permute-start.7 = (bf16[2,2,64,1024]{3,2,1,0:T(8,128)(2,1)}, bf16[2,2,64,1024]{3,2,1,0:T(8,128)(2,1)}, u32[]{:S(2)}, u32[]{:S(2)}) collective-permute-start(bf16[2,2,64,1024]{3,2,1,0:T(8,128)(2,1)} %fusion), channel_id=1, source_target_pairs={{0,4},{1,5},{2,6},{3,7},{4,0},{5,1},{6,2},{7,3},{8,12},{9,13},{10,... | collective-permute-start | bytes 1572872 | tf_op jit(solution)/shard_map/ppermute | solution.py:17
  64.7 16.4 %copy-start.4 = (bf16[1024,1024]{1,0:T(8,128)(2,1)S(1)}, bf16[1024,1024]{1,0:T(8,128)(2,1)}, u32[]{:S(2)}) copy-start(bf16[1024,1024]{1,0:T(8,128)(2,1)} %weight_ref.3) | copy-start | bytes 6291460
  64.7 29.5 %collective-permute-start.10 = (bf16[512,1312]{0,1:T(8,128)(2,1)}, bf16[512,1312]{0,1:T(8,128)(2,1)}, u32[]{:S(2)}, u32[]{:S(2)}) collective-permute-start(bf16[512,1312]{0,1:T(8,128)(2,1)} %copy.27), channel_id=1, source_target_pairs={{0,1},{1,0},{2,3},{3,2},{4,5},{5,4},{6,7},{7,6},{8,9},{9,8},{10,11... | collective-permute-start | bytes 4030472 | tf_op jit(solution)/shard_map/ppermute | solution.py:17
  78.3 14.5 %collective-permute-start.8 = (bf16[2,64,1024]{2,1,0:T(8,128)(2,1)}, bf16[2,64,1024]{2,1,0:T(8,128)(2,1)S(1)}, u32[]{:S(2)}, u32[]{:S(2)}) collective-permute-start(bf16[2,64,1024]{2,1,0:T(8,128)(2,1)} %fusion.3), channel_id=1, source_target_pairs={{0,8},{1,9},{2,10},{3,11},{4,12},{5,13},{6,14},{7,15},{8,0},{9,1},... | collective-permute-start | bytes 786440 | tf_op jit(solution)/shard_map/ppermute | solution.py:17
  81.0 1.2 copy-start.6
  82.3 10.5 %copy-start.16 = (f32[2,2,64,1024]{3,2,1,0:T(8,128)S(1)}, f32[2,2,64,1024]{3,2,1,0:T(8,128)}, u32[]{:S(2)}) copy-start(f32[2,2,64,1024]{3,2,1,0:T(8,128)} %copy-done.15) | copy-start | bytes 3145732
  85.3 10.8 %copy-start.8 = (f32[512,288]{1,0:T(8,128)S(1)}, f32[512,288]{1,0:T(8,128)}, u32[]{:S(2)}) copy-start(f32[512,288]{1,0:T(8,128)} %copy-done.7) | copy-start | bytes 1769476
  92.9 6.7 %collective-permute-start.9 = (bf16[64,1024]{1,0:T(8,128)(2,1)S(1)}, bf16[64,1024]{1,0:T(8,128)(2,1)S(1)}, u32[]{:S(2)}, u32[]{:S(2)}) collective-permute-start(bf16[64,1024]{1,0:T(8,128)(2,1)S(1)} %fusion.7), channel_id=1, source_target_pairs={{0,2},{1,3},{2,0},{3,1},{4,6},{5,7},{6,4},{7,5},{8,10},{9,11},{10,... | collective-permute-start | bytes 393224 | tf_op jit(solution)/shard_map/ppermute | solution.py:17
  98.8 8.3 %collective-permute-start.14 = (bf16[2,2,64,640]{3,2,0,1:T(8,128)(2,1)S(1)}, bf16[2,2,64,640]{3,2,0,1:T(8,128)(2,1)S(1)}, u32[]{:S(2)}, u32[]{:S(2)}) collective-permute-start(bf16[2,2,64,640]{3,2,0,1:T(8,128)(2,1)S(1)} %fusion.2), channel_id=1, source_target_pairs={{0,2},{1,3},{2,0},{3,1},{4,6},{5,7},{6,4},{7,5},{8,10},{9,11},{10,... | collective-permute-start | bytes 983048 | tf_op jit(solution)/shard_map/ppermute | solution.py:17
  100.5 11.4 %collective-permute-start.11 = (bf16[2,2,64,672]{3,2,1,0:T(8,128)(2,1)S(1)}, bf16[2,2,64,672]{3,2,1,0:T(8,128)(2,1)S(1)}, u32[]{:S(2)}, u32[]{:S(2)}) collective-permute-start(bf16[2,2,64,672]{3,2,1,0:T(8,128)(2,1)S(1)} %fusion.1), channel_id=1, source_target_pairs={{0,4},{1,5},{2,6},{3,7},{4,0},{5,1},{6,2},{7,3},{8,12},{9,13},{10,... | collective-permute-start | bytes 1032200 | tf_op jit(solution)/shard_map/ppermute | solution.py:17
  107.2 8.5 %collective-permute-start.15 = (bf16[2,64,640]{2,1,0:T(8,128)(2,1)S(1)}, bf16[2,64,640]{2,1,0:T(8,128)(2,1)S(1)}, u32[]{:S(2)}, u32[]{:S(2)}) collective-permute-start(bf16[2,64,640]{2,1,0:T(8,128)(2,1)S(1)} %fusion.6), channel_id=1, source_target_pairs={{0,4},{1,5},{2,6},{3,7},{4,0},{5,1},{6,2},{7,3},{8,12},{9,13},{10,... | collective-permute-start | bytes 491528 | tf_op jit(solution)/shard_map/ppermute | solution.py:17
  112.0 12.7 %collective-permute-start.12 = (bf16[2,64,672]{2,1,0:T(8,128)(2,1)S(1)}, bf16[2,64,672]{2,1,0:T(8,128)(2,1)S(1)}, u32[]{:S(2)}, u32[]{:S(2)}) collective-permute-start(bf16[2,64,672]{2,1,0:T(8,128)(2,1)S(1)} %fusion.5), channel_id=1, source_target_pairs={{0,8},{1,9},{2,10},{3,11},{4,12},{5,13},{6,14},{7,15},{8,0},{9,1},... | collective-permute-start | bytes 516104 | tf_op jit(solution)/shard_map/ppermute | solution.py:17
  115.8 9.7 %collective-permute-start.16 = (bf16[64,640]{1,0:T(8,128)(2,1)S(1)}, bf16[64,640]{1,0:T(8,128)(2,1)S(1)}, u32[]{:S(2)}, u32[]{:S(2)}) collective-permute-start(bf16[64,640]{1,0:T(8,128)(2,1)S(1)} %fusion.9), channel_id=1, source_target_pairs={{0,8},{1,9},{2,10},{3,11},{4,12},{5,13},{6,14},{7,15},{8,0},{9,1},... | collective-permute-start | bytes 245768 | tf_op jit(solution)/shard_map/ppermute | solution.py:17
  124.7 4.7 %collective-permute-start.13 = (bf16[64,672]{1,0:T(8,128)(2,1)S(1)}, bf16[64,672]{1,0:T(8,128)(2,1)S(1)}, u32[]{:S(2)}, u32[]{:S(2)}) collective-permute-start(bf16[64,672]{1,0:T(8,128)(2,1)S(1)} %fusion.8), channel_id=1, source_target_pairs={{0,2},{1,3},{2,0},{3,1},{4,6},{5,7},{6,4},{7,5},{8,10},{9,11},{10,... | collective-permute-start | bytes 258056 | tf_op jit(solution)/shard_map/ppermute | solution.py:17
  (4 other events, 4.0 us)

commit v2 on v0

v2 whole, which is shorter than its diff:
```python
import math

import jax
import jax.numpy as jnp
from jax import lax
from jax.experimental import pallas as pl
from jax.experimental.pallas import tpu as pltpu
from jax.sharding import PartitionSpec as P

BF = jnp.bfloat16
F32 = jnp.float32
TAPS = 9
ROWS = 4


def exchange(array, bit):
    count = lax.axis_size("space")
    return lax.ppermute(array, "space", [(i, i ^ (1 << bit)) for i in range(count)])


def exchange_across(array):
    count = lax.axis_size("space")
    route = []
    for low in range(count):
        high = low + 2
        if low & 2 and high < count:
            route += [(low, high), (high, low)]
    return lax.ppermute(array, "space", route)


def after(value, *others):
    return lax.optimization_barrier((value, *others))[0]


def call(kernel, name, place, operands, outs, scratch=(), megabytes=12, pinned=True):
    inputs, specs = [], [pl.BlockSpec(memory_space=pltpu.SMEM)]
    for operand in operands:
        if isinstance(operand, tuple):
            inputs.append(pltpu.with_memory_space_constraint(operand[0], pltpu.HBM))
            specs.append(pl.BlockSpec(memory_space=pltpu.HBM))
        else:
            inputs.append(operand)
            specs.append(pl.BlockSpec(memory_space=pltpu.VMEM))
    kind = pltpu.VMEM if pinned else jax.ShapeDtypeStruct
    return pl.pallas_call(
        kernel,
        in_specs=specs,
        out_specs=[pl.BlockSpec(memory_space=pltpu.VMEM)] * len(outs),
        out_shape=[kind(*out) for out in outs],
        scratch_shapes=scratch,
        compiler_params=pltpu.CompilerParams(vmem_limit_bytes=megabytes * 1024 * 1024),
        cost_estimate=pl.CostEstimate(flops=0, bytes_accessed=0, transcendentals=0),
        name=name,
    )(place, *inputs)


def nt_dot(a, b):
    return lax.dot_general(a, b, (((1,), (1,)), ((), ())), preferred_element_type=F32)


def halves(value, bit):
    low, high = value[:, 0], value[:, 1]
    return jnp.where(bit == 0, low, high), jnp.where(bit == 0, high, low)


def pack_kernel(
    place_ref, second_ref, grad_ref, mask_ref,
    near_own_ref, near_core_ref, far_ref, edge_ref, grads_ref, masks_ref, sems,
):
    rows, width, _ = near_own_ref.shape
    core, half = place_ref[0], place_ref[1]
    edge_at = (1 - core) * (width - 16)
    copies = []
    for row in range(ROWS):
        there = pl.ds(pl.multiple_of(row * width + edge_at, 16), 16)
        copies.append((grad_ref.at[there], grads_ref.at[row]))
        copies.append((mask_ref.at[there], masks_ref.at[row]))
    for target, row_at, column_at in (
        (far_ref.at[0], 1 - half, core),
        (far_ref.at[1], 1 - half, 1 - core),
        (near_core_ref, half, 1 - core),
        (near_own_ref, half, core),
    ):
        source = second_ref.at[0, pl.ds(row_at * rows, rows), pl.ds(column_at * width, width)]
        copies.append((source, target))
    copies = [pltpu.make_async_copy(*pair, sems.at[at]) for at, pair in enumerate(copies)]
    for copy in copies:
        copy.start()
    for copy in copies:
        copy.wait()
    lines = []
    for buffer in (grads_ref, masks_ref):
        for row in range(ROWS):
            value = buffer[row].astype(F32)
            lines.append(jnp.where(core == 0, value[15:16], value[0:1]))
    lines += [jnp.zeros_like(lines[0])] * (16 - 2 * ROWS)
    edge_ref[...] = jnp.concatenate(lines).astype(BF)


def pack_of(place, second_input, grad_rows, third_rows):
    _, rows, columns, shard = second_input.shape
    channels = grad_rows.shape[1]
    out = (rows // 2, columns // 2, shard)
    return call(
        pack_kernel,
        "pack",
        place,
        [(second_input,), (grad_rows,), (third_rows,)],
        [(out, BF), (out, BF), ((2, *out), BF), ((16, channels), BF)],
        [
            pltpu.VMEM((ROWS, 16, channels), BF),
            pltpu.VMEM((ROWS, 16, channels), BF),
            pltpu.SemaphoreType.DMA((4 + 2 * ROWS,)),
        ],
    )


def inner_kernel(
    place_ref, grad_ref, weight_ref, mask_ref, edge_ref,
    out_ref, rim_ref, inside_ref, outside_ref,
):
    channels = weight_ref.shape[0]
    step = channels // 2
    width = grad_ref.shape[0] // ROWS
    half = place_ref[1]
    for part in range(2):
        here = slice(part * step, (part + 1) * step)
        weight = weight_ref[here, :]
        back = nt_dot(grad_ref[...], weight)
        inner = jnp.where(mask_ref[:, here] > 0, back, 0.0).astype(BF)
        out_ref[:, here] = inner
        beside = nt_dot(edge_ref[...], weight)
        kept = edge_ref[:, here].astype(F32)
        lines = [
            jnp.where(kept[ROWS + row : ROWS + row + 1] > 0, beside[row : row + 1], 0.0)
            for row in range(ROWS)
        ]
        nothing = [jnp.zeros_like(lines[0])]
        rim_ref[:, here] = jnp.concatenate(lines + nothing * (16 - ROWS)).astype(BF)
        first, last = inner[:width], inner[(ROWS - 1) * width :]
        upper = jnp.concatenate([lines[0]] + nothing * 15).astype(BF)
        lower = jnp.concatenate([lines[-1]] + nothing * 15).astype(BF)
        inside_ref[:width, here] = jnp.where(half == 0, last, first)
        inside_ref[width:, here] = jnp.where(half == 0, lower, upper)
        outside_ref[:width, here] = jnp.where(half == 0, first, last)
        outside_ref[width:, here] = jnp.where(half == 0, upper, lower)


def inner_of(place, grad_rows, third_weight, third_rows, edge):
    rows, channels = grad_rows.shape
    rim = ((rows // ROWS + 16, channels), BF)
    return call(
        inner_kernel,
        "inner",
        place,
        [grad_rows, third_weight, third_rows, edge],
        [((rows, channels), BF), ((16, channels), BF), rim, rim],
    )


def third_kernel(
    piece, place_ref, left_hbm, right_hbm, weight_hbm,
    keep_ref, send_ref, left_ref, right_ref, weight_ref, sems,
):
    copies = [
        pltpu.make_async_copy(*pair, sems.at[at])
        for at, pair in enumerate(
            ((left_hbm, left_ref), (right_hbm, right_ref), (weight_hbm, weight_ref))
        )
    ]
    for copy in copies:
        copy.start()
    copies[0].wait()
    copies[1].wait()
    channels = left_ref.shape[1]
    step = channels // 4
    for part in range(4):
        term = lax.dot_general(
            left_ref[:, part * step : (part + 1) * step],
            right_ref[...],
            (((0,), (0,)), ((), ())),
            preferred_element_type=F32,
        )
        columns = term.shape[1]
        keep, send = halves(term.reshape(step // (2 * piece), 2, piece, columns), place_ref[0])
        here = slice(part * step // 2, (part + 1) * step // 2)
        keep_ref[here, :] = keep.reshape(step // 2, columns)
        send_ref[here, :] = send.reshape(step // 2, columns).astype(BF)
    copies[2].wait()


def third_of(place, third_rows, grad_rows, third_weight, piece):
    positions, channels = grad_rows.shape
    wide = ((positions, channels), BF)
    return call(
        lambda *refs: third_kernel(piece, *refs),
        "third",
        place,
        [(third_rows,), (grad_rows,), (third_weight,)],
        [
            ((channels // 2, channels), F32),
            ((channels // 2, channels), BF),
            wide,
            wide,
            ((channels, channels), BF),
        ],
        [pltpu.SemaphoreType.DMA((3,))],
    )


def fold_kernel(bit, place_ref, total_ref, received_ref, keep_ref, send_ref):
    for at in range(total_ref.shape[0]):
        total = total_ref[at] + received_ref[at].astype(F32)
        keep, send = halves(total[None], place_ref[bit])
        keep_ref[at] = keep[0]
        send_ref[at] = send[0].astype(BF)


def fold_of(place, total, received, left, bit, piece):
    at = left.index(bit)
    columns = total.shape[-1]
    shape = (1 << at, 2, piece << (len(left) - at - 1), columns)
    out = (shape[0], *shape[2:])
    return call(
        lambda *refs: fold_kernel(bit, *refs),
        "fold",
        place,
        [total.reshape(shape), received.reshape(shape)],
        [(out, F32), (out, BF)],
    )


def summed_up(place, keep, send, order, left, piece):
    received = exchange(send, order[0])
    for bit in order[1:]:
        keep, send = fold_of(place, keep, received, left, bit, piece)
        left = [b for b in left if b != bit]
        received = exchange(send, bit)
    columns = keep.shape[-1]
    return keep.reshape(piece, columns), received.reshape(piece, columns)


def ready_kernel(gw, piece, place_ref, weight_ref, input_ref, spread_ref, keep_ref, send_ref):
    shards, _, _, step = spread_ref.shape
    positions = input_ref.shape[0]
    source = lax.broadcasted_iota(jnp.int32, (gw, step), 0)
    column = lax.broadcasted_iota(jnp.int32, (gw, step), 1) % gw
    chooser = jnp.where(source == column, 1.0, 0.0).astype(BF)
    row_group = lax.broadcasted_iota(jnp.int32, (step, step), 0) // gw
    column_group = lax.broadcasted_iota(jnp.int32, (step, step), 1) // gw
    mine = row_group == column_group
    for shard in range(shards):
        here = slice(shard * step, (shard + 1) * step)
        for tap in range(TAPS):
            copies = lax.dot_general(
                weight_ref[tap * gw : (tap + 1) * gw, here],
                chooser,
                (((0,), (0,)), ((), ())),
                preferred_element_type=F32,
            )
            spread_ref[shard, tap // 3, (tap % 3) * step : (tap % 3 + 1) * step, :] = jnp.where(
                mine, copies, 0.0
            ).astype(BF)
        turned = input_ref[:, here]
        if piece % 16:
            turned = turned.astype(F32)
        turned = turned.T.reshape(step // (2 * piece), 2, piece, positions)
        keep, send = halves(turned, place_ref[0])
        here = slice(shard * step // 2, (shard + 1) * step // 2)
        keep_ref[here, :] = keep.reshape(step // 2, positions).astype(BF)
        send_ref[here, :] = send.reshape(step // 2, positions).astype(BF)


def ready_of(place, group_weight, input_rows, shard, gw, piece):
    positions, channels = input_rows.shape
    turned = ((channels // 2, positions), BF)
    return call(
        lambda *refs: ready_kernel(gw, piece, *refs),
        "ready",
        place,
        [group_weight, input_rows],
        [((channels // shard, 3, 3 * shard, shard), BF), turned, turned],
    )


def shifted(line, left, right):
    wide = line.astype(F32)
    width = wide.shape[0]
    at = lax.broadcasted_iota(jnp.int32, wide.shape, 0)
    return (
        jnp.where(at == width - 1, right, pltpu.roll(wide, width - 1, 0)).astype(BF),
        line,
        jnp.where(at == 0, left, pltpu.roll(wide, 1, 0)).astype(BF),
    )


def own_groups(term, gw):
    step = term.shape[1]
    lane_group = lax.broadcasted_iota(jnp.int32, (gw, step), 1) // gw
    mine = term[:gw]
    for group in range(1, step // gw):
        mine = jnp.where(lane_group == group, term[group * gw : (group + 1) * gw], mine)
    return mine


def body_kernel(
    gw, near, place_ref, inner_ref, edge_ref, own_ref, other_ref, spread_ref,
    back_ref, term_ref, window_ref,
):
    positions = inner_ref.shape[0]
    step = own_ref.shape[2]
    width = positions // ROWS
    core = place_ref[0]
    side = place_ref[1] if near else 1 - place_ref[1]
    for slot, second_ref in enumerate((own_ref, other_ref)):
        shard = 2 * side + (core if slot == 0 else 1 - core)
        columns = pl.ds(pl.multiple_of(shard * step, step), step)
        edges = edge_ref[:, columns].astype(F32)
        for row in range(ROWS):
            here = pl.ds(row * width, width)
            edge = edges[row : row + 1]
            left, right = jnp.where(core == 1, edge, 0.0), jnp.where(core == 0, edge, 0.0)
            for at, line in enumerate(shifted(inner_ref[here, columns], left, right)):
                window_ref[here, at * step : (at + 1) * step] = line
        flipped = second_ref[...].reshape(positions, step).T
        for tap_row in (1, 0, 2):
            count = ROWS if tap_row == 1 else ROWS - 1
            take = pl.ds(width if tap_row == 0 else 0, count * width)
            start = width if tap_row == 2 else 0
            put = pl.ds(start, count * width)
            window = window_ref[take, :]
            back = jnp.dot(window, spread_ref[shard, tap_row], preferred_element_type=F32)
            term = jnp.dot(
                flipped[:, start : start + count * width], window, preferred_element_type=F32
            )
            for tap_col in range(3):
                tap = 3 * tap_row + tap_col
                term_ref[slot, tap * gw : (tap + 1) * gw, :] = own_groups(
                    term[:, tap_col * step : (tap_col + 1) * step], gw
                )
            if tap_row == 1:
                back_ref[slot] = back
            else:
                back_ref[slot, put, :] += back


def body_of(place, near, inner, edge, own, other, spread, gw):
    positions = inner.shape[0]
    shard = own.shape[2]
    return call(
        lambda *refs: body_kernel(gw, near, *refs),
        "body_near" if near else "body_far",
        place,
        [inner, edge, own, other, spread],
        [((2, positions, shard), F32), ((2, TAPS * gw, shard), F32)],
        [pltpu.VMEM((positions, 3 * shard), BF)],
    )


def close_kernel(
    gw, piece, near, place_ref, back_ref, term_ref, own_ref, other_ref, inside_ref, outside_ref,
    spread_ref, keep_in_ref, send_in_ref,
    first_ref, keep_ref, send_ref, group_keep_ref, group_send_ref,
):
    _, positions, step = back_ref.shape
    width = positions // ROWS
    core, half = place_ref[0], place_ref[1]
    side = half if near else 1 - half
    for slot, second_ref in enumerate((own_ref, other_ref)):
        turn = core if slot == 0 else 1 - core
        shard = 2 * side + turn
        columns = pl.ds(pl.multiple_of(shard * step, step), step)
        inside, outside = inside_ref[:, columns], outside_ref[:, columns]
        second = second_ref[...].reshape(positions, step)
        backs, terms = {}, {}
        for tap_row, row in ((2, 0), (0, ROWS - 1)):
            rim = jnp.where(half == (0 if row == 0 else 1), outside, inside)
            edge = rim[width:].astype(F32)[0:1]
            left, right = jnp.where(core == 1, edge, 0.0), jnp.where(core == 0, edge, 0.0)
            flipped = second[row * width : (row + 1) * width].T
            window = jnp.concatenate(shifted(rim[:width], left, right), 1)
            backs[row] = jnp.dot(window, spread_ref[shard, tap_row], preferred_element_type=F32)
            term = jnp.dot(flipped, window, preferred_element_type=F32)
            terms[tap_row] = [
                own_groups(term[:, at * step : (at + 1) * step], gw) for at in range(3)
            ]
        lines = []
        for row in range(ROWS):
            here = slice(row * width, (row + 1) * width)
            back = back_ref[slot, here, :]
            if row in backs:
                back = back + backs[row]
            lines.append(jnp.where(second[here] > 0, back, 0.0).astype(BF))
        first = jnp.concatenate(lines)
        place_at = pl.ds(pl.multiple_of(turn * step, step), step)
        first_ref[:, place_at] = first
        keep_ref[:, place_at] = jnp.dot(keep_in_ref[...], first, preferred_element_type=F32)
        send_ref[:, place_at] = jnp.dot(
            send_in_ref[...], first, preferred_element_type=F32
        ).astype(BF)
        term = term_ref[slot]
        parts = []
        for tap_row in range(3):
            part = term[3 * tap_row * gw : 3 * (tap_row + 1) * gw]
            if tap_row in terms:
                part = part + jnp.concatenate(terms[tap_row])
            parts.append(part)
        turned = jnp.concatenate(parts).T.reshape(step // (2 * piece), 2, piece, TAPS * gw)
        keep, send = halves(turned, core)
        here = pl.ds(pl.multiple_of(turn * (step // 2), step // 2), step // 2)
        group_keep_ref[here, :] = keep.reshape(step // 2, TAPS * gw)
        group_send_ref[here, :] = send.reshape(step // 2, TAPS * gw).astype(BF)


def close_of(place, near, back, term, own, other, inside, outside, spread, keep_in, send_in, piece):
    _, positions, shard = back.shape
    rows = keep_in.shape[0]
    gw = term.shape[1] // TAPS
    return call(
        lambda *refs: close_kernel(gw, piece, near, *refs),
        "close_near" if near else "close_far",
        place,
        [back, term, own, other, inside, outside, spread, keep_in, send_in],
        [
            ((positions, 2 * shard), BF),
            ((rows, 2 * shard), F32),
            ((rows, 2 * shard), BF),
            ((shard, TAPS * gw), F32),
            ((shard, TAPS * gw), BF),
        ],
    )


def split_kernel(
    piece,
    place_ref,
    near_ref,
    far_ref,
    near_got_ref,
    far_got_ref,
    group_near_ref,
    group_far_ref,
    group_near_got_ref,
    group_far_got_ref,
    one_keep_ref,
    one_send_ref,
    two_keep_ref,
    two_send_ref,
):
    half = place_ref[1]
    pre = one_keep_ref.shape[0]
    size = 4 * piece

    def by_second(value):
        keep, send = halves(value.reshape(1, 2, size // 2, value.shape[1]), place_ref[2])
        return keep[0], send[0].astype(BF)

    def by_first(value):
        keep, send = halves(value.reshape(2, 2, piece, value.shape[1]), half)
        rows = (size // 2, value.shape[1])
        return keep.reshape(rows), send.reshape(rows).astype(BF)

    for at in range(pre):
        here = slice(at * size, (at + 1) * size)
        near = near_ref[here, :] + near_got_ref[here, :].astype(F32)
        far = far_ref[here, :] + far_got_ref[here, :].astype(F32)
        low = jnp.where(half == 0, near, far)
        high = jnp.where(half == 0, far, near)
        there = slice(at % (pre // 2) * size, (at % (pre // 2) + 1) * size)
        group = jnp.where(
            half == at // (pre // 2),
            group_near_ref[there, :] + group_near_got_ref[there, :].astype(F32),
            group_far_ref[there, :] + group_far_got_ref[there, :].astype(F32),
        )
        cut = low.shape[1] // 2
        one_keep_ref[at, :, :cut], one_send_ref[at, :, :cut] = by_second(low[:, :cut])
        one_keep_ref[at, :, cut:], one_send_ref[at, :, cut:] = by_second(group)
        two_keep_ref[at, :, :cut], two_send_ref[at, :, :cut] = by_first(low[:, cut:])
        two_keep_ref[at, :, cut:], two_send_ref[at, :, cut:] = by_first(high)


def split_of(place, near, far, near_got, far_got, group, group_got, piece):
    rows, columns = near.shape
    pre = rows // (4 * piece)
    cut = columns // 2
    outs = []
    for size in (cut + group[0].shape[1], cut + columns):
        for kind in (F32, BF):
            outs.append(((pre, 2 * piece, size), kind))
    return call(
        lambda *refs: split_kernel(piece, *refs),
        "split",
        place,
        [near, far, near_got, far_got, *group, *group_got],
        outs,
    )


def last_kernel(scale, place_ref, one_ref, one_got_ref, two_ref, two_got_ref, first_ref, group_ref):
    one = (one_ref[...] + one_got_ref[...].astype(F32)) * scale
    cut = one.shape[1] - group_ref.shape[1]
    first_ref[:, :cut] = one[:, :cut]
    group_ref[...] = one[:, cut:]
    first_ref[:, cut:] = (two_ref[...] + two_got_ref[...].astype(F32)) * scale


def last_of(place, scale, one, one_got, two, two_got, channels, group_columns):
    piece = one.shape[0]
    return call(
        lambda *refs: last_kernel(scale, *refs),
        "last",
        place,
        [one, one_got, two, two_got],
        [((piece, channels), F32), ((piece, group_columns), F32)],
        pinned=False,
    )


def result_kernel(place_ref, near_ref, far_ref, grad_ref, weight_hbm, out_hbm, weight_ref, out_ref, sems):
    channels = grad_ref.shape[1]
    step = channels // 4
    halfway = channels // 2
    pieces = [pl.ds(part * step, step) for part in range(4)]
    copies = [
        pltpu.make_async_copy(weight_hbm.at[here], weight_ref.at[here], sems.at[part])
        for part, here in enumerate(pieces)
    ]
    for copy in copies:
        copy.start()
    near = pl.ds(pl.multiple_of(place_ref[1] * halfway, halfway), halfway)
    far = pl.ds(pl.multiple_of((1 - place_ref[1]) * halfway, halfway), halfway)
    outs = []
    for part, here in enumerate(pieces):
        copies[part].wait()
        summed = nt_dot(near_ref[...], weight_ref[here, near])
        summed += nt_dot(far_ref[...], weight_ref[here, far])
        columns = slice(part * step, (part + 1) * step)
        out_ref[:, columns] = (summed + grad_ref[:, columns].astype(F32)).astype(BF)
        outs.append(pltpu.make_async_copy(out_ref.at[:, here], out_hbm.at[:, here], sems.at[4 + part]))
        outs[-1].start()
    for out in outs:
        out.wait()


def result_of(place, near, far, first_weight, grad_rows):
    rows, channels = grad_rows.shape
    vmem, hbm = (pl.BlockSpec(memory_space=kind) for kind in (pltpu.VMEM, pltpu.HBM))
    return pl.pallas_call(
        result_kernel,
        in_specs=[pl.BlockSpec(memory_space=pltpu.SMEM), vmem, vmem, vmem, hbm],
        out_specs=hbm,
        out_shape=jax.ShapeDtypeStruct((rows, channels), BF),
        scratch_shapes=[
            pltpu.VMEM((channels, channels), BF),
            pltpu.VMEM((rows, channels), BF),
            pltpu.SemaphoreType.DMA((8,)),
        ],
        compiler_params=pltpu.CompilerParams(vmem_limit_bytes=12 * 1024 * 1024),
        cost_estimate=pl.CostEstimate(flops=0, bytes_accessed=0, transcendentals=0),
        name="result",
    )(place, near, far, grad_rows, pltpu.with_memory_space_constraint(first_weight, pltpu.HBM))


def per_device(
    outer_grad, block_input, third_input, second_input, third_weight, group_weight, first_weight
):
    devices = lax.axis_size("space")
    position = lax.axis_index("space")
    n_bits = devices.bit_length() - 1
    place = (position >> jnp.arange(n_bits, dtype=jnp.int32)) & 1
    place = place.astype(jnp.int32)
    _, tile_rows, width, channels = outer_grad.shape
    positions = tile_rows * width
    shard = channels // 4
    gw = group_weight.shape[1] // TAPS
    piece = channels // devices
    normalizer = 1.0 / math.sqrt(positions * devices)
    grad_rows = outer_grad.reshape(positions, channels)
    third_rows = third_input.reshape(positions, channels)
    input_rows = block_input.reshape(positions, channels)
    left = list(range(n_bits - 1, 0, -1))
    z_first = [*range(2, n_bits), 1]
    x_first = [*range(1, n_bits)]

    near_own, near_core, far_sent, edge = pack_of(place, second_input, grad_rows, third_rows)
    edge_got = exchange(edge, 0)
    near_other = exchange(near_core, 0)
    far = exchange(far_sent, 1)

    kept, sent, third_copy, grad_copy, weight_copy = third_of(
        after(place, edge), third_rows, grad_rows, third_weight, piece
    )
    inner, edge, inside, outside = inner_of(
        after(place, sent), grad_copy, weight_copy, third_copy, edge_got
    )
    got = exchange(sent, 0)
    kept, sent = fold_of(after(place, inside), kept, got, left, 2, piece)
    inside = exchange(inside, 1)
    outside = exchange_across(outside)

    spread, keep_in, send_in = ready_of(
        after(place, sent, far), group_weight.T, input_rows, shard, gw, piece
    )
    near = body_of(place, True, inner, edge, near_own, near_other, spread, gw)
    far_own = far[0]
    far_other = exchange(far[1], 0)
    far = body_of(after(place, near[0]), False, inner, edge, far_own, far_other, spread, gw)

    order = [2, 1, *range(3, n_bits)]
    left_after = [b for b in left if b != 2]
    got = exchange(sent, 2)
    kept, sent = fold_of(after(place, far[0], inside, outside), kept, got, left_after, order[1], piece)
    closing = after(place, sent)
    left_after.remove(order[1])
    got = exchange(sent, order[1])
    kept, sent = fold_of(place, kept, got, left_after, order[2], piece)
    splitting = after(place, sent)
    left_after.remove(order[2])

    near_first, near_kept, near_send, group_near_kept, group_near_send = close_of(
        closing, True, *near, near_own, near_other, inside, outside, spread, keep_in, send_in, piece
    )
    near_got = exchange(near_send, 0)
    group_near_got = exchange(group_near_send, 0)
    far_first, far_kept, far_send, group_far_kept, group_far_send = close_of(
        closing, False, *far, far_own, far_other, inside, outside, spread, keep_in, send_in, piece
    )
    far_got = exchange(far_send, 0)
    group_far_got = exchange(group_far_send, 0)

    one_kept, one_sent, two_kept, two_sent = split_of(
        place, near_kept, far_kept, near_got, far_got,
        (group_near_kept, group_far_kept), (group_near_got, group_far_got), piece,
    )
    kept, got = summed_up(place, kept, sent, order[2:], left_after, piece)
    third_wgrad = (kept + got.astype(F32)) * normalizer
    one = summed_up(place, one_kept, one_sent, z_first, [b for b in left if b != 2], piece)
    input_grad = result_of(place, near_first, far_first, first_weight, grad_copy)
    two = summed_up(after(place, input_grad), two_kept, two_sent, x_first, [b for b in left if b != 1], piece)
    first_wgrad, group_wgrad = last_of(place, normalizer, *one, *two, channels, TAPS * gw)
    return (input_grad.reshape(outer_grad.shape), third_wgrad, group_wgrad, first_wgrad)


def solution(mesh):
    tiles = P(("parts", "space"), None, None, None)
    rows = P(("parts", "space"), None)
    return jax.shard_map(
        per_device,
        mesh=mesh,
        in_specs=(tiles, tiles, tiles, tiles, P(), P(), P()),
        out_specs=(tiles, rows, rows, rows),
        check_vma=False,
    )
```

time: 279 us -> 84.6 us (0.30)
  waiting for transfers between devices: 194 us -> 26.3 us
  local copies, waits for them, and re-layouts: 33.1 us -> 0.05 us
  Pallas kernels: 0 us -> 32.2 us
  matrix products: 22.7 us -> 0 us
  starting transfers between devices: 10.4 us -> 24.3 us
  between operations: 14.2 us -> 0.88 us
  other arithmetic: 4.05 us -> 0.74 us
    reduce_scatter x2 -> x0, waiting for transfers between devices: 86.3 us -> none  [the longest x1 76.6 us: per_device(): lax.psum_scatter(lax.dot_general(left_cols, grad_rows, (((0,), (0,)), (()...]
    unnamed x4 -> x0, waiting for transfers between devices: 76.1 us -> none
    pallas_call x0 -> x18, Pallas kernels: none -> 32.2 us  [the longest x17 26.9 us: call(): pl.pallas_call(kernel, in_specs=specs, out_specs=[pl.BlockSpec(memory_spa...]
    dot_general x22 -> x0, matrix products: 22.7 us -> none  [the longest x1 4.48 us: per_device(): lax.dot_general(left_cols, grad_rows, (((0,), (0,)), ((), ())), preferred...]
    ppermute x6 -> x20, starting transfers between devices: 10.1 us -> 24.3 us  [the longest x19 23.5 us: exchange(): lax.ppermute(array, 'space', [(i, i ^ 1 << bit) for i in range(count)])]
    unnamed x44 -> x4, local copies, waits for them, and re-layouts: 12.1 us -> 0.01 us
    ppermute x6 -> x20, waiting for transfers between devices: 31.2 us -> 26.3 us  [the longest x19 26.3 us: exchange(): lax.ppermute(array, 'space', [(i, i ^ 1 << bit) for i in range(count)])]
    slice x3 -> x0, local copies, waits for them, and re-layouts: 4.28 us -> none  [the longest x1 2.36 us: group_backward(): padded[2 - tap_row:2 - tap_row + tile_rows, 2 - tap_col:2 - tap_col + til...]
  transfers between devices with their start and end apart: 9 -> 20, of which waited for: 8 -> 9; matrix products, arithmetic and copies ran while one was open for 12% -> 1% of each run, Pallas kernels for 0% -> 26%
where the time goes in v2:
time: 84.6 us; the launch traced here: 84.4 us
  Pallas kernels  32.2 us (38%)
  waiting for transfers between devices  26.3 us (31%)
  starting transfers between devices  24.3 us (29%)
  between operations  0.88 us (1%)
    pallas_call x17, Pallas kernels, call(): pl.pallas_call(kernel, in_specs=specs, out_specs=[pl.BlockSpec(memory_spa...  26.9 us
    ppermute x19, waiting for transfers between devices, exchange(): lax.ppermute(array, 'space', [(i, i ^ 1 << bit) for i in range(count)])  26.3 us
    ppermute x19, starting transfers between devices, exchange(): lax.ppermute(array, 'space', [(i, i ^ 1 << bit) for i in range(count)])  23.5 us
    pallas_call x1, Pallas kernels, result_of(): pl.pallas_call(result_kernel, in_specs=[pl.BlockSpec(memory_space=pltpu.S...  5.26 us
  transfers between devices with their start and end apart: 20, of which 9 were waited for; matrix products, arithmetic and copies ran while one was open for 1% of the time, Pallas kernels for 26%

profile of v2, /device:TPU:0, one launch (start us, length us, event | category | flops | bytes accessed | tf_op | source)
XLA Modules:
  0.0 84.4 jit_solution(16471121348412964199)
XLA Ops:
  0.6 2.0 %pack.1 = (bf16[4,128,256]{2,1,0:T(8,128)(2,1)S(1)}, bf16[4,128,256]{2,1,0:T(8,128)(2,1)S(1)}, bf16[2,4,128,256]{3,2,1,0:T(8,128)(2,1)S(1)}, bf16[16,1024]{1,0:T(8,128)(2,1)S(1)}) custom-call(s32[4]{0:T(128)S(1)} %shift-right-arithmetic_and_fusion.place_ref.refs_0_, bf16[1,8,256,256]{3,2,1,0:T(8,128)(2,1)} %second_ref.1, bf16[512,1024]{1,0:T(8,128)(2,1)} %bitcast.51, ...), custom_call_target="tpu_custom_call" | custom-call | tf_op jit(solution)/shard_map/pack/pallas_call | solution.py:45
  2.7 3.4 %third.1 = (f32[512,1024]{1,0:T(8,128)S(1)}, bf16[512,1024]{1,0:T(8,128)(2,1)S(1)}, bf16[512,1024]{1,0:T(8,128)(2,1)S(1)}, bf16[512,1024]{1,0:T(8,128)(2,1)S(1)}, bf16[1024,1024]{1,0:T(8,128)(2,1)S(1)}) custom-call(s32[4]{0:T(128)S(1)} %shift-right-arithmetic_and_fusion.place_ref.refs_0_, bf16[512,1024]{1,0:T(8,128)(2,1)} %bitcast.50, ...), custom_call_target="tpu_custom_call" | custom-call | tf_op jit(solution)/shard_map/third/pallas_call | solution.py:45
  6.7 2.6 %collective-permute-start.3 = (bf16[2,4,128,256]{3,2,1,0:T(8,128)(2,1)S(1)}, bf16[2,4,128,256]{3,2,1,0:T(8,128)(2,1)S(1)}, u32[]{:S(2)}, u32[]{:S(2)}) collective-permute-start(bf16[2,4,128,256]{3,2,1,0:T(8,128)(2,1)S(1)} %get-tuple-element.77), channel_id=1, source_target_pairs={{0,2},{1,3},{2,0},{3,1},{4,6},{5,7},{6,4},{7,5},{8,10},{9,11},{10,... | collective-permute-start | bytes 1572872 | tf_op jit(solution)/shard_map/ppermute | solution.py:18
  9.4 1.0 %collective-permute-done.edge_ref = bf16[16,1024]{1,0:T(8,128)(2,1)S(1)} collective-permute-done((bf16[16,1024]{1,0:T(8,128)(2,1)S(1)}, bf16[16,1024]{1,0:T(8,128)(2,1)S(1)}, u32[]{:S(2)}, u32[]{:S(2)}) %collective-permute-start) | collective-permute-done | bytes 32800 | tf_op jit(solution)/shard_map/ppermute | solution.py:18
  10.4 2.5 %inner.1 = (bf16[512,1024]{1,0:T(8,128)(2,1)S(1)}, bf16[16,1024]{1,0:T(8,128)(2,1)S(1)}, bf16[144,1024]{1,0:T(8,128)(2,1)S(1)}, bf16[144,1024]{1,0:T(8,128)(2,1)S(1)}) custom-call(s32[4]{0:T(128)S(1)} %shift-right-arithmetic_and_fusion.place_ref.refs_0_, bf16[512,1024]{1,0:T(8,128)(2,1)S(1)} %get-tuple-element.66.grad_ref, ...), custom_call_target="tpu_custom_call" | custom-call | tf_op jit(solution)/shard_map/inner/pallas_call | solution.py:45
  12.9 0.8 fold.7
  13.8 1.6 %collective-permute-start.7 = (bf16[2,128,1024]{2,1,0:T(8,128)(2,1)S(1)}, bf16[2,128,1024]{2,1,0:T(8,128)(2,1)S(1)}, u32[]{:S(2)}, u32[]{:S(2)}) collective-permute-start(bf16[2,128,1024]{2,1,0:T(8,128)(2,1)S(1)} %get-tuple-element.76), channel_id=1, source_target_pairs={{0,4},{1,5},{2,6},{3,7},{4,0},{5,1},{6,2},{7,3},{8,12},{9,13},{10,... | collective-permute-start | bytes 1572872 | tf_op jit(solution)/shard_map/ppermute | solution.py:18
  15.4 1.4 %collective-permute-start.5 = (bf16[144,1024]{1,0:T(8,128)(2,1)S(1)}, bf16[144,1024]{1,0:T(8,128)(2,1)S(1)}, u32[]{:S(2)}, u32[]{:S(2)}) collective-permute-start(bf16[144,1024]{1,0:T(8,128)(2,1)S(1)} %get-tuple-element.73), channel_id=1, source_target_pairs={{0,2},{1,3},{2,0},{3,1},{4,6},{5,7},{6,4},{7,5},{8,10},{9,11},{10,... | collective-permute-start | bytes 884744 | tf_op jit(solution)/shard_map/ppermute | solution.py:18
  16.8 0.8 %collective-permute-start.6 = (bf16[144,1024]{1,0:T(8,128)(2,1)S(1)}, bf16[144,1024]{1,0:T(8,128)(2,1)S(1)}, u32[]{:S(2)}, u32[]{:S(2)}) collective-permute-start(bf16[144,1024]{1,0:T(8,128)(2,1)S(1)} %get-tuple-element.83), channel_id=1, source_target_pairs={{2,4},{4,2},{3,5},{5,3},{6,8},{8,6},{7,9},{9,7},{10,12},{12,10},{1... | collective-permute-start | bytes 884744 | tf_op jit(solution)/shard_map/ppermute | solution.py:28
  17.7 4.3 %collective-permute-done.3 = bf16[2,4,128,256]{3,2,1,0:T(8,128)(2,1)S(1)} collective-permute-done((bf16[2,4,128,256]{3,2,1,0:T(8,128)(2,1)S(1)}, bf16[2,4,128,256]{3,2,1,0:T(8,128)(2,1)S(1)}, u32[]{:S(2)}, u32[]{:S(2)}) %collective-permute-start.3) | collective-permute-done | bytes 524320 | tf_op jit(solution)/shard_map/ppermute | solution.py:18
  22.1 2.0 %ready.1 = (bf16[4,3,768,256]{3,2,1,0:T(8,128)(2,1)S(1)}, bf16[512,512]{1,0:T(8,128)(2,1)S(1)}, bf16[512,512]{1,0:T(8,128)(2,1)S(1)}) custom-call(s32[4]{0:T(128)S(1)} %shift-right-arithmetic_and_fusion.place_ref.refs_0_, bf16[288,1024]{1,0:T(8,128)(2,1)S(1)} %bitcast.35, bf16[512,1024]{1,0:T(8,128)(2,1)S(1)} %bitcast.30), custom_call_target="tpu_custom_call" | custom-call | tf_op jit(solution)/shard_map/ready/pallas_call | solution.py:45
  24.2 3.0 %body_near.1 = (f32[2,512,256]{2,1,0:T(8,128)S(1)}, f32[2,288,256]{2,1,0:T(8,128)S(1)}) custom-call(s32[4]{0:T(128)S(1)} %shift-right-arithmetic_and_fusion.place_ref.refs_0_, bf16[512,1024]{1,0:T(8,128)(2,1)S(1)} %get-tuple-element.69.refs_1_, bf16[16,1024]{1,0:T(8,128)(2,1)S(1)} %get-tuple-element.70.refs_2_, ...), custom_call_target="tpu_custom_call" | custom-call | tf_op jit(solution)/shard_map/body_near/pallas_call | solution.py:45
  27.2 3.0 %body_far.1 = (f32[2,512,256]{2,1,0:T(8,128)S(1)}, f32[2,288,256]{2,1,0:T(8,128)S(1)}) custom-call(s32[4]{0:T(128)S(1)} %shift-right-arithmetic_and_fusion.place_ref.refs_0_, bf16[512,1024]{1,0:T(8,128)(2,1)S(1)} %get-tuple-element.69.refs_1_, bf16[16,1024]{1,0:T(8,128)(2,1)S(1)} %get-tuple-element.70.refs_2_, ...), custom_call_target="tpu_custom_call" | custom-call | tf_op jit(solution)/shard_map/body_far/pallas_call | solution.py:45
  30.2 3.5 %collective-permute-done.5.refs_5_ = bf16[144,1024]{1,0:T(8,128)(2,1)S(1)} collective-permute-done((bf16[144,1024]{1,0:T(8,128)(2,1)S(1)}, bf16[144,1024]{1,0:T(8,128)(2,1)S(1)}, u32[]{:S(2)}, u32[]{:S(2)}) %collective-permute-start.5) | collective-permute-done | bytes 294944 | tf_op jit(solution)/shard_map/ppermute | solution.py:18
  33.7 0.7 fold.8
  34.4 2.0 %close_far.1 = (bf16[512,512]{1,0:T(8,128)(2,1)S(1)}, f32[512,512]{1,0:T(8,128)S(1)}, bf16[512,512]{1,0:T(8,128)(2,1)S(1)}, f32[256,288]{1,0:T(8,128)S(1)}, bf16[256,288]{1,0:T(8,128)(2,1)S(1)}) custom-call(s32[4]{0:T(128)S(1)} %shift-right-arithmetic_and_fusion.place_ref.refs_0_, f32[2,512,256]{2,1,0:T(8,128)S(1)} %get-tuple-element.82.refs_1_, ...), custom_call_target="tpu_custom_call" | custom-call | tf_op jit(solution)/shard_map/close_far/pallas_call | solution.py:45
  36.5 2.0 %close_near.1 = (bf16[512,512]{1,0:T(8,128)(2,1)S(1)}, f32[512,512]{1,0:T(8,128)S(1)}, bf16[512,512]{1,0:T(8,128)(2,1)S(1)}, f32[256,288]{1,0:T(8,128)S(1)}, bf16[256,288]{1,0:T(8,128)(2,1)S(1)}) custom-call(s32[4]{0:T(128)S(1)} %shift-right-arithmetic_and_fusion.place_ref.refs_0_, f32[2,512,256]{2,1,0:T(8,128)S(1)} %get-tuple-element.80.refs_1_, ...), custom_call_target="tpu_custom_call" | custom-call | tf_op jit(solution)/shard_map/close_near/pallas_call | solution.py:45
  39.6 1.3 %collective-permute-done.13.refs_8_ = bf16[256,288]{1,0:T(8,128)(2,1)S(1)} collective-permute-done((bf16[256,288]{1,0:T(8,128)(2,1)S(1)}, bf16[256,288]{1,0:T(8,128)(2,1)S(1)}, u32[]{:S(2)}, u32[]{:S(2)}) %collective-permute-start.13) | collective-permute-done | bytes 147488 | tf_op jit(solution)/shard_map/ppermute | solution.py:18
  41.2 1.1 %split.1 = (f32[2,128,544]{2,1,0:T(8,128)S(1)}, bf16[2,128,544]{2,1,0:T(8,128)(2,1)S(1)}, f32[2,128,768]{2,1,0:T(8,128)S(1)}, bf16[2,128,768]{2,1,0:T(8,128)(2,1)S(1)}) custom-call(s32[4]{0:T(128)S(1)} %shift-right-arithmetic_and_fusion.place_ref.refs_0_, f32[512,512]{1,0:T(8,128)S(1)} %get-tuple-element.97.refs_1_, ...), custom_call_target="tpu_custom_call" | custom-call | tf_op jit(solution)/shard_map/split/pallas_call | solution.py:45
  42.3 2.5 %collective-permute-start.17 = (bf16[2,128,768]{2,1,0:T(8,128)(2,1)S(1)}, bf16[2,128,768]{2,1,0:T(8,128)(2,1)S(1)}, u32[]{:S(2)}, u32[]{:S(2)}) collective-permute-start(bf16[2,128,768]{2,1,0:T(8,128)(2,1)S(1)} %get-tuple-element.113), channel_id=1, source_target_pairs={{0,2},{1,3},{2,0},{3,1},{4,6},{5,7},{6,4},{7,5},{8,10},{9,11},{10,... | collective-permute-start | bytes 1179656 | tf_op jit(solution)/shard_map/ppermute | solution.py:18
  44.8 4.2 %collective-permute-start.14 = (bf16[2,128,544]{2,1,0:T(8,128)(2,1)S(1)}, bf16[2,128,544]{2,1,0:T(8,128)(2,1)S(1)}, u32[]{:S(2)}, u32[]{:S(2)}) collective-permute-start(bf16[2,128,544]{2,1,0:T(8,128)(2,1)S(1)} %get-tuple-element.106), channel_id=1, source_target_pairs={{0,4},{1,5},{2,6},{3,7},{4,0},{5,1},{6,2},{7,3},{8,12},{9,13},{10,... | collective-permute-start | bytes 835592 | tf_op jit(solution)/shard_map/ppermute | solution.py:18
  49.1 5.3 %result.1 = bf16[512,1024]{1,0:T(8,128)(2,1)} custom-call(s32[4]{0:T(128)S(1)} %shift-right-arithmetic_and_fusion.place_ref.refs_0_, bf16[512,512]{1,0:T(8,128)(2,1)S(1)} %get-tuple-element.91.near_ref, bf16[512,512]{1,0:T(8,128)(2,1)S(1)} %get-tuple-element.93.far_ref, bf16[512,1024]{1,0:T(8,128)(2,1)S(1)} %get-tuple-element.66.grad_ref, ...), custom_call_target="tpu_custom_call" | custom-call | tf_op jit(solution)/shard_map/result/pallas_call | solution.py:548
  54.8 0.6 fold.12
  55.4 4.2 %collective-permute-start.18 = (bf16[2,64,768]{2,1,0:T(8,128)(2,1)S(1)}, bf16[2,64,768]{2,1,0:T(8,128)(2,1)S(1)}, u32[]{:S(2)}, u32[]{:S(2)}) collective-permute-start(bf16[2,64,768]{2,1,0:T(8,128)(2,1)S(1)} %get-tuple-element.115), channel_id=1, source_target_pairs={{0,4},{1,5},{2,6},{3,7},{4,0},{5,1},{6,2},{7,3},{8,12},{9,13},{10,... | collective-permute-start | bytes 589832 | tf_op jit(solution)/shard_map/ppermute | solution.py:18
  60.3 0.9 %collective-permute-start.15 = (bf16[1,128,544]{2,1,0:T(8,128)(2,1)S(1)}, bf16[1,128,544]{2,1,0:T(8,128)(2,1)S(1)}, u32[]{:S(2)}, u32[]{:S(2)}) collective-permute-start(bf16[1,128,544]{2,1,0:T(8,128)(2,1)S(1)} %get-tuple-element.108), channel_id=1, source_target_pairs={{0,8},{1,9},{2,10},{3,11},{4,12},{5,13},{6,14},{7,15},{8,0},{9,1},... | collective-permute-start | bytes 417800 | tf_op jit(solution)/shard_map/ppermute | solution.py:18
  61.7 2.2 %collective-permute-start.9 = (bf16[1,64,1024]{2,1,0:T(8,128)(2,1)S(1)}, bf16[1,64,1024]{2,1,0:T(8,128)(2,1)S(1)}, u32[]{:S(2)}, u32[]{:S(2)}) collective-permute-start(bf16[1,64,1024]{2,1,0:T(8,128)(2,1)S(1)} %get-tuple-element.96), channel_id=1, source_target_pairs={{0,8},{1,9},{2,10},{3,11},{4,12},{5,13},{6,14},{7,15},{8,0},{9,1},... | collective-permute-start | bytes 393224 | tf_op jit(solution)/shard_map/ppermute | solution.py:18
  63.9 10.6 %collective-permute-done.15 = bf16[1,128,544]{2,1,0:T(8,128)(2,1)S(1)} collective-permute-done((bf16[1,128,544]{2,1,0:T(8,128)(2,1)S(1)}, bf16[1,128,544]{2,1,0:T(8,128)(2,1)S(1)}, u32[]{:S(2)}, u32[]{:S(2)}) %collective-permute-start.15) | collective-permute-done | bytes 139296 | tf_op jit(solution)/shard_map/ppermute | solution.py:18
  75.1 1.8 %collective-permute-start.16 = (bf16[1,64,544]{2,1,0:T(8,128)(2,1)S(1)}, bf16[1,64,544]{2,1,0:T(8,128)(2,1)S(1)}, u32[]{:S(2)}, u32[]{:S(2)}) collective-permute-start(bf16[1,64,544]{2,1,0:T(8,128)(2,1)S(1)} %get-tuple-element.110), channel_id=1, source_target_pairs={{0,2},{1,3},{2,0},{3,1},{4,6},{5,7},{6,4},{7,5},{8,10},{9,11},{10,... | collective-permute-start | bytes 208904 | tf_op jit(solution)/shard_map/ppermute | solution.py:18
  77.6 0.7 multiply_bitcast_fusion
  78.3 1.3 %collective-permute-done.16 = bf16[1,64,544]{2,1,0:T(8,128)(2,1)S(1)} collective-permute-done((bf16[1,64,544]{2,1,0:T(8,128)(2,1)S(1)}, bf16[1,64,544]{2,1,0:T(8,128)(2,1)S(1)}, u32[]{:S(2)}, u32[]{:S(2)}) %collective-permute-start.16) | collective-permute-done | bytes 69664 | tf_op jit(solution)/shard_map/ppermute | solution.py:18
  79.6 3.4 %collective-permute-done.19 = bf16[1,64,768]{2,1,0:T(8,128)(2,1)S(1)} collective-permute-done((bf16[1,64,768]{2,1,0:T(8,128)(2,1)S(1)}, bf16[1,64,768]{2,1,0:T(8,128)(2,1)S(1)}, u32[]{:S(2)}, u32[]{:S(2)}) %collective-permute-start.19) | collective-permute-done | bytes 98336 | tf_op jit(solution)/shard_map/ppermute | solution.py:18
  83.1 1.3 %last.1 = (f32[64,1024]{1,0:T(8,128)}, f32[64,288]{1,0:T(8,128)}) custom-call(s32[4]{0:T(128)S(1)} %shift-right-arithmetic_and_fusion.place_ref.refs_0_, f32[64,544]{1,0:T(8,128)S(1)} %bitcast.45, bf16[64,544]{1,0:T(8,128)(2,1)S(1)} %bitcast.48, f32[64,768]{1,0:T(8,128)S(1)} %bitcast.43, bf16[64,768]{1,0:T(8,128)(2,1)S(1)} %bitcast.47), custom_call_target="tpu_custom_call" | custom-call | tf_op jit(solution)/shard_map/last/pallas_call | solution.py:45
  (33 shorter events, 5.2 us)
Async XLA Ops:
  6.1 6.8 %collective-permute-start.2 = (bf16[512,1024]{1,0:T(8,128)(2,1)S(1)}, bf16[512,1024]{1,0:T(8,128)(2,1)S(1)}, u32[]{:S(2)}, u32[]{:S(2)}) collective-permute-start(bf16[512,1024]{1,0:T(8,128)(2,1)S(1)} %get-tuple-element.64), channel_id=1, source_target_pairs={{0,1},{1,0},{2,3},{3,2},{4,5},{5,4},{6,7},{7,6},{8,9},{9,8},{10,11... | collective-permute-start | bytes 3145736 | tf_op jit(solution)/shard_map/ppermute | solution.py:18
  6.7 15.3 %collective-permute-start.3 = (bf16[2,4,128,256]{3,2,1,0:T(8,128)(2,1)S(1)}, bf16[2,4,128,256]{3,2,1,0:T(8,128)(2,1)S(1)}, u32[]{:S(2)}, u32[]{:S(2)}) collective-permute-start(bf16[2,4,128,256]{3,2,1,0:T(8,128)(2,1)S(1)} %get-tuple-element.77), channel_id=1, source_target_pairs={{0,2},{1,3},{2,0},{3,1},{4,6},{5,7},{6,4},{7,5},{8,10},{9,11},{10,... | collective-permute-start | bytes 1572872 | tf_op jit(solution)/shard_map/ppermute | solution.py:18
  9.2 1.2 %collective-permute-start = (bf16[16,1024]{1,0:T(8,128)(2,1)S(1)}, bf16[16,1024]{1,0:T(8,128)(2,1)S(1)}, u32[]{:S(2)}, u32[]{:S(2)}) collective-permute-start(bf16[16,1024]{1,0:T(8,128)(2,1)S(1)} %get-tuple-element.62), channel_id=1, source_target_pairs={{0,1},{1,0},{2,3},{3,2},{4,5},{5,4},{6,7},{7,6},{8,9},{9,8},{10,11... | collective-permute-start | bytes 98312 | tf_op jit(solution)/shard_map/ppermute | solution.py:18
  12.9 9.2 %copy-start = (bf16[1,4,128,1024]{3,2,1,0:T(8,128)(2,1)S(1)}, bf16[1,4,128,1024]{3,2,1,0:T(8,128)(2,1)}, u32[]{:S(2)}) copy-start(bf16[1,4,128,1024]{3,2,1,0:T(8,128)(2,1)} %param.8) | copy-start | bytes 3145732
  12.9 9.2 %copy-start.1 = (bf16[1024,288]{0,1:T(8,128)(2,1)S(1)}, bf16[1024,288]{0,1:T(8,128)(2,1)}, u32[]{:S(2)}) copy-start(bf16[1024,288]{0,1:T(8,128)(2,1)} %param.12) | copy-start | bytes 1769476
  13.8 19.9 %collective-permute-start.7 = (bf16[2,128,1024]{2,1,0:T(8,128)(2,1)S(1)}, bf16[2,128,1024]{2,1,0:T(8,128)(2,1)S(1)}, u32[]{:S(2)}, u32[]{:S(2)}) collective-permute-start(bf16[2,128,1024]{2,1,0:T(8,128)(2,1)S(1)} %get-tuple-element.76), channel_id=1, source_target_pairs={{0,4},{1,5},{2,6},{3,7},{4,0},{5,1},{6,2},{7,3},{8,12},{9,13},{10,... | collective-permute-start | bytes 1572872 | tf_op jit(solution)/shard_map/ppermute | solution.py:18
  15.4 8.8 %collective-permute-start.1 = (bf16[4,128,256]{2,1,0:T(8,128)(2,1)S(1)}, bf16[4,128,256]{2,1,0:T(8,128)(2,1)S(1)}, u32[]{:S(2)}, u32[]{:S(2)}) collective-permute-start(bf16[4,128,256]{2,1,0:T(8,128)(2,1)S(1)} %get-tuple-element.72), channel_id=1, source_target_pairs={{0,1},{1,0},{2,3},{3,2},{4,5},{5,4},{6,7},{7,6},{8,9},{9,8},{10,11... | collective-permute-start | bytes 786440 | tf_op jit(solution)/shard_map/ppermute | solution.py:18
  15.4 18.3 %collective-permute-start.5 = (bf16[144,1024]{1,0:T(8,128)(2,1)S(1)}, bf16[144,1024]{1,0:T(8,128)(2,1)S(1)}, u32[]{:S(2)}, u32[]{:S(2)}) collective-permute-start(bf16[144,1024]{1,0:T(8,128)(2,1)S(1)} %get-tuple-element.73), channel_id=1, source_target_pairs={{0,2},{1,3},{2,0},{3,1},{4,6},{5,7},{6,4},{7,5},{8,10},{9,11},{10,... | collective-permute-start | bytes 884744 | tf_op jit(solution)/shard_map/ppermute | solution.py:18
  16.8 13.3 %collective-permute-start.6 = (bf16[144,1024]{1,0:T(8,128)(2,1)S(1)}, bf16[144,1024]{1,0:T(8,128)(2,1)S(1)}, u32[]{:S(2)}, u32[]{:S(2)}) collective-permute-start(bf16[144,1024]{1,0:T(8,128)(2,1)S(1)} %get-tuple-element.83), channel_id=1, source_target_pairs={{2,4},{4,2},{3,5},{5,3},{6,8},{8,6},{7,9},{9,7},{10,12},{12,10},{1... | collective-permute-start | bytes 884744 | tf_op jit(solution)/shard_map/ppermute | solution.py:28
  22.0 5.1 %collective-permute-start.4 = (bf16[4,128,256]{2,1,0:T(8,128)(2,1)S(1)}, bf16[4,128,256]{2,1,0:T(8,128)(2,1)S(1)}, u32[]{:S(2)}, u32[]{:S(2)}) collective-permute-start(bf16[4,128,256]{2,1,0:T(8,128)(2,1)S(1)} %get-tuple-element.120), channel_id=1, source_target_pairs={{0,1},{1,0},{2,3},{3,2},{4,5},{5,4},{6,7},{7,6},{8,9},{9,8},{10,11... | collective-permute-start | bytes 786440 | tf_op jit(solution)/shard_map/ppermute | solution.py:18
  36.4 4.8 %collective-permute-start.11 = (bf16[512,512]{1,0:T(8,128)(2,1)S(1)}, bf16[512,512]{1,0:T(8,128)(2,1)S(1)}, u32[]{:S(2)}, u32[]{:S(2)}) collective-permute-start(bf16[512,512]{1,0:T(8,128)(2,1)S(1)} %get-tuple-element.100), channel_id=1, source_target_pairs={{0,1},{1,0},{2,3},{3,2},{4,5},{5,4},{6,7},{7,6},{8,9},{9,8},{10,11... | collective-permute-start | bytes 1572872 | tf_op jit(solution)/shard_map/ppermute | solution.py:18
  38.5 2.7 %collective-permute-start.10 = (bf16[512,512]{1,0:T(8,128)(2,1)S(1)}, bf16[512,512]{1,0:T(8,128)(2,1)S(1)}, u32[]{:S(2)}, u32[]{:S(2)}) collective-permute-start(bf16[512,512]{1,0:T(8,128)(2,1)S(1)} %get-tuple-element.99), channel_id=1, source_target_pairs={{0,1},{1,0},{2,3},{3,2},{4,5},{5,4},{6,7},{7,6},{8,9},{9,8},{10,11... | collective-permute-start | bytes 1572872 | tf_op jit(solution)/shard_map/ppermute | solution.py:18
  39.1 1.8 %collective-permute-start.13 = (bf16[256,288]{1,0:T(8,128)(2,1)S(1)}, bf16[256,288]{1,0:T(8,128)(2,1)S(1)}, u32[]{:S(2)}, u32[]{:S(2)}) collective-permute-start(bf16[256,288]{1,0:T(8,128)(2,1)S(1)} %get-tuple-element.104), channel_id=1, source_target_pairs={{0,1},{1,0},{2,3},{3,2},{4,5},{5,4},{6,7},{7,6},{8,9},{9,8},{10,11... | collective-permute-start | bytes 442376 | tf_op jit(solution)/shard_map/ppermute | solution.py:18
  39.1 2.0 %collective-permute-start.12 = (bf16[256,288]{1,0:T(8,128)(2,1)S(1)}, bf16[256,288]{1,0:T(8,128)(2,1)S(1)}, u32[]{:S(2)}, u32[]{:S(2)}) collective-permute-start(bf16[256,288]{1,0:T(8,128)(2,1)S(1)} %get-tuple-element.103), channel_id=1, source_target_pairs={{0,1},{1,0},{2,3},{3,2},{4,5},{5,4},{6,7},{7,6},{8,9},{9,8},{10,11... | collective-permute-start | bytes 442376 | tf_op jit(solution)/shard_map/ppermute | solution.py:18
  42.3 12.5 %collective-permute-start.17 = (bf16[2,128,768]{2,1,0:T(8,128)(2,1)S(1)}, bf16[2,128,768]{2,1,0:T(8,128)(2,1)S(1)}, u32[]{:S(2)}, u32[]{:S(2)}) collective-permute-start(bf16[2,128,768]{2,1,0:T(8,128)(2,1)S(1)} %get-tuple-element.113), channel_id=1, source_target_pairs={{0,2},{1,3},{2,0},{3,1},{4,6},{5,7},{6,4},{7,5},{8,10},{9,11},{10,... | collective-permute-start | bytes 1179656 | tf_op jit(solution)/shard_map/ppermute | solution.py:18
  44.8 14.8 %collective-permute-start.14 = (bf16[2,128,544]{2,1,0:T(8,128)(2,1)S(1)}, bf16[2,128,544]{2,1,0:T(8,128)(2,1)S(1)}, u32[]{:S(2)}, u32[]{:S(2)}) collective-permute-start(bf16[2,128,544]{2,1,0:T(8,128)(2,1)S(1)} %get-tuple-element.106), channel_id=1, source_target_pairs={{0,4},{1,5},{2,6},{3,7},{4,0},{5,1},{6,2},{7,3},{8,12},{9,13},{10,... | collective-permute-start | bytes 835592 | tf_op jit(solution)/shard_map/ppermute | solution.py:18
  49.0 12.1 %collective-permute-start.8 = (bf16[2,64,1024]{2,1,0:T(8,128)(2,1)S(1)}, bf16[2,64,1024]{2,1,0:T(8,128)(2,1)S(1)}, u32[]{:S(2)}, u32[]{:S(2)}) collective-permute-start(bf16[2,64,1024]{2,1,0:T(8,128)(2,1)S(1)} %get-tuple-element.86), channel_id=1, source_target_pairs={{0,2},{1,3},{2,0},{3,1},{4,6},{5,7},{6,4},{7,5},{8,10},{9,11},{10,... | collective-permute-start | bytes 786440 | tf_op jit(solution)/shard_map/ppermute | solution.py:18
  55.4 21.5 %collective-permute-start.18 = (bf16[2,64,768]{2,1,0:T(8,128)(2,1)S(1)}, bf16[2,64,768]{2,1,0:T(8,128)(2,1)S(1)}, u32[]{:S(2)}, u32[]{:S(2)}) collective-permute-start(bf16[2,64,768]{2,1,0:T(8,128)(2,1)S(1)} %get-tuple-element.115), channel_id=1, source_target_pairs={{0,4},{1,5},{2,6},{3,7},{4,0},{5,1},{6,2},{7,3},{8,12},{9,13},{10,... | collective-permute-start | bytes 589832 | tf_op jit(solution)/shard_map/ppermute | solution.py:18
  60.3 14.3 %collective-permute-start.15 = (bf16[1,128,544]{2,1,0:T(8,128)(2,1)S(1)}, bf16[1,128,544]{2,1,0:T(8,128)(2,1)S(1)}, u32[]{:S(2)}, u32[]{:S(2)}) collective-permute-start(bf16[1,128,544]{2,1,0:T(8,128)(2,1)S(1)} %get-tuple-element.108), channel_id=1, source_target_pairs={{0,8},{1,9},{2,10},{3,11},{4,12},{5,13},{6,14},{7,15},{8,0},{9,1},... | collective-permute-start | bytes 417800 | tf_op jit(solution)/shard_map/ppermute | solution.py:18
  61.7 15.8 %collective-permute-start.9 = (bf16[1,64,1024]{2,1,0:T(8,128)(2,1)S(1)}, bf16[1,64,1024]{2,1,0:T(8,128)(2,1)S(1)}, u32[]{:S(2)}, u32[]{:S(2)}) collective-permute-start(bf16[1,64,1024]{2,1,0:T(8,128)(2,1)S(1)} %get-tuple-element.96), channel_id=1, source_target_pairs={{0,8},{1,9},{2,10},{3,11},{4,12},{5,13},{6,14},{7,15},{8,0},{9,1},... | collective-permute-start | bytes 393224 | tf_op jit(solution)/shard_map/ppermute | solution.py:18
  75.1 4.5 %collective-permute-start.16 = (bf16[1,64,544]{2,1,0:T(8,128)(2,1)S(1)}, bf16[1,64,544]{2,1,0:T(8,128)(2,1)S(1)}, u32[]{:S(2)}, u32[]{:S(2)}) collective-permute-start(bf16[1,64,544]{2,1,0:T(8,128)(2,1)S(1)} %get-tuple-element.110), channel_id=1, source_target_pairs={{0,2},{1,3},{2,0},{3,1},{4,6},{5,7},{6,4},{7,5},{8,10},{9,11},{10,... | collective-permute-start | bytes 208904 | tf_op jit(solution)/shard_map/ppermute | solution.py:18
  77.5 5.6 %collective-permute-start.19 = (bf16[1,64,768]{2,1,0:T(8,128)(2,1)S(1)}, bf16[1,64,768]{2,1,0:T(8,128)(2,1)S(1)}, u32[]{:S(2)}, u32[]{:S(2)}) collective-permute-start(bf16[1,64,768]{2,1,0:T(8,128)(2,1)S(1)} %get-tuple-element.117), channel_id=1, source_target_pairs={{0,8},{1,9},{2,10},{3,11},{4,12},{5,13},{6,14},{7,15},{8,0},{9,1},... | collective-permute-start | bytes 294920 | tf_op jit(solution)/shard_map/ppermute | solution.py:18

commit v3 on v2

--- a/solution.py
+++ b/solution.py
@@ -29,7 +29,7 @@
 
 
 def after(value, *others):
-    return lax.optimization_barrier((value, *others))[0]
+    return value if not others else lax.optimization_barrier((value, *others))[0]
 
 
 def call(kernel, name, place, operands, outs, scratch=(), megabytes=12, pinned=True):
@@ -61,58 +61,6 @@
 def halves(value, bit):
     low, high = value[:, 0], value[:, 1]
     return jnp.where(bit == 0, low, high), jnp.where(bit == 0, high, low)
-
-
-def pack_kernel(
-    place_ref, second_ref, grad_ref, mask_ref,
-    near_own_ref, near_core_ref, far_ref, edge_ref, grads_ref, masks_ref, sems,
-):
-    rows, width, _ = near_own_ref.shape
-    core, half = place_ref[0], place_ref[1]
-    edge_at = (1 - core) * (width - 16)
-    copies = []
-    for row in range(ROWS):
-        there = pl.ds(pl.multiple_of(row * width + edge_at, 16), 16)
-        copies.append((grad_ref.at[there], grads_ref.at[row]))
-        copies.append((mask_ref.at[there], masks_ref.at[row]))
-    for target, row_at, column_at in (
-        (far_ref.at[0], 1 - half, core),
-        (far_ref.at[1], 1 - half, 1 - core),
-        (near_core_ref, half, 1 - core),
-        (near_own_ref, half, core),
-    ):
-        source = second_ref.at[0, pl.ds(row_at * rows, rows), pl.ds(column_at * width, width)]
-        copies.append((source, target))
-    copies = [pltpu.make_async_copy(*pair, sems.at[at]) for at, pair in enumerate(copies)]
-    for copy in copies:
-        copy.start()
-    for copy in copies:
-        copy.wait()
-    lines = []
-    for buffer in (grads_ref, masks_ref):
-        for row in range(ROWS):
-            value = buffer[row].astype(F32)
-            lines.append(jnp.where(core == 0, value[15:16], value[0:1]))
-    lines += [jnp.zeros_like(lines[0])] * (16 - 2 * ROWS)
-    edge_ref[...] = jnp.concatenate(lines).astype(BF)
-
-
-def pack_of(place, second_input, grad_rows, third_rows):
-    _, rows, columns, shard = second_input.shape
-    channels = grad_rows.shape[1]
-    out = (rows // 2, columns // 2, shard)
-    return call(
-        pack_kernel,
-        "pack",
-        place,
-        [(second_input,), (grad_rows,), (third_rows,)],
-        [(out, BF), (out, BF), ((2, *out), BF), ((16, channels), BF)],
-        [
-            pltpu.VMEM((ROWS, 16, channels), BF),
-            pltpu.VMEM((ROWS, 16, channels), BF),
-            pltpu.SemaphoreType.DMA((4 + 2 * ROWS,)),
-        ],
-    )
 
 
 def inner_kernel(
@@ -158,16 +106,24 @@
     )
 
 
-def third_kernel(
-    piece, place_ref, left_hbm, right_hbm, weight_hbm,
-    keep_ref, send_ref, left_ref, right_ref, weight_ref, sems,
+def front_kernel(
+    piece, place_ref, left_hbm, right_hbm, weight_hbm, second_hbm,
+    keep_ref, send_ref, left_ref, right_ref, weight_ref,
+    near_own_ref, near_core_ref, far_own_ref, far_core_ref, edge_ref, sems,
 ):
-    copies = [
-        pltpu.make_async_copy(*pair, sems.at[at])
-        for at, pair in enumerate(
-            ((left_hbm, left_ref), (right_hbm, right_ref), (weight_hbm, weight_ref))
-        )
-    ]
+    rows, width, _ = near_own_ref.shape
+    core, half = place_ref[0], place_ref[1]
+    copies = [(left_hbm, left_ref), (right_hbm, right_ref)]
+    for target, row_at, column_at in (
+        (far_own_ref, 1 - half, core),
+        (far_core_ref, 1 - half, 1 - core),
+        (near_core_ref, half, 1 - core),
+        (near_own_ref, half, core),
+    ):
+        source = second_hbm.at[0, pl.ds(row_at * rows, rows), pl.ds(column_at * width, width)]
+        copies.append((source, target))
+    copies.append((weight_hbm, weight_ref))
+    copies = [pltpu.make_async_copy(*pair, sems.at[at]) for at, pair in enumerate(copies)]
     for copy in copies:
         copy.start()
     copies[0].wait()
@@ -182,29 +138,42 @@
             preferred_element_type=F32,
         )
         columns = term.shape[1]
-        keep, send = halves(term.reshape(step // (2 * piece), 2, piece, columns), place_ref[0])
+        keep, send = halves(term.reshape(step // (2 * piece), 2, piece, columns), core)
         here = slice(part * step // 2, (part + 1) * step // 2)
         keep_ref[here, :] = keep.reshape(step // 2, columns)
         send_ref[here, :] = send.reshape(step // 2, columns).astype(BF)
-    copies[2].wait()
-
-
-def third_of(place, third_rows, grad_rows, third_weight, piece):
+    lines = []
+    for value_ref in (right_ref, left_ref):
+        for row in range(ROWS):
+            first = value_ref[row * width : row * width + 16, :].astype(F32)[0:1]
+            last = value_ref[(row + 1) * width - 16 : (row + 1) * width, :].astype(F32)[15:16]
+            lines.append(jnp.where(core == 0, last, first))
+    lines += [jnp.zeros_like(lines[0])] * (16 - 2 * ROWS)
+    edge_ref[...] = jnp.concatenate(lines).astype(BF)
+    for copy in copies[2:]:
+        copy.wait()
+
+
+def front_of(place, third_rows, grad_rows, third_weight, second_input, piece):
     positions, channels = grad_rows.shape
+    _, rows, columns, shard = second_input.shape
     wide = ((positions, channels), BF)
-    return call(
-        lambda *refs: third_kernel(piece, *refs),
-        "third",
-        place,
-        [(third_rows,), (grad_rows,), (third_weight,)],
+    quarter = ((rows // 2, columns // 2, shard), BF)
+    return call(
+        lambda *refs: front_kernel(piece, *refs),
+        "front",
+        place,
+        [(third_rows,), (grad_rows,), (third_weight,), (second_input,)],
         [
             ((channels // 2, channels), F32),
             ((channels // 2, channels), BF),
             wide,
             wide,
             ((channels, channels), BF),
+            *[quarter] * 4,
+            ((16, channels), BF),
         ],
-        [pltpu.SemaphoreType.DMA((3,))],
+        [pltpu.SemaphoreType.DMA((7,))],
     )
 
 
@@ -230,14 +199,18 @@
     )
 
 
-def summed_up(place, keep, send, order, left, piece):
+def summed_up(place, keep, send, order, left, piece, gates={}):
     received = exchange(send, order[0])
-    for bit in order[1:]:
-        keep, send = fold_of(place, keep, received, left, bit, piece)
+    sent = []
+    for step, bit in enumerate(order[1:]):
+        keep, send = fold_of(
+            after(place, *gates.get(step, ())), keep, received, left, bit, piece
+        )
         left = [b for b in left if b != bit]
+        sent.append(send)
         received = exchange(send, bit)
     columns = keep.shape[-1]
-    return keep.reshape(piece, columns), received.reshape(piece, columns)
+    return keep.reshape(piece, columns), received.reshape(piece, columns), sent
 
 
 def ready_kernel(gw, piece, place_ref, weight_ref, input_ref, spread_ref, keep_ref, send_ref):
@@ -431,75 +404,80 @@
     )
 
 
+def both_halves(half, near_ref, far_ref, near_got_ref, far_got_ref, here):
+    near = near_ref[here, :] + near_got_ref[here, :].astype(F32)
+    far = far_ref[here, :] + far_got_ref[here, :].astype(F32)
+    return jnp.where(half == 0, near, far), jnp.where(half == 0, far, near)
+
+
 def split_kernel(
-    piece,
-    place_ref,
-    near_ref,
-    far_ref,
-    near_got_ref,
-    far_got_ref,
-    group_near_ref,
-    group_far_ref,
-    group_near_got_ref,
-    group_far_got_ref,
-    one_keep_ref,
-    one_send_ref,
-    two_keep_ref,
-    two_send_ref,
+    cut, piece, place_ref, near_ref, far_ref, near_got_ref, far_got_ref, keep_ref, send_ref
 ):
+    size = 4 * piece
+    for at in range(keep_ref.shape[0]):
+        here = slice(at * size, (at + 1) * size)
+        low, high = both_halves(
+            place_ref[1], near_ref, far_ref, near_got_ref, far_got_ref, here
+        )
+        edge = low.shape[1] - cut
+        for columns, value in ((slice(0, edge), low[:, cut:]), (slice(edge, None), high)):
+            keep, send = halves(value.reshape(2, 2, piece, value.shape[1]), place_ref[1])
+            rows = (size // 2, value.shape[1])
+            keep_ref[at, :, columns] = keep.reshape(rows)
+            send_ref[at, :, columns] = send.reshape(rows).astype(BF)
+
+
+def split_group_kernel(cut, piece, place_ref, *refs):
+    *wide, near_ref, far_ref, near_got_ref, far_got_ref, keep_ref, send_ref = refs
     half = place_ref[1]
-    pre = one_keep_ref.shape[0]
+    pre = keep_ref.shape[0]
     size = 4 * piece
-
-    def by_second(value):
-        keep, send = halves(value.reshape(1, 2, size // 2, value.shape[1]), place_ref[2])
-        return keep[0], send[0].astype(BF)
-
-    def by_first(value):
-        keep, send = halves(value.reshape(2, 2, piece, value.shape[1]), half)
-        rows = (size // 2, value.shape[1])
-        return keep.reshape(rows), send.reshape(rows).astype(BF)
-
     for at in range(pre):
-        here = slice(at * size, (at + 1) * size)
-        near = near_ref[here, :] + near_got_ref[here, :].astype(F32)
-        far = far_ref[here, :] + far_got_ref[here, :].astype(F32)
-        low = jnp.where(half == 0, near, far)
-        high = jnp.where(half == 0, far, near)
         there = slice(at % (pre // 2) * size, (at % (pre // 2) + 1) * size)
-        group = jnp.where(
+        value = jnp.where(
             half == at // (pre // 2),
-            group_near_ref[there, :] + group_near_got_ref[there, :].astype(F32),
-            group_far_ref[there, :] + group_far_got_ref[there, :].astype(F32),
+            near_ref[there, :] + near_got_ref[there, :].astype(F32),
+            far_ref[there, :] + far_got_ref[there, :].astype(F32),
         )
-        cut = low.shape[1] // 2
-        one_keep_ref[at, :, :cut], one_send_ref[at, :, :cut] = by_second(low[:, :cut])
-        one_keep_ref[at, :, cut:], one_send_ref[at, :, cut:] = by_second(group)
-        two_keep_ref[at, :, :cut], two_send_ref[at, :, :cut] = by_first(low[:, cut:])
-        two_keep_ref[at, :, cut:], two_send_ref[at, :, cut:] = by_first(high)
-
-
-def split_of(place, near, far, near_got, far_got, group, group_got, piece):
+        parts = [(slice(cut, None), value)]
+        if cut:
+            low, _ = both_halves(half, *wide, slice(at * size, (at + 1) * size))
+            parts.append((slice(0, cut), low[:, :cut]))
+        for columns, value in parts:
+            keep, send = halves(value.reshape(1, 2, size // 2, value.shape[1]), place_ref[2])
+            keep_ref[at, :, columns] = keep[0]
+            send_ref[at, :, columns] = send[0].astype(BF)
+
+
+def split_of(place, near, far, near_got, far_got, cut, piece):
     rows, columns = near.shape
-    pre = rows // (4 * piece)
-    cut = columns // 2
-    outs = []
-    for size in (cut + group[0].shape[1], cut + columns):
-        for kind in (F32, BF):
-            outs.append(((pre, 2 * piece, size), kind))
-    return call(
-        lambda *refs: split_kernel(piece, *refs),
+    out = (rows // (4 * piece), 2 * piece, 2 * columns - cut)
+    return call(
+        lambda *refs: split_kernel(cut, piece, *refs),
         "split",
         place,
-        [near, far, near_got, far_got, *group, *group_got],
-        outs,
+        [near, far, near_got, far_got],
+        [(out, F32), (out, BF)],
+    )
+
+
+def split_group_of(place, wide, group, cut, piece):
+    rows = wide[0].shape[0]
+    out = (rows // (4 * piece), 2 * piece, cut + group[0].shape[1])
+    return call(
+        lambda *refs: split_group_kernel(cut, piece, *refs),
+        "split_group",
+        place,
+        [*(wide if cut else ()), *group],
+        [(out, F32), (out, BF)],
     )
 
 
 def last_kernel(scale, place_ref, one_ref, one_got_ref, two_ref, two_got_ref, first_ref, group_ref):
     one = (one_ref[...] + one_got_ref[...].astype(F32)) * scale
     cut = one.shape[1] - group_ref.shape[1]
-    first_ref[:, :cut] = one[:, :cut]
+    if cut:
+        first_ref[:, :cut] = one[:, :cut]
     group_ref[...] = one[:, cut:]
     first_ref[:, cut:] = (two_ref[...] + two_got_ref[...].astype(F32)) * scale
 
@@ -516,27 +494,22 @@
     )
 
 
-def result_kernel(place_ref, near_ref, far_ref, grad_ref, weight_hbm, out_hbm, weight_ref, out_ref, sems):
+def result_kernel(place_ref, near_ref, far_ref, grad_ref, weight_ref, out_hbm, out_ref, sems):
     channels = grad_ref.shape[1]
     step = channels // 4
     halfway = channels // 2
-    pieces = [pl.ds(part * step, step) for part in range(4)]
-    copies = [
-        pltpu.make_async_copy(weight_hbm.at[here], weight_ref.at[here], sems.at[part])
-        for part, here in enumerate(pieces)
-    ]
-    for copy in copies:
-        copy.start()
     near = pl.ds(pl.multiple_of(place_ref[1] * halfway, halfway), halfway)
     far = pl.ds(pl.multiple_of((1 - place_ref[1]) * halfway, halfway), halfway)
     outs = []
-    for part, here in enumerate(pieces):
-        copies[part].wait()
+    for part in range(4):
+        here = slice(part * step, (part + 1) * step)
         summed = nt_dot(near_ref[...], weight_ref[here, near])
         summed += nt_dot(far_ref[...], weight_ref[here, far])
-        columns = slice(part * step, (part + 1) * step)
-        out_ref[:, columns] = (summed + grad_ref[:, columns].astype(F32)).astype(BF)
-        outs.append(pltpu.make_async_copy(out_ref.at[:, here], out_hbm.at[:, here], sems.at[4 + part]))
+        out_ref[:, here] = (summed + grad_ref[:, here].astype(F32)).astype(BF)
+        columns = pl.ds(part * step, step)
+        outs.append(
+            pltpu.make_async_copy(out_ref.at[:, columns], out_hbm.at[:, columns], sems.at[part])
+        )
         outs[-1].start()
     for out in outs:
         out.wait()
@@ -547,18 +520,14 @@
     vmem, hbm = (pl.BlockSpec(memory_space=kind) for kind in (pltpu.VMEM, pltpu.HBM))
     return pl.pallas_call(
         result_kernel,
-        in_specs=[pl.BlockSpec(memory_space=pltpu.SMEM), vmem, vmem, vmem, hbm],
+        in_specs=[pl.BlockSpec(memory_space=pltpu.SMEM), vmem, vmem, vmem, vmem],
         out_specs=hbm,
         out_shape=jax.ShapeDtypeStruct((rows, channels), BF),
-        scratch_shapes=[
-            pltpu.VMEM((channels, channels), BF),
-            pltpu.VMEM((rows, channels), BF),
-            pltpu.SemaphoreType.DMA((8,)),
-        ],
+        scratch_shapes=[pltpu.VMEM((rows, channels), BF), pltpu.SemaphoreType.DMA((4,))],
         compiler_params=pltpu.CompilerParams(vmem_limit_bytes=12 * 1024 * 1024),
         cost_estimate=pl.CostEstimate(flops=0, bytes_accessed=0, transcendentals=0),
         name="result",
-    )(place, near, far, grad_rows, pltpu.with_memory_space_constraint(first_weight, pltpu.HBM))
+    )(place, near, far, grad_rows, first_weight)
 
 
 def per_device(
@@ -582,31 +551,31 @@
     z_first = [*range(2, n_bits), 1]
     x_first = [*range(1, n_bits)]
 
-    near_own, near_core, far_sent, edge = pack_of(place, second_input, grad_rows, third_rows)
+    (
+        kept, sent, third_copy, grad_copy, weight_copy,
+        near_own, near_core, far_own, far_core, edge,
+    ) = front_of(place, third_rows, grad_rows, third_weight, second_input, piece)
     edge_got = exchange(edge, 0)
     near_other = exchange(near_core, 0)
-    far = exchange(far_sent, 1)
-
-    kept, sent, third_copy, grad_copy, weight_copy = third_of(
-        after(place, edge), third_rows, grad_rows, third_weight, piece
-    )
+    far_own = exchange(far_own, 1)
+    far_core = exchange(far_core, 1)
+    got = exchange(sent, 0)
+
+    kept, sent = fold_of(place, kept, got, left, 2, piece)
     inner, edge, inside, outside = inner_of(
         after(place, sent), grad_copy, weight_copy, third_copy, edge_got
     )
-    got = exchange(sent, 0)
-    kept, sent = fold_of(after(place, inside), kept, got, left, 2, piece)
     inside = exchange(inside, 1)
     outside = exchange_across(outside)
 
     spread, keep_in, send_in = ready_of(
-        after(place, sent, far), group_weight.T, input_rows, shard, gw, piece
+        after(place, sent, far_core, far_own), group_weight.T, input_rows, shard, gw, piece
     )
     near = body_of(place, True, inner, edge, near_own, near_other, spread, gw)
-    far_own = far[0]
-    far_other = exchange(far[1], 0)
+    far_other = exchange(far_core, 0)
     far = body_of(after(place, near[0]), False, inner, edge, far_own, far_other, spread, gw)
 
-    order = [2, 1, *range(3, n_bits)]
+    order = z_first
     left_after = [b for b in left if b != 2]
     got = exchange(sent, 2)
     kept, sent = fold_of(after(place, far[0], inside, outside), kept, got, left_after, order[1], piece)
@@ -628,15 +597,22 @@
     far_got = exchange(far_send, 0)
     group_far_got = exchange(group_far_send, 0)
 
-    one_kept, one_sent, two_kept, two_sent = split_of(
-        place, near_kept, far_kept, near_got, far_got,
-        (group_near_kept, group_far_kept), (group_near_got, group_far_got), piece,
-    )
-    kept, got = summed_up(place, kept, sent, order[2:], left_after, piece)
+    cut = shard // 2
+    wide = (near_kept, far_kept, near_got, far_got)
+    two_kept, two_sent = split_of(place, *wide, cut, piece)
+    one_kept, one_sent = split_group_of(
+        place, wide, (group_near_kept, group_far_kept, group_near_got, group_far_got), cut, piece
+    )
+    third_sent = sent
+    kept, got, _ = summed_up(place, kept, sent, order[2:], left_after, piece)
     third_wgrad = (kept + got.astype(F32)) * normalizer
-    one = summed_up(place, one_kept, one_sent, z_first, [b for b in left if b != 2], piece)
     input_grad = result_of(place, near_first, far_first, first_weight, grad_copy)
-    two = summed_up(after(place, input_grad), two_kept, two_sent, x_first, [b for b in left if b != 1], piece)
+    *two, two_sent = summed_up(
+        place, two_kept, two_sent, x_first, [b for b in left if b != 1], piece, {0: (input_grad,)}
+    )
+    *one, _ = summed_up(
+        place, one_kept, one_sent, z_first, [b for b in left if b != 2], piece, {0: (third_sent,), len(z_first) - 2: (two_sent[-1],)}
+    )
     first_wgrad, group_wgrad = last_of(place, normalizer, *one, *two, channels, TAPS * gw)
     return (input_grad.reshape(outer_grad.shape), third_wgrad, group_wgrad, first_wgrad)
 

time: 84.6 us -> 77.5 us (0.916)
  waiting for transfers between devices: 26.3 us -> 16.7 us
  starting transfers between devices: 24.3 us -> 30.7 us
  Pallas kernels: 32.2 us -> 28.3 us
    ppermute x19 -> x20, waiting for transfers between devices: 26.3 us -> 16.7 us  [exchange(): lax.ppermute(array, 'space', [(i, i ^ 1 << bit) for i in range(count)])]
    ppermute x19 -> x20, starting transfers between devices: 23.5 us -> 29.9 us  [exchange(): lax.ppermute(array, 'space', [(i, i ^ 1 << bit) for i in range(count)])]
    pallas_call x1, Pallas kernels: 5.26 us -> 2.71 us  [result_of(): pl.pallas_call(result_kernel, in_specs=[pl.BlockSpec(memory_space=pltpu.S...]
    pallas_call x17, Pallas kernels: 26.9 us -> 25.6 us  [call(): pl.pallas_call(kernel, in_specs=specs, out_specs=[pl.BlockSpec(memory_spa...]
  transfers between devices with their start and end apart: 20 -> 21, of which waited for: 9 -> 7; matrix products, arithmetic and copies ran while one was open for 1% -> 1% of each run, Pallas kernels for 26% -> 26%
where the time goes in v3:
time: 77.5 us; the launch traced here: 77.3 us
  starting transfers between devices  30.7 us (40%)
  Pallas kernels  28.3 us (37%)
  waiting for transfers between devices  16.7 us (22%)
  between operations  0.82 us (1%)
    ppermute x20, starting transfers between devices, exchange(): lax.ppermute(array, 'space', [(i, i ^ 1 << bit) for i in range(count)])  29.9 us
    pallas_call x17, Pallas kernels, call(): pl.pallas_call(kernel, in_specs=specs, out_specs=[pl.BlockSpec(memory_spa...  25.6 us
    ppermute x20, waiting for transfers between devices, exchange(): lax.ppermute(array, 'space', [(i, i ^ 1 << bit) for i in range(count)])  16.7 us
    pallas_call x1, Pallas kernels, result_of(): pl.pallas_call(result_kernel, in_specs=[pl.BlockSpec(memory_space=pltpu.S...  2.71 us
  transfers between devices with their start and end apart: 21, of which 7 were waited for; matrix products, arithmetic and copies ran while one was open for 1% of the time, Pallas kernels for 26%

profile of v3, /device:TPU:0, one launch (start us, length us, event | category | flops | bytes accessed | tf_op | source)
XLA Modules:
  0.0 77.3 jit_solution(13126013928760413542)
XLA Ops:
  0.6 3.5 %front.1 = (f32[512,1024]{1,0:T(8,128)S(1)}, bf16[512,1024]{1,0:T(8,128)(2,1)S(1)}, bf16[512,1024]{1,0:T(8,128)(2,1)S(1)}, bf16[512,1024]{1,0:T(8,128)(2,1)S(1)}...) custom-call(s32[4]{0:T(128)S(1)} %shift-right-arithmetic_and_fusion., ...), custom_call_target="tpu_custom_call" | custom-call | tf_op jit(solution)/shard_map/front/pallas_call | solution.py:45
  4.7 2.6 %collective-permute-start.3 = (bf16[4,128,256]{2,1,0:T(8,128)(2,1)S(1)}, bf16[4,128,256]{2,1,0:T(8,128)(2,1)S(1)}, u32[]{:S(2)}, u32[]{:S(2)}) collective-permute-start(bf16[4,128,256]{2,1,0:T(8,128)(2,1)S(1)} %get-tuple-element.75), channel_id=1, source_target_pairs={{0,2},{1,3},{2,0},{3,1},{4,6},{5,7},{6,4},{7,5},{8,10},{9,11},{10,... | collective-permute-start | bytes 786440 | tf_op jit(solution)/shard_map/ppermute | solution.py:18
  7.3 0.8 %fold.7 = (f32[2,128,1024]{2,1,0:T(8,128)S(1)}, bf16[2,128,1024]{2,1,0:T(8,128)(2,1)S(1)}) custom-call(s32[4]{0:T(128)S(1)} %shift-right-arithmetic_and_fusion.refs_0_.place_ref, f32[2,2,128,1024]{3,2,1,0:T(8,128)S(1)} %bitcast.25, bf16[2,2,128,1024]{3,2,1,0:T(8,128)(2,1)S(1)} %bitcast.28), custom_call_target="tpu_custom_call" | custom-call | tf_op jit(solution)/shard_map/fold/pallas_call | solution.py:45
  8.2 2.6 %collective-permute-start.8 = (bf16[2,128,1024]{2,1,0:T(8,128)(2,1)S(1)}, bf16[2,128,1024]{2,1,0:T(8,128)(2,1)S(1)}, u32[]{:S(2)}, u32[]{:S(2)}) collective-permute-start(bf16[2,128,1024]{2,1,0:T(8,128)(2,1)S(1)} %get-tuple-element.65), channel_id=1, source_target_pairs={{0,4},{1,5},{2,6},{3,7},{4,0},{5,1},{6,2},{7,3},{8,12},{9,13},{10,... | collective-permute-start | bytes 1572872 | tf_op jit(solution)/shard_map/ppermute | solution.py:18
  10.8 1.2 %collective-permute-done.1.edge_ref = bf16[16,1024]{1,0:T(8,128)(2,1)S(1)} collective-permute-done((bf16[16,1024]{1,0:T(8,128)(2,1)S(1)}, bf16[16,1024]{1,0:T(8,128)(2,1)S(1)}, u32[]{:S(2)}, u32[]{:S(2)}) %collective-permute-start.1) | collective-permute-done | bytes 32800 | tf_op jit(solution)/shard_map/ppermute | solution.py:18
  12.0 2.4 %inner.1 = (bf16[512,1024]{1,0:T(8,128)(2,1)S(1)}, bf16[16,1024]{1,0:T(8,128)(2,1)S(1)}, bf16[144,1024]{1,0:T(8,128)(2,1)S(1)}, bf16[144,1024]{1,0:T(8,128)(2,1)S(1)}) custom-call(s32[4]{0:T(128)S(1)} %shift-right-arithmetic_and_fusion.refs_0_.place_ref, bf16[512,1024]{1,0:T(8,128)(2,1)S(1)} %get-tuple-element.67.grad_ref, ...), custom_call_target="tpu_custom_call" | custom-call | tf_op jit(solution)/shard_map/inner/pallas_call | solution.py:45
  14.5 1.6 %collective-permute-start.6 = (bf16[144,1024]{1,0:T(8,128)(2,1)S(1)}, bf16[144,1024]{1,0:T(8,128)(2,1)S(1)}, u32[]{:S(2)}, u32[]{:S(2)}) collective-permute-start(bf16[144,1024]{1,0:T(8,128)(2,1)S(1)} %get-tuple-element.82), channel_id=1, source_target_pairs={{0,2},{1,3},{2,0},{3,1},{4,6},{5,7},{6,4},{7,5},{8,10},{9,11},{10,... | collective-permute-start | bytes 884744 | tf_op jit(solution)/shard_map/ppermute | solution.py:18
  16.0 0.8 %collective-permute-start.7 = (bf16[144,1024]{1,0:T(8,128)(2,1)S(1)}, bf16[144,1024]{1,0:T(8,128)(2,1)S(1)}, u32[]{:S(2)}, u32[]{:S(2)}) collective-permute-start(bf16[144,1024]{1,0:T(8,128)(2,1)S(1)} %get-tuple-element.83), channel_id=1, source_target_pairs={{2,4},{4,2},{3,5},{5,3},{6,8},{8,6},{7,9},{9,7},{10,12},{12,10},{1... | collective-permute-start | bytes 884744 | tf_op jit(solution)/shard_map/ppermute | solution.py:28
  17.0 3.0 %collective-permute-done.4.refs_3_ = bf16[4,128,256]{2,1,0:T(8,128)(2,1)S(1)} collective-permute-done((bf16[4,128,256]{2,1,0:T(8,128)(2,1)S(1)}, bf16[4,128,256]{2,1,0:T(8,128)(2,1)S(1)}, u32[]{:S(2)}, u32[]{:S(2)}) %collective-permute-start.4) | collective-permute-done | bytes 262176 | tf_op jit(solution)/shard_map/ppermute | solution.py:18
  20.0 2.0 %ready.1 = (bf16[4,3,768,256]{3,2,1,0:T(8,128)(2,1)S(1)}, bf16[512,512]{1,0:T(8,128)(2,1)S(1)}, bf16[512,512]{1,0:T(8,128)(2,1)S(1)}) custom-call(s32[4]{0:T(128)S(1)} %shift-right-arithmetic_and_fusion.refs_0_.place_ref, bf16[288,1024]{1,0:T(8,128)(2,1)S(1)} %bitcast.30, bf16[512,1024]{1,0:T(8,128)(2,1)S(1)} %bitcast.26), custom_call_target="tpu_custom_call" | custom-call | tf_op jit(solution)/shard_map/ready/pallas_call | solution.py:45
  22.1 3.0 %body_near.1 = (f32[2,512,256]{2,1,0:T(8,128)S(1)}, f32[2,288,256]{2,1,0:T(8,128)S(1)}) custom-call(s32[4]{0:T(128)S(1)} %shift-right-arithmetic_and_fusion.refs_0_.place_ref, bf16[512,1024]{1,0:T(8,128)(2,1)S(1)} %get-tuple-element.71.refs_1_, bf16[16,1024]{1,0:T(8,128)(2,1)S(1)} %get-tuple-element.72.refs_2_, ...), custom_call_target="tpu_custom_call" | custom-call | tf_op jit(solution)/shard_map/body_near/pallas_call | solution.py:45
  25.1 3.0 %body_far.1 = (f32[2,512,256]{2,1,0:T(8,128)S(1)}, f32[2,288,256]{2,1,0:T(8,128)S(1)}) custom-call(s32[4]{0:T(128)S(1)} %shift-right-arithmetic_and_fusion.refs_0_.place_ref, bf16[512,1024]{1,0:T(8,128)(2,1)S(1)} %get-tuple-element.71.refs_1_, bf16[16,1024]{1,0:T(8,128)(2,1)S(1)} %get-tuple-element.72.refs_2_, ...), custom_call_target="tpu_custom_call" | custom-call | tf_op jit(solution)/shard_map/body_far/pallas_call | solution.py:45
  28.1 3.6 %collective-permute-done.6.refs_5_ = bf16[144,1024]{1,0:T(8,128)(2,1)S(1)} collective-permute-done((bf16[144,1024]{1,0:T(8,128)(2,1)S(1)}, bf16[144,1024]{1,0:T(8,128)(2,1)S(1)}, u32[]{:S(2)}, u32[]{:S(2)}) %collective-permute-start.6) | collective-permute-done | bytes 294944 | tf_op jit(solution)/shard_map/ppermute | solution.py:18
  31.7 0.7 fold.8
  32.4 2.0 %close_far.1 = (bf16[512,512]{1,0:T(8,128)(2,1)S(1)}, f32[512,512]{1,0:T(8,128)S(1)}, bf16[512,512]{1,0:T(8,128)(2,1)S(1)}, f32[256,288]{1,0:T(8,128)S(1)}, bf16[256,288]{1,0:T(8,128)(2,1)S(1)}) custom-call(s32[4]{0:T(128)S(1)} %shift-right-arithmetic_and_fusion.refs_0_.place_ref, f32[2,512,256]{2,1,0:T(8,128)S(1)} %get-tuple-element.81.refs_1_, ...), custom_call_target="tpu_custom_call" | custom-call | tf_op jit(solution)/shard_map/close_far/pallas_call | solution.py:45
  34.5 2.0 %close_near.1 = (bf16[512,512]{1,0:T(8,128)(2,1)S(1)}, f32[512,512]{1,0:T(8,128)S(1)}, bf16[512,512]{1,0:T(8,128)(2,1)S(1)}, f32[256,288]{1,0:T(8,128)S(1)}, bf16[256,288]{1,0:T(8,128)(2,1)S(1)}) custom-call(s32[4]{0:T(128)S(1)} %shift-right-arithmetic_and_fusion.refs_0_.place_ref, f32[2,512,256]{2,1,0:T(8,128)S(1)} %get-tuple-element.79.refs_1_, ...), custom_call_target="tpu_custom_call" | custom-call | tf_op jit(solution)/shard_map/close_near/pallas_call | solution.py:45
  37.1 1.5 %collective-permute-done.11.refs_3_ = bf16[512,512]{1,0:T(8,128)(2,1)S(1)} collective-permute-done((bf16[512,512]{1,0:T(8,128)(2,1)S(1)}, bf16[512,512]{1,0:T(8,128)(2,1)S(1)}, u32[]{:S(2)}, u32[]{:S(2)}) %collective-permute-start.11) | collective-permute-done | bytes 524320 | tf_op jit(solution)/shard_map/ppermute | solution.py:18
  38.6 0.9 %split.1 = (f32[2,128,896]{2,1,0:T(8,128)S(1)}, bf16[2,128,896]{2,1,0:T(8,128)(2,1)S(1)}) custom-call(s32[4]{0:T(128)S(1)} %shift-right-arithmetic_and_fusion.refs_0_.place_ref, f32[512,512]{1,0:T(8,128)S(1)} %get-tuple-element.98.refs_1_, f32[512,512]{1,0:T(8,128)S(1)} %get-tuple-element.99.refs_2_, bf16[512,512]{1,0:T(8,128)(2,1)S(1)} %collective-permute-done.11.refs_3_, ...), custom_call_target="tpu_custom_call" | custom-call | tf_op jit(solution)/shard_map/split/pallas_call | solution.py:45
  39.6 2.6 %collective-permute-start.13 = (bf16[2,128,896]{2,1,0:T(8,128)(2,1)S(1)}, bf16[2,128,896]{2,1,0:T(8,128)(2,1)S(1)}, u32[]{:S(2)}, u32[]{:S(2)}) collective-permute-start(bf16[2,128,896]{2,1,0:T(8,128)(2,1)S(1)} %get-tuple-element.103), channel_id=1, source_target_pairs={{0,2},{1,3},{2,0},{3,1},{4,6},{5,7},{6,4},{7,5},{8,10},{9,11},{10,... | collective-permute-start | bytes 1376264 | tf_op jit(solution)/shard_map/ppermute | solution.py:18
  42.6 2.6 %collective-permute-start.9 = (bf16[1,128,1024]{2,1,0:T(8,128)(2,1)S(1)}, bf16[1,128,1024]{2,1,0:T(8,128)(2,1)S(1)}, u32[]{:S(2)}, u32[]{:S(2)}) collective-permute-start(bf16[1,128,1024]{2,1,0:T(8,128)(2,1)S(1)} %get-tuple-element.86), channel_id=1, source_target_pairs={{0,8},{1,9},{2,10},{3,11},{4,12},{5,13},{6,14},{7,15},{8,0},{9,1},... | collective-permute-start | bytes 786440 | tf_op jit(solution)/shard_map/ppermute | solution.py:18
  45.3 0.8 %split_group.1 = (f32[2,128,416]{2,1,0:T(8,128)S(1)}, bf16[2,128,416]{2,1,0:T(8,128)(2,1)S(1)}) custom-call(s32[4]{0:T(128)S(1)} %shift-right-arithmetic_and_fusion.refs_0_.place_ref, f32[512,512]{1,0:T(8,128)S(1)} %get-tuple-element.98.refs_1_, f32[512,512]{1,0:T(8,128)S(1)} %get-tuple-element.99.refs_2_, ...), custom_call_target="tpu_custom_call" | custom-call | tf_op jit(solution)/shard_map/split_group/pallas_call | solution.py:45
  46.1 2.8 %collective-permute-start.17 = (bf16[2,128,416]{2,1,0:T(8,128)(2,1)S(1)}, bf16[2,128,416]{2,1,0:T(8,128)(2,1)S(1)}, u32[]{:S(2)}, u32[]{:S(2)}) collective-permute-start(bf16[2,128,416]{2,1,0:T(8,128)(2,1)S(1)} %get-tuple-element.114), channel_id=1, source_target_pairs={{0,4},{1,5},{2,6},{3,7},{4,0},{5,1},{6,2},{7,3},{8,12},{9,13},{10,... | collective-permute-start | bytes 638984 | tf_op jit(solution)/shard_map/ppermute | solution.py:18
  48.9 2.7 %result.1 = bf16[512,1024]{1,0:T(8,128)(2,1)} custom-call(s32[4]{0:T(128)S(1)} %shift-right-arithmetic_and_fusion.refs_0_.place_ref, bf16[512,512]{1,0:T(8,128)(2,1)S(1)} %get-tuple-element.91.near_ref, bf16[512,512]{1,0:T(8,128)(2,1)S(1)} %get-tuple-element.93.far_ref, bf16[512,1024]{1,0:T(8,128)(2,1)S(1)} %get-tuple-element.67.grad_ref, ...), custom_call_target="tpu_custom_call" | custom-call | tf_op jit(solution)/shard_map/result/pallas_call | solution.py:521
  51.6 1.6 %collective-permute-done.13 = bf16[2,128,896]{2,1,0:T(8,128)(2,1)S(1)} collective-permute-done((bf16[2,128,896]{2,1,0:T(8,128)(2,1)S(1)}, bf16[2,128,896]{2,1,0:T(8,128)(2,1)S(1)}, u32[]{:S(2)}, u32[]{:S(2)}) %collective-permute-start.13) | collective-permute-done | bytes 458784 | tf_op jit(solution)/shard_map/ppermute | solution.py:18
  53.8 3.9 %collective-permute-start.14 = (bf16[2,64,896]{2,1,0:T(8,128)(2,1)S(1)}, bf16[2,64,896]{2,1,0:T(8,128)(2,1)S(1)}, u32[]{:S(2)}, u32[]{:S(2)}) collective-permute-start(bf16[2,64,896]{2,1,0:T(8,128)(2,1)S(1)} %get-tuple-element.105), channel_id=1, source_target_pairs={{0,4},{1,5},{2,6},{3,7},{4,0},{5,1},{6,2},{7,3},{8,12},{9,13},{10,... | collective-permute-start | bytes 688136 | tf_op jit(solution)/shard_map/ppermute | solution.py:18
  58.4 1.8 %collective-permute-start.10 = (bf16[1,64,1024]{2,1,0:T(8,128)(2,1)S(1)}, bf16[1,64,1024]{2,1,0:T(8,128)(2,1)S(1)}, u32[]{:S(2)}, u32[]{:S(2)}) collective-permute-start(bf16[1,64,1024]{2,1,0:T(8,128)(2,1)S(1)} %get-tuple-element.96), channel_id=1, source_target_pairs={{0,2},{1,3},{2,0},{3,1},{4,6},{5,7},{6,4},{7,5},{8,10},{9,11},{10,... | collective-permute-start | bytes 393224 | tf_op jit(solution)/shard_map/ppermute | solution.py:18
  60.8 2.7 %collective-permute-start.18 = (bf16[1,128,416]{2,1,0:T(8,128)(2,1)S(1)}, bf16[1,128,416]{2,1,0:T(8,128)(2,1)S(1)}, u32[]{:S(2)}, u32[]{:S(2)}) collective-permute-start(bf16[1,128,416]{2,1,0:T(8,128)(2,1)S(1)} %get-tuple-element.116), channel_id=1, source_target_pairs={{0,8},{1,9},{2,10},{3,11},{4,12},{5,13},{6,14},{7,15},{8,0},{9,1},... | collective-permute-start | bytes 319496 | tf_op jit(solution)/shard_map/ppermute | solution.py:18
  64.1 4.4 %collective-permute-start.20 = (bf16[1,64,896]{2,1,0:T(8,128)(2,1)S(1)}, bf16[1,64,896]{2,1,0:T(8,128)(2,1)S(1)}, u32[]{:S(2)}, u32[]{:S(2)}) collective-permute-start(bf16[1,64,896]{2,1,0:T(8,128)(2,1)S(1)} %get-tuple-element.106), channel_id=1, source_target_pairs={{0,8},{1,9},{2,10},{3,11},{4,12},{5,13},{6,14},{7,15},{8,0},{9,1},... | collective-permute-start | bytes 344072 | tf_op jit(solution)/shard_map/ppermute | solution.py:18
  68.5 2.5 %collective-permute-done.18 = bf16[1,128,416]{2,1,0:T(8,128)(2,1)S(1)} collective-permute-done((bf16[1,128,416]{2,1,0:T(8,128)(2,1)S(1)}, bf16[1,128,416]{2,1,0:T(8,128)(2,1)S(1)}, u32[]{:S(2)}, u32[]{:S(2)}) %collective-permute-start.18) | collective-permute-done | bytes 106528 | tf_op jit(solution)/shard_map/ppermute | solution.py:18
  72.2 0.7 multiply_bitcast_fusion
  72.9 3.1 %collective-permute-done.19 = bf16[1,64,416]{2,1,0:T(8,128)(2,1)S(1)} collective-permute-done((bf16[1,64,416]{2,1,0:T(8,128)(2,1)S(1)}, bf16[1,64,416]{2,1,0:T(8,128)(2,1)S(1)}, u32[]{:S(2)}, u32[]{:S(2)}) %collective-permute-start.19) | collective-permute-done | bytes 53280 | tf_op jit(solution)/shard_map/ppermute | solution.py:18
  76.0 1.3 %last.1 = (f32[64,1024]{1,0:T(8,128)}, f32[64,288]{1,0:T(8,128)}) custom-call(s32[4]{0:T(128)S(1)} %shift-right-arithmetic_and_fusion.refs_0_.place_ref, f32[64,416]{1,0:T(8,128)S(1)} %bitcast.41, bf16[64,416]{1,0:T(8,128)(2,1)S(1)} %bitcast.44, f32[64,896]{1,0:T(8,128)S(1)} %bitcast.39, bf16[64,896]{1,0:T(8,128)(2,1)S(1)} %bitcast.43), custom_call_target="tpu_custom_call" | custom-call | tf_op jit(solution)/shard_map/last/pallas_call | solution.py:45
  (36 shorter events, 5.4 us)
Async XLA Ops:
  4.2 3.2 %collective-permute-start = (bf16[512,1024]{1,0:T(8,128)(2,1)S(1)}, bf16[512,1024]{1,0:T(8,128)(2,1)S(1)}, u32[]{:S(2)}, u32[]{:S(2)}) collective-permute-start(bf16[512,1024]{1,0:T(8,128)(2,1)S(1)} %get-tuple-element.64), channel_id=1, source_target_pairs={{0,1},{1,0},{2,3},{3,2},{4,5},{5,4},{6,7},{7,6},{8,9},{9,8},{10,11... | collective-permute-start | bytes 3145736 | tf_op jit(solution)/shard_map/ppermute | solution.py:18
  4.7 12.2 %collective-permute-start.3 = (bf16[4,128,256]{2,1,0:T(8,128)(2,1)S(1)}, bf16[4,128,256]{2,1,0:T(8,128)(2,1)S(1)}, u32[]{:S(2)}, u32[]{:S(2)}) collective-permute-start(bf16[4,128,256]{2,1,0:T(8,128)(2,1)S(1)} %get-tuple-element.75), channel_id=1, source_target_pairs={{0,2},{1,3},{2,0},{3,1},{4,6},{5,7},{6,4},{7,5},{8,10},{9,11},{10,... | collective-permute-start | bytes 786440 | tf_op jit(solution)/shard_map/ppermute | solution.py:18
  7.3 12.8 %collective-permute-start.4 = (bf16[4,128,256]{2,1,0:T(8,128)(2,1)S(1)}, bf16[4,128,256]{2,1,0:T(8,128)(2,1)S(1)}, u32[]{:S(2)}, u32[]{:S(2)}) collective-permute-start(bf16[4,128,256]{2,1,0:T(8,128)(2,1)S(1)} %get-tuple-element.76), channel_id=1, source_target_pairs={{0,2},{1,3},{2,0},{3,1},{4,6},{5,7},{6,4},{7,5},{8,10},{9,11},{10,... | collective-permute-start | bytes 786440 | tf_op jit(solution)/shard_map/ppermute | solution.py:18
  8.2 23.5 %collective-permute-start.8 = (bf16[2,128,1024]{2,1,0:T(8,128)(2,1)S(1)}, bf16[2,128,1024]{2,1,0:T(8,128)(2,1)S(1)}, u32[]{:S(2)}, u32[]{:S(2)}) collective-permute-start(bf16[2,128,1024]{2,1,0:T(8,128)(2,1)S(1)} %get-tuple-element.65), channel_id=1, source_target_pairs={{0,4},{1,5},{2,6},{3,7},{4,0},{5,1},{6,2},{7,3},{8,12},{9,13},{10,... | collective-permute-start | bytes 1572872 | tf_op jit(solution)/shard_map/ppermute | solution.py:18
  10.8 1.2 %collective-permute-start.1 = (bf16[16,1024]{1,0:T(8,128)(2,1)S(1)}, bf16[16,1024]{1,0:T(8,128)(2,1)S(1)}, u32[]{:S(2)}, u32[]{:S(2)}) collective-permute-start(bf16[16,1024]{1,0:T(8,128)(2,1)S(1)} %get-tuple-element.70), channel_id=1, source_target_pairs={{0,1},{1,0},{2,3},{3,2},{4,5},{5,4},{6,7},{7,6},{8,9},{9,8},{10,11... | collective-permute-start | bytes 98312 | tf_op jit(solution)/shard_map/ppermute | solution.py:18
  12.0 8.0 %copy-start.1 = (bf16[1,4,128,1024]{3,2,1,0:T(8,128)(2,1)S(1)}, bf16[1,4,128,1024]{3,2,1,0:T(8,128)(2,1)}, u32[]{:S(2)}) copy-start(bf16[1,4,128,1024]{3,2,1,0:T(8,128)(2,1)} %param.8) | copy-start | bytes 3145732
  12.0 8.0 %copy-start.2 = (bf16[1024,288]{0,1:T(8,128)(2,1)S(1)}, bf16[1024,288]{0,1:T(8,128)(2,1)}, u32[]{:S(2)}) copy-start(bf16[1024,288]{0,1:T(8,128)(2,1)} %param.12) | copy-start | bytes 1769476
  14.5 17.2 %collective-permute-start.6 = (bf16[144,1024]{1,0:T(8,128)(2,1)S(1)}, bf16[144,1024]{1,0:T(8,128)(2,1)S(1)}, u32[]{:S(2)}, u32[]{:S(2)}) collective-permute-start(bf16[144,1024]{1,0:T(8,128)(2,1)S(1)} %get-tuple-element.82), channel_id=1, source_target_pairs={{0,2},{1,3},{2,0},{3,1},{4,6},{5,7},{6,4},{7,5},{8,10},{9,11},{10,... | collective-permute-start | bytes 884744 | tf_op jit(solution)/shard_map/ppermute | solution.py:18
  16.0 15.7 %collective-permute-start.7 = (bf16[144,1024]{1,0:T(8,128)(2,1)S(1)}, bf16[144,1024]{1,0:T(8,128)(2,1)S(1)}, u32[]{:S(2)}, u32[]{:S(2)}) collective-permute-start(bf16[144,1024]{1,0:T(8,128)(2,1)S(1)} %get-tuple-element.83), channel_id=1, source_target_pairs={{2,4},{4,2},{3,5},{5,3},{6,8},{8,6},{7,9},{9,7},{10,12},{12,10},{1... | collective-permute-start | bytes 884744 | tf_op jit(solution)/shard_map/ppermute | solution.py:28
  16.9 5.2 %collective-permute-start.2 = (bf16[4,128,256]{2,1,0:T(8,128)(2,1)S(1)}, bf16[4,128,256]{2,1,0:T(8,128)(2,1)S(1)}, u32[]{:S(2)}, u32[]{:S(2)}) collective-permute-start(bf16[4,128,256]{2,1,0:T(8,128)(2,1)S(1)} %get-tuple-element.74), channel_id=1, source_target_pairs={{0,1},{1,0},{2,3},{3,2},{4,5},{5,4},{6,7},{7,6},{8,9},{9,8},{10,11... | collective-permute-start | bytes 786440 | tf_op jit(solution)/shard_map/ppermute | solution.py:18
  20.0 5.0 %collective-permute-start.5 = (bf16[4,128,256]{2,1,0:T(8,128)(2,1)S(1)}, bf16[4,128,256]{2,1,0:T(8,128)(2,1)S(1)}, u32[]{:S(2)}, u32[]{:S(2)}) collective-permute-start(bf16[4,128,256]{2,1,0:T(8,128)(2,1)S(1)} %collective-permute-done.3), channel_id=1, source_target_pairs={{0,1},{1,0},{2,3},{3,2},{4,5},{5,4},{6,7},{7,6},{8,9},{9,8},{10,11... | collective-permute-start | bytes 786440 | tf_op jit(solution)/shard_map/ppermute | solution.py:18
  34.4 2.7 %collective-permute-start.12 = (bf16[512,512]{1,0:T(8,128)(2,1)S(1)}, bf16[512,512]{1,0:T(8,128)(2,1)S(1)}, u32[]{:S(2)}, u32[]{:S(2)}) collective-permute-start(bf16[512,512]{1,0:T(8,128)(2,1)S(1)} %get-tuple-element.101), channel_id=1, source_target_pairs={{0,1},{1,0},{2,3},{3,2},{4,5},{5,4},{6,7},{7,6},{8,9},{9,8},{10,11... | collective-permute-start | bytes 1572872 | tf_op jit(solution)/shard_map/ppermute | solution.py:18
  36.5 2.1 %collective-permute-start.11 = (bf16[512,512]{1,0:T(8,128)(2,1)S(1)}, bf16[512,512]{1,0:T(8,128)(2,1)S(1)}, u32[]{:S(2)}, u32[]{:S(2)}) collective-permute-start(bf16[512,512]{1,0:T(8,128)(2,1)S(1)} %get-tuple-element.100), channel_id=1, source_target_pairs={{0,1},{1,0},{2,3},{3,2},{4,5},{5,4},{6,7},{7,6},{8,9},{9,8},{10,11... | collective-permute-start | bytes 1572872 | tf_op jit(solution)/shard_map/ppermute | solution.py:18
  39.6 13.6 %collective-permute-start.13 = (bf16[2,128,896]{2,1,0:T(8,128)(2,1)S(1)}, bf16[2,128,896]{2,1,0:T(8,128)(2,1)S(1)}, u32[]{:S(2)}, u32[]{:S(2)}) collective-permute-start(bf16[2,128,896]{2,1,0:T(8,128)(2,1)S(1)} %get-tuple-element.103), channel_id=1, source_target_pairs={{0,2},{1,3},{2,0},{3,1},{4,6},{5,7},{6,4},{7,5},{8,10},{9,11},{10,... | collective-permute-start | bytes 1376264 | tf_op jit(solution)/shard_map/ppermute | solution.py:18
  42.1 3.1 %collective-permute-start.16 = (bf16[256,288]{1,0:T(8,128)(2,1)S(1)}, bf16[256,288]{1,0:T(8,128)(2,1)S(1)}, u32[]{:S(2)}, u32[]{:S(2)}) collective-permute-start(bf16[256,288]{1,0:T(8,128)(2,1)S(1)} %get-tuple-element.112), channel_id=1, source_target_pairs={{0,1},{1,0},{2,3},{3,2},{4,5},{5,4},{6,7},{7,6},{8,9},{9,8},{10,11... | collective-permute-start | bytes 442376 | tf_op jit(solution)/shard_map/ppermute | solution.py:18
  42.2 3.0 %collective-permute-start.15 = (bf16[256,288]{1,0:T(8,128)(2,1)S(1)}, bf16[256,288]{1,0:T(8,128)(2,1)S(1)}, u32[]{:S(2)}, u32[]{:S(2)}) collective-permute-start(bf16[256,288]{1,0:T(8,128)(2,1)S(1)} %get-tuple-element.111), channel_id=1, source_target_pairs={{0,1},{1,0},{2,3},{3,2},{4,5},{5,4},{6,7},{7,6},{8,9},{9,8},{10,11... | collective-permute-start | bytes 442376 | tf_op jit(solution)/shard_map/ppermute | solution.py:18
  42.6 15.1 %collective-permute-start.9 = (bf16[1,128,1024]{2,1,0:T(8,128)(2,1)S(1)}, bf16[1,128,1024]{2,1,0:T(8,128)(2,1)S(1)}, u32[]{:S(2)}, u32[]{:S(2)}) collective-permute-start(bf16[1,128,1024]{2,1,0:T(8,128)(2,1)S(1)} %get-tuple-element.86), channel_id=1, source_target_pairs={{0,8},{1,9},{2,10},{3,11},{4,12},{5,13},{6,14},{7,15},{8,0},{9,1},... | collective-permute-start | bytes 786440 | tf_op jit(solution)/shard_map/ppermute | solution.py:18
  45.2 3.6 %copy-start = (bf16[1024,1024]{1,0:T(8,128)(2,1)S(1)}, bf16[1024,1024]{1,0:T(8,128)(2,1)}, u32[]{:S(2)}) copy-start(bf16[1024,1024]{1,0:T(8,128)(2,1)} %weight_ref.1) | copy-start | bytes 6291460
  46.1 14.1 %collective-permute-start.17 = (bf16[2,128,416]{2,1,0:T(8,128)(2,1)S(1)}, bf16[2,128,416]{2,1,0:T(8,128)(2,1)S(1)}, u32[]{:S(2)}, u32[]{:S(2)}) collective-permute-start(bf16[2,128,416]{2,1,0:T(8,128)(2,1)S(1)} %get-tuple-element.114), channel_id=1, source_target_pairs={{0,4},{1,5},{2,6},{3,7},{4,0},{5,1},{6,2},{7,3},{8,12},{9,13},{10,... | collective-permute-start | bytes 638984 | tf_op jit(solution)/shard_map/ppermute | solution.py:18
  53.8 9.7 %collective-permute-start.14 = (bf16[2,64,896]{2,1,0:T(8,128)(2,1)S(1)}, bf16[2,64,896]{2,1,0:T(8,128)(2,1)S(1)}, u32[]{:S(2)}, u32[]{:S(2)}) collective-permute-start(bf16[2,64,896]{2,1,0:T(8,128)(2,1)S(1)} %get-tuple-element.105), channel_id=1, source_target_pairs={{0,4},{1,5},{2,6},{3,7},{4,0},{5,1},{6,2},{7,3},{8,12},{9,13},{10,... | collective-permute-start | bytes 688136 | tf_op jit(solution)/shard_map/ppermute | solution.py:18
  58.4 13.8 %collective-permute-start.10 = (bf16[1,64,1024]{2,1,0:T(8,128)(2,1)S(1)}, bf16[1,64,1024]{2,1,0:T(8,128)(2,1)S(1)}, u32[]{:S(2)}, u32[]{:S(2)}) collective-permute-start(bf16[1,64,1024]{2,1,0:T(8,128)(2,1)S(1)} %get-tuple-element.96), channel_id=1, source_target_pairs={{0,2},{1,3},{2,0},{3,1},{4,6},{5,7},{6,4},{7,5},{8,10},{9,11},{10,... | collective-permute-start | bytes 393224 | tf_op jit(solution)/shard_map/ppermute | solution.py:18
  60.8 10.2 %collective-permute-start.18 = (bf16[1,128,416]{2,1,0:T(8,128)(2,1)S(1)}, bf16[1,128,416]{2,1,0:T(8,128)(2,1)S(1)}, u32[]{:S(2)}, u32[]{:S(2)}) collective-permute-start(bf16[1,128,416]{2,1,0:T(8,128)(2,1)S(1)} %get-tuple-element.116), channel_id=1, source_target_pairs={{0,8},{1,9},{2,10},{3,11},{4,12},{5,13},{6,14},{7,15},{8,0},{9,1},... | collective-permute-start | bytes 319496 | tf_op jit(solution)/shard_map/ppermute | solution.py:18
  64.1 11.9 %collective-permute-start.20 = (bf16[1,64,896]{2,1,0:T(8,128)(2,1)S(1)}, bf16[1,64,896]{2,1,0:T(8,128)(2,1)S(1)}, u32[]{:S(2)}, u32[]{:S(2)}) collective-permute-start(bf16[1,64,896]{2,1,0:T(8,128)(2,1)S(1)} %get-tuple-element.106), channel_id=1, source_target_pairs={{0,8},{1,9},{2,10},{3,11},{4,12},{5,13},{6,14},{7,15},{8,0},{9,1},... | collective-permute-start | bytes 344072 | tf_op jit(solution)/shard_map/ppermute | solution.py:18
  71.7 4.3 %collective-permute-start.19 = (bf16[1,64,416]{2,1,0:T(8,128)(2,1)S(1)}, bf16[1,64,416]{2,1,0:T(8,128)(2,1)S(1)}, u32[]{:S(2)}, u32[]{:S(2)}) collective-permute-start(bf16[1,64,416]{2,1,0:T(8,128)(2,1)S(1)} %get-tuple-element.118), channel_id=1, source_target_pairs={{0,2},{1,3},{2,0},{3,1},{4,6},{5,7},{6,4},{7,5},{8,10},{9,11},{10,... | collective-permute-start | bytes 159752 | tf_op jit(solution)/shard_map/ppermute | solution.py:18

commit v4 on v3

--- a/solution.py
+++ b/solution.py
@@ -109,14 +109,14 @@
 def front_kernel(
     piece, place_ref, left_hbm, right_hbm, weight_hbm, second_hbm,
     keep_ref, send_ref, left_ref, right_ref, weight_ref,
-    near_own_ref, near_core_ref, far_own_ref, far_core_ref, edge_ref, sems,
+    near_own_ref, near_core_ref, far_ref, edge_ref, sems,
 ):
     rows, width, _ = near_own_ref.shape
     core, half = place_ref[0], place_ref[1]
     copies = [(left_hbm, left_ref), (right_hbm, right_ref)]
     for target, row_at, column_at in (
-        (far_own_ref, 1 - half, core),
-        (far_core_ref, 1 - half, 1 - core),
+        (far_ref.at[0], 1 - half, core),
+        (far_ref.at[1], 1 - half, 1 - core),
         (near_core_ref, half, 1 - core),
         (near_own_ref, half, core),
     ):
@@ -158,7 +158,7 @@
     positions, channels = grad_rows.shape
     _, rows, columns, shard = second_input.shape
     wide = ((positions, channels), BF)
-    quarter = ((rows // 2, columns // 2, shard), BF)
+    quarter = (rows // 2, columns // 2, shard)
     return call(
         lambda *refs: front_kernel(piece, *refs),
         "front",
@@ -170,33 +170,43 @@
             wide,
             wide,
             ((channels, channels), BF),
-            *[quarter] * 4,
+            (quarter, BF),
+            (quarter, BF),
+            ((2, *quarter), BF),
             ((16, channels), BF),
         ],
         [pltpu.SemaphoreType.DMA((7,))],
     )
 
 
-def fold_kernel(bit, place_ref, total_ref, received_ref, keep_ref, send_ref):
-    for at in range(total_ref.shape[0]):
-        total = total_ref[at] + received_ref[at].astype(F32)
-        keep, send = halves(total[None], place_ref[bit])
-        keep_ref[at] = keep[0]
-        send_ref[at] = send[0].astype(BF)
-
-
-def fold_of(place, total, received, left, bit, piece):
+def fold_kernel(bit, got, place_ref, total_ref, *refs):
+    received_refs, (keep_ref, *send_refs) = refs[:got], refs[got:]
+    pre = total_ref.shape[0]
+    for at in range(pre):
+        pair = []
+        for side in range(2):
+            which, row = divmod(2 * at + side, 2 * pre // got)
+            pair.append(total_ref[at, side] + received_refs[which][row].astype(F32))
+        low, high = pair
+        keep_ref[at] = jnp.where(place_ref[bit] == 0, low, high)
+        which, row = divmod(at, pre // len(send_refs))
+        send_refs[which][row] = jnp.where(place_ref[bit] == 0, high, low).astype(BF)
+
+
+def fold_of(place, total, received, left, bit, piece, parts=1):
     at = left.index(bit)
     columns = total.shape[-1]
-    shape = (1 << at, 2, piece << (len(left) - at - 1), columns)
-    out = (shape[0], *shape[2:])
-    return call(
-        lambda *refs: fold_kernel(bit, *refs),
+    pre, rows = 1 << at, piece << (len(left) - at - 1)
+    got = len(received)
+    received = [part.reshape(2 * pre // got, rows, columns) for part in received]
+    keep, *send = call(
+        lambda *refs: fold_kernel(bit, got, *refs),
         "fold",
         place,
-        [total.reshape(shape), received.reshape(shape)],
-        [(out, F32), (out, BF)],
-    )
+        [total.reshape(pre, 2, rows, columns), *received],
+        [((pre, rows, columns), F32)] + [((pre // parts, rows, columns), BF)] * parts,
+    )
+    return keep, (send if parts > 1 else send[0])
 
 
 def summed_up(place, keep, send, order, left, piece, gates={}):
@@ -204,7 +214,7 @@
     sent = []
     for step, bit in enumerate(order[1:]):
         keep, send = fold_of(
-            after(place, *gates.get(step, ())), keep, received, left, bit, piece
+            after(place, *gates.get(step, ())), keep, [received], left, bit, piece
         )
         left = [b for b in left if b != bit]
         sent.append(send)
@@ -276,16 +286,20 @@
     return mine
 
 
+def whole(refs, positions, step):
+    return jnp.concatenate([ref[...].reshape(-1, step) for ref in refs])
+
+
 def body_kernel(
-    gw, near, place_ref, inner_ref, edge_ref, own_ref, other_ref, spread_ref,
-    back_ref, term_ref, window_ref,
+    gw, near, place_ref, inner_ref, edge_ref, spread_ref, *refs
 ):
-    positions = inner_ref.shape[0]
-    step = own_ref.shape[2]
+    *slots, back_ref, term_ref, window_ref = refs
+    slots = slots[:1], slots[1:]
+    positions, step = back_ref.shape[1:]
     width = positions // ROWS
     core = place_ref[0]
     side = place_ref[1] if near else 1 - place_ref[1]
-    for slot, second_ref in enumerate((own_ref, other_ref)):
+    for slot, second_refs in enumerate(slots):
         shard = 2 * side + (core if slot == 0 else 1 - core)
         columns = pl.ds(pl.multiple_of(shard * step, step), step)
         edges = edge_ref[:, columns].astype(F32)
@@ -295,7 +309,7 @@
             left, right = jnp.where(core == 1, edge, 0.0), jnp.where(core == 0, edge, 0.0)
             for at, line in enumerate(shifted(inner_ref[here, columns], left, right)):
                 window_ref[here, at * step : (at + 1) * step] = line
-        flipped = second_ref[...].reshape(positions, step).T
+        flipped = whole(second_refs, positions, step).T
         for tap_row in (1, 0, 2):
             count = ROWS if tap_row == 1 else ROWS - 1
             take = pl.ds(width if tap_row == 0 else 0, count * width)
@@ -324,27 +338,28 @@
         lambda *refs: body_kernel(gw, near, *refs),
         "body_near" if near else "body_far",
         place,
-        [inner, edge, own, other, spread],
+        [inner, edge, spread, own, *other],
         [((2, positions, shard), F32), ((2, TAPS * gw, shard), F32)],
         [pltpu.VMEM((positions, 3 * shard), BF)],
     )
 
 
 def close_kernel(
-    gw, piece, near, place_ref, back_ref, term_ref, own_ref, other_ref, inside_ref, outside_ref,
-    spread_ref, keep_in_ref, send_in_ref,
-    first_ref, keep_ref, send_ref, group_keep_ref, group_send_ref,
+    gw, piece, near, place_ref, back_ref, term_ref, inside_ref, outside_ref,
+    spread_ref, keep_in_ref, send_in_ref, *refs
 ):
+    *slots, first_ref, keep_ref, send_ref, group_keep_ref, group_send_ref = refs
+    slots = slots[:1], slots[1:]
     _, positions, step = back_ref.shape
     width = positions // ROWS
     core, half = place_ref[0], place_ref[1]
     side = half if near else 1 - half
-    for slot, second_ref in enumerate((own_ref, other_ref)):
+    for slot, second_refs in enumerate(slots):
         turn = core if slot == 0 else 1 - core
         shard = 2 * side + turn
         columns = pl.ds(pl.multiple_of(shard * step, step), step)
         inside, outside = inside_ref[:, columns], outside_ref[:, columns]
-        second = second_ref[...].reshape(positions, step)
+        second = whole(second_refs, positions, step)
         backs, terms = {}, {}
         for tap_row, row in ((2, 0), (0, ROWS - 1)):
             rim = jnp.where(half == (0 if row == 0 else 1), outside, inside)
@@ -393,7 +408,7 @@
         lambda *refs: close_kernel(gw, piece, near, *refs),
         "close_near" if near else "close_far",
         place,
-        [back, term, own, other, inside, outside, spread, keep_in, send_in],
+        [back, term, inside, outside, spread, keep_in, send_in, own, *other],
         [
             ((positions, 2 * shard), BF),
             ((rows, 2 * shard), F32),
@@ -553,15 +568,15 @@
 
     (
         kept, sent, third_copy, grad_copy, weight_copy,
-        near_own, near_core, far_own, far_core, edge,
+        near_own, near_core, far, edge,
     ) = front_of(place, third_rows, grad_rows, third_weight, second_input, piece)
     edge_got = exchange(edge, 0)
     near_other = exchange(near_core, 0)
-    far_own = exchange(far_own, 1)
-    far_core = exchange(far_core, 1)
+    far = exchange(far, 1)
     got = exchange(sent, 0)
 
-    kept, sent = fold_of(place, kept, got, left, 2, piece)
+    kept, sent_parts = fold_of(place, kept, [got], left, 2, piece, parts=2)
+    sent = sent_parts[0]
     inner, edge, inside, outside = inner_of(
         after(place, sent), grad_copy, weight_copy, third_copy, edge_got
     )
@@ -569,27 +584,28 @@
     outside = exchange_across(outside)
 
     spread, keep_in, send_in = ready_of(
-        after(place, sent, far_core, far_own), group_weight.T, input_rows, shard, gw, piece
-    )
-    near = body_of(place, True, inner, edge, near_own, near_other, spread, gw)
-    far_other = exchange(far_core, 0)
+        after(place, sent), group_weight.T, input_rows, shard, gw, piece
+    )
+    near = body_of(place, True, inner, edge, near_own, (near_other,), spread, gw)
+    far_own = far[0]
+    far_other = tuple(exchange(far[1, r : r + ROWS // 2], 0) for r in (0, ROWS // 2))
     far = body_of(after(place, near[0]), False, inner, edge, far_own, far_other, spread, gw)
 
     order = z_first
     left_after = [b for b in left if b != 2]
-    got = exchange(sent, 2)
-    kept, sent = fold_of(after(place, far[0], inside, outside), kept, got, left_after, order[1], piece)
-    closing = after(place, sent)
+    got = [exchange(part, 2) for part in sent_parts]
+    kept, sent = fold_of(after(place, near[0]), kept, got, left_after, order[1], piece)
+    closing = place
     left_after.remove(order[1])
     got = exchange(sent, order[1])
-    kept, sent = fold_of(place, kept, got, left_after, order[2], piece)
+    kept, sent = fold_of(place, kept, [got], left_after, order[2], piece)
     splitting = after(place, sent)
     left_after.remove(order[2])
 
     near_first, near_kept, near_send, group_near_kept, group_near_send = close_of(
-        closing, True, *near, near_own, near_other, inside, outside, spread, keep_in, send_in, piece
-    )
-    near_got = exchange(near_send, 0)
+        closing, True, *near, near_own, (near_other,), inside, outside, spread, keep_in, send_in, piece
+    )
+    near_got = exchange(after(near_send, sent), 0)
     group_near_got = exchange(group_near_send, 0)
     far_first, far_kept, far_send, group_far_kept, group_far_send = close_of(
         closing, False, *far, far_own, far_other, inside, outside, spread, keep_in, send_in, piece
@@ -611,7 +627,7 @@
         place, two_kept, two_sent, x_first, [b for b in left if b != 1], piece, {0: (input_grad,)}
     )
     *one, _ = summed_up(
-        place, one_kept, one_sent, z_first, [b for b in left if b != 2], piece, {0: (third_sent,), len(z_first) - 2: (two_sent[-1],)}
+        place, one_kept, one_sent, z_first, [b for b in left if b != 2], piece, {len(z_first) - 2: (two_sent[-1],)}
     )
     first_wgrad, group_wgrad = last_of(place, normalizer, *one, *two, channels, TAPS * gw)
     return (input_grad.reshape(outer_grad.shape), third_wgrad, group_wgrad, first_wgrad)

time: 77.5 us -> 76.5 us (0.987)
  starting transfers between devices: 30.7 us -> 21.3 us
  waiting for transfers between devices: 16.7 us -> 25.1 us
    ppermute x20 -> x21, starting transfers between devices: 29.9 us -> 20.5 us  [exchange(): lax.ppermute(array, 'space', [(i, i ^ 1 << bit) for i in range(count)])]
    ppermute x20 -> x21, waiting for transfers between devices: 16.7 us -> 25.1 us  [exchange(): lax.ppermute(array, 'space', [(i, i ^ 1 << bit) for i in range(count)])]
  transfers between devices with their start and end apart: 21 -> 22, of which waited for: 7 -> 12; matrix products, arithmetic and copies ran while one was open for 1% -> 1% of each run, Pallas kernels for 26% -> 29%
where the time goes in v4:
time: 76.5 us; the launch traced here: 76.4 us
  Pallas kernels  28.3 us (37%)
  waiting for transfers between devices  25.1 us (33%)
  starting transfers between devices  21.3 us (28%)
  between operations  0.85 us (1%)
    pallas_call x17, Pallas kernels, call(): pl.pallas_call(kernel, in_specs=specs, out_specs=[pl.BlockSpec(memory_spa...  25.6 us
    ppermute x21, waiting for transfers between devices, exchange(): lax.ppermute(array, 'space', [(i, i ^ 1 << bit) for i in range(count)])  25.1 us
    ppermute x21, starting transfers between devices, exchange(): lax.ppermute(array, 'space', [(i, i ^ 1 << bit) for i in range(count)])  20.5 us
    pallas_call x1, Pallas kernels, result_of(): pl.pallas_call(result_kernel, in_specs=[pl.BlockSpec(memory_space=pltpu.S...  2.7 us
  transfers between devices with their start and end apart: 22, of which 12 were waited for; matrix products, arithmetic and copies ran while one was open for 1% of the time, Pallas kernels for 29%

profile of v4, /device:TPU:0, one launch (start us, length us, event | category | flops | bytes accessed | tf_op | source)
XLA Modules:
  0.0 76.4 jit_solution(3563687816042248406)
XLA Ops:
  0.6 3.5 %front.1 = (f32[512,1024]{1,0:T(8,128)S(1)}, bf16[512,1024]{1,0:T(8,128)(2,1)S(1)}, bf16[512,1024]{1,0:T(8,128)(2,1)S(1)}, bf16[512,1024]{1,0:T(8,128)(2,1)S(1)}...) custom-call(s32[4]{0:T(128)S(1)} %shift-right-arithmetic_and_fusion., ...), custom_call_target="tpu_custom_call" | custom-call | tf_op jit(solution)/shard_map/front/pallas_call | solution.py:45
  4.7 2.6 %collective-permute-start.5 = (bf16[2,4,128,256]{3,2,1,0:T(8,128)(2,1)S(1)}, bf16[2,4,128,256]{3,2,1,0:T(8,128)(2,1)S(1)}, u32[]{:S(2)}, u32[]{:S(2)}) collective-permute-start(bf16[2,4,128,256]{3,2,1,0:T(8,128)(2,1)S(1)} %get-tuple-element.81), channel_id=1, source_target_pairs={{0,2},{1,3},{2,0},{3,1},{4,6},{5,7},{6,4},{7,5},{8,10},{9,11},{10,... | collective-permute-start | bytes 1572872 | tf_op jit(solution)/shard_map/ppermute | solution.py:18
  7.4 0.8 %fold.7 = (f32[2,128,1024]{2,1,0:T(8,128)S(1)}, bf16[1,128,1024]{2,1,0:T(8,128)(2,1)S(1)}, bf16[1,128,1024]{2,1,0:T(8,128)(2,1)S(1)}) custom-call(s32[4]{0:T(128)S(1)} %shift-right-arithmetic_and_fusion.refs_0_.place_ref, f32[2,2,128,1024]{3,2,1,0:T(8,128)S(1)} %bitcast.28, bf16[4,128,1024]{2,1,0:T(8,128)(2,1)S(1)} %bitcast.31), custom_call_target="tpu_custom_call" | custom-call | tf_op jit(solution)/shard_map/fold/pallas_call | solution.py:45
  8.2 2.6 %collective-permute-start.9 = (bf16[1,128,1024]{2,1,0:T(8,128)(2,1)S(1)}, bf16[1,128,1024]{2,1,0:T(8,128)(2,1)S(1)}, u32[]{:S(2)}, u32[]{:S(2)}) collective-permute-start(bf16[1,128,1024]{2,1,0:T(8,128)(2,1)S(1)} %get-tuple-element.86), channel_id=1, source_target_pairs={{0,4},{1,5},{2,6},{3,7},{4,0},{5,1},{6,2},{7,3},{8,12},{9,13},{10,... | collective-permute-start | bytes 786440 | tf_op jit(solution)/shard_map/ppermute | solution.py:18
  10.9 1.2 %collective-permute-done.1.edge_ref = bf16[16,1024]{1,0:T(8,128)(2,1)S(1)} collective-permute-done((bf16[16,1024]{1,0:T(8,128)(2,1)S(1)}, bf16[16,1024]{1,0:T(8,128)(2,1)S(1)}, u32[]{:S(2)}, u32[]{:S(2)}) %collective-permute-start.1) | collective-permute-done | bytes 32800 | tf_op jit(solution)/shard_map/ppermute | solution.py:18
  12.1 2.4 %inner.1 = (bf16[512,1024]{1,0:T(8,128)(2,1)S(1)}, bf16[16,1024]{1,0:T(8,128)(2,1)S(1)}, bf16[144,1024]{1,0:T(8,128)(2,1)S(1)}, bf16[144,1024]{1,0:T(8,128)(2,1)S(1)}) custom-call(s32[4]{0:T(128)S(1)} %shift-right-arithmetic_and_fusion.refs_0_.place_ref, bf16[512,1024]{1,0:T(8,128)(2,1)S(1)} %get-tuple-element.64.grad_ref, ...), custom_call_target="tpu_custom_call" | custom-call | tf_op jit(solution)/shard_map/inner/pallas_call | solution.py:45
  14.6 1.9 %collective-permute-start.3 = (bf16[144,1024]{1,0:T(8,128)(2,1)S(1)}, bf16[144,1024]{1,0:T(8,128)(2,1)S(1)}, u32[]{:S(2)}, u32[]{:S(2)}) collective-permute-start(bf16[144,1024]{1,0:T(8,128)(2,1)S(1)} %get-tuple-element.75), channel_id=1, source_target_pairs={{0,2},{1,3},{2,0},{3,1},{4,6},{5,7},{6,4},{7,5},{8,10},{9,11},{10,... | collective-permute-start | bytes 884744 | tf_op jit(solution)/shard_map/ppermute | solution.py:18
  16.5 2.0 %ready.1 = (bf16[4,3,768,256]{3,2,1,0:T(8,128)(2,1)S(1)}, bf16[512,512]{1,0:T(8,128)(2,1)S(1)}, bf16[512,512]{1,0:T(8,128)(2,1)S(1)}) custom-call(s32[4]{0:T(128)S(1)} %shift-right-arithmetic_and_fusion.refs_0_.place_ref, bf16[288,1024]{1,0:T(8,128)(2,1)S(1)} %bitcast.33, bf16[512,1024]{1,0:T(8,128)(2,1)S(1)} %bitcast.29), custom_call_target="tpu_custom_call" | custom-call | tf_op jit(solution)/shard_map/ready/pallas_call | solution.py:45
  18.5 0.9 %collective-permute-start.4 = (bf16[144,1024]{1,0:T(8,128)(2,1)S(1)}, bf16[144,1024]{1,0:T(8,128)(2,1)S(1)}, u32[]{:S(2)}, u32[]{:S(2)}) collective-permute-start(bf16[144,1024]{1,0:T(8,128)(2,1)S(1)} %get-tuple-element.76), channel_id=1, source_target_pairs={{2,4},{4,2},{3,5},{5,3},{6,8},{8,6},{7,9},{9,7},{10,12},{12,10},{1... | collective-permute-start | bytes 884744 | tf_op jit(solution)/shard_map/ppermute | solution.py:28
  19.4 3.0 %body_near.1 = (f32[2,512,256]{2,1,0:T(8,128)S(1)}, f32[2,288,256]{2,1,0:T(8,128)S(1)}) custom-call(s32[4]{0:T(128)S(1)} %shift-right-arithmetic_and_fusion.refs_0_.place_ref, bf16[512,1024]{1,0:T(8,128)(2,1)S(1)} %get-tuple-element.68.refs_1_, bf16[16,1024]{1,0:T(8,128)(2,1)S(1)} %get-tuple-element.69.refs_2_, ...), custom_call_target="tpu_custom_call" | custom-call | tf_op jit(solution)/shard_map/body_near/pallas_call | solution.py:45
  22.4 0.9 %collective-permute-done.8.refs_2_ = bf16[1,128,1024]{2,1,0:T(8,128)(2,1)S(1)} collective-permute-done((bf16[1,128,1024]{2,1,0:T(8,128)(2,1)S(1)}, bf16[1,128,1024]{2,1,0:T(8,128)(2,1)S(1)}, u32[]{:S(2)}, u32[]{:S(2)}) %collective-permute-start.8) | collective-permute-done | bytes 262176 | tf_op jit(solution)/shard_map/ppermute | solution.py:18
  23.3 0.7 fold.8
  23.9 3.4 %collective-permute-start.10 = (bf16[1,128,1024]{2,1,0:T(8,128)(2,1)S(1)}, bf16[1,128,1024]{2,1,0:T(8,128)(2,1)S(1)}, u32[]{:S(2)}, u32[]{:S(2)}) collective-permute-start(bf16[1,128,1024]{2,1,0:T(8,128)(2,1)S(1)} %get-tuple-element.88), channel_id=1, source_target_pairs={{0,8},{1,9},{2,10},{3,11},{4,12},{5,13},{6,14},{7,15},{8,0},{9,1},... | collective-permute-start | bytes 786440 | tf_op jit(solution)/shard_map/ppermute | solution.py:18
  28.0 0.8 %collective-permute-done.7.refs_6_.refs_10_ = bf16[2,128,256]{2,1,0:T(8,128)(2,1)S(1)} collective-permute-done((bf16[2,128,256]{2,1,0:T(8,128)(2,1)S(1)}, bf16[2,128,256]{2,1,0:T(8,128)(2,1)S(1)}, u32[]{:S(2)}, u32[]{:S(2)}) %collective-permute-start.7) | collective-permute-done | bytes 131104 | tf_op jit(solution)/shard_map/ppermute | solution.py:18
  29.0 3.0 %body_far.1 = (f32[2,512,256]{2,1,0:T(8,128)S(1)}, f32[2,288,256]{2,1,0:T(8,128)S(1)}) custom-call(s32[4]{0:T(128)S(1)} %shift-right-arithmetic_and_fusion.refs_0_.place_ref, bf16[512,1024]{1,0:T(8,128)(2,1)S(1)} %get-tuple-element.68.refs_1_, bf16[16,1024]{1,0:T(8,128)(2,1)S(1)} %get-tuple-element.69.refs_2_, ...), custom_call_target="tpu_custom_call" | custom-call | tf_op jit(solution)/shard_map/body_far/pallas_call | solution.py:45
  32.0 2.1 %close_far.1 = (bf16[512,512]{1,0:T(8,128)(2,1)S(1)}, f32[512,512]{1,0:T(8,128)S(1)}, bf16[512,512]{1,0:T(8,128)(2,1)S(1)}, f32[256,288]{1,0:T(8,128)S(1)}, bf16[256,288]{1,0:T(8,128)(2,1)S(1)}) custom-call(s32[4]{0:T(128)S(1)} %shift-right-arithmetic_and_fusion.refs_0_.place_ref, f32[2,512,256]{2,1,0:T(8,128)S(1)} %get-tuple-element.82.refs_1_, ...), custom_call_target="tpu_custom_call" | custom-call | tf_op jit(solution)/shard_map/close_far/pallas_call | solution.py:45
  34.5 2.0 %close_near.1 = (bf16[512,512]{1,0:T(8,128)(2,1)S(1)}, f32[512,512]{1,0:T(8,128)S(1)}, bf16[512,512]{1,0:T(8,128)(2,1)S(1)}, f32[256,288]{1,0:T(8,128)S(1)}, bf16[256,288]{1,0:T(8,128)(2,1)S(1)}) custom-call(s32[4]{0:T(128)S(1)} %shift-right-arithmetic_and_fusion.refs_0_.place_ref, f32[2,512,256]{2,1,0:T(8,128)S(1)} %get-tuple-element.73.refs_1_, ...), custom_call_target="tpu_custom_call" | custom-call | tf_op jit(solution)/shard_map/close_near/pallas_call | solution.py:45
  36.5 5.0 %collective-permute-done.10 = bf16[1,128,1024]{2,1,0:T(8,128)(2,1)S(1)} collective-permute-done((bf16[1,128,1024]{2,1,0:T(8,128)(2,1)S(1)}, bf16[1,128,1024]{2,1,0:T(8,128)(2,1)S(1)}, u32[]{:S(2)}, u32[]{:S(2)}) %collective-permute-start.10) | collective-permute-done | bytes 262176 | tf_op jit(solution)/shard_map/ppermute | solution.py:18
  42.2 1.9 %collective-permute-done.12.refs_3_ = bf16[512,512]{1,0:T(8,128)(2,1)S(1)} collective-permute-done((bf16[512,512]{1,0:T(8,128)(2,1)S(1)}, bf16[512,512]{1,0:T(8,128)(2,1)S(1)}, u32[]{:S(2)}, u32[]{:S(2)}) %collective-permute-start.12) | collective-permute-done | bytes 524320 | tf_op jit(solution)/shard_map/ppermute | solution.py:18
  44.1 0.9 %split.1 = (f32[2,128,896]{2,1,0:T(8,128)S(1)}, bf16[2,128,896]{2,1,0:T(8,128)(2,1)S(1)}) custom-call(s32[4]{0:T(128)S(1)} %shift-right-arithmetic_and_fusion.refs_0_.place_ref, f32[512,512]{1,0:T(8,128)S(1)} %get-tuple-element.92.refs_1_, f32[512,512]{1,0:T(8,128)S(1)} %get-tuple-element.93.refs_2_, bf16[512,512]{1,0:T(8,128)(2,1)S(1)} %collective-permute-done.12.refs_3_, ...), custom_call_target="tpu_custom_call" | custom-call | tf_op jit(solution)/shard_map/split/pallas_call | solution.py:45
  45.9 0.9 %collective-permute-done.17.refs_8_ = bf16[256,288]{1,0:T(8,128)(2,1)S(1)} collective-permute-done((bf16[256,288]{1,0:T(8,128)(2,1)S(1)}, bf16[256,288]{1,0:T(8,128)(2,1)S(1)}, u32[]{:S(2)}, u32[]{:S(2)}) %collective-permute-start.17) | collective-permute-done | bytes 147488 | tf_op jit(solution)/shard_map/ppermute | solution.py:18
  47.1 0.8 %split_group.1 = (f32[2,128,416]{2,1,0:T(8,128)S(1)}, bf16[2,128,416]{2,1,0:T(8,128)(2,1)S(1)}) custom-call(s32[4]{0:T(128)S(1)} %shift-right-arithmetic_and_fusion.refs_0_.place_ref, f32[512,512]{1,0:T(8,128)S(1)} %get-tuple-element.92.refs_1_, f32[512,512]{1,0:T(8,128)S(1)} %get-tuple-element.93.refs_2_, ...), custom_call_target="tpu_custom_call" | custom-call | tf_op jit(solution)/shard_map/split_group/pallas_call | solution.py:45
  47.9 0.9 %collective-permute-start.18 = (bf16[2,128,416]{2,1,0:T(8,128)(2,1)S(1)}, bf16[2,128,416]{2,1,0:T(8,128)(2,1)S(1)}, u32[]{:S(2)}, u32[]{:S(2)}) collective-permute-start(bf16[2,128,416]{2,1,0:T(8,128)(2,1)S(1)} %get-tuple-element.108), channel_id=1, source_target_pairs={{0,4},{1,5},{2,6},{3,7},{4,0},{5,1},{6,2},{7,3},{8,12},{9,13},{10,... | collective-permute-start | bytes 638984 | tf_op jit(solution)/shard_map/ppermute | solution.py:18
  48.8 2.7 %result.1 = bf16[512,1024]{1,0:T(8,128)(2,1)} custom-call(s32[4]{0:T(128)S(1)} %shift-right-arithmetic_and_fusion.refs_0_.place_ref, bf16[512,512]{1,0:T(8,128)(2,1)S(1)} %get-tuple-element.79.near_ref, bf16[512,512]{1,0:T(8,128)(2,1)S(1)} %get-tuple-element.84.far_ref, bf16[512,1024]{1,0:T(8,128)(2,1)S(1)} %get-tuple-element.64.grad_ref, ...), custom_call_target="tpu_custom_call" | custom-call | tf_op jit(solution)/shard_map/result/pallas_call | solution.py:536
  51.6 6.1 %collective-permute-done.14 = bf16[2,128,896]{2,1,0:T(8,128)(2,1)S(1)} collective-permute-done((bf16[2,128,896]{2,1,0:T(8,128)(2,1)S(1)}, bf16[2,128,896]{2,1,0:T(8,128)(2,1)S(1)}, u32[]{:S(2)}, u32[]{:S(2)}) %collective-permute-start.14) | collective-permute-done | bytes 458784 | tf_op jit(solution)/shard_map/ppermute | solution.py:18
  58.4 1.1 %collective-permute-start.11 = (bf16[1,64,1024]{2,1,0:T(8,128)(2,1)S(1)}, bf16[1,64,1024]{2,1,0:T(8,128)(2,1)S(1)}, u32[]{:S(2)}, u32[]{:S(2)}) collective-permute-start(bf16[1,64,1024]{2,1,0:T(8,128)(2,1)S(1)} %get-tuple-element.90), channel_id=1, source_target_pairs={{0,2},{1,3},{2,0},{3,1},{4,6},{5,7},{6,4},{7,5},{8,10},{9,11},{10,... | collective-permute-start | bytes 393224 | tf_op jit(solution)/shard_map/ppermute | solution.py:18
  60.1 3.4 %collective-permute-start.19 = (bf16[1,128,416]{2,1,0:T(8,128)(2,1)S(1)}, bf16[1,128,416]{2,1,0:T(8,128)(2,1)S(1)}, u32[]{:S(2)}, u32[]{:S(2)}) collective-permute-start(bf16[1,128,416]{2,1,0:T(8,128)(2,1)S(1)} %get-tuple-element.110), channel_id=1, source_target_pairs={{0,8},{1,9},{2,10},{3,11},{4,12},{5,13},{6,14},{7,15},{8,0},{9,1},... | collective-permute-start | bytes 319496 | tf_op jit(solution)/shard_map/ppermute | solution.py:18
  63.6 4.4 %collective-permute-done.15.refs_2_ = bf16[2,64,896]{2,1,0:T(8,128)(2,1)S(1)} collective-permute-done((bf16[2,64,896]{2,1,0:T(8,128)(2,1)S(1)}, bf16[2,64,896]{2,1,0:T(8,128)(2,1)S(1)}, u32[]{:S(2)}, u32[]{:S(2)}) %collective-permute-start.15) | collective-permute-done | bytes 229408 | tf_op jit(solution)/shard_map/ppermute | solution.py:18
  68.6 1.4 %collective-permute-start.21 = (bf16[1,64,896]{2,1,0:T(8,128)(2,1)S(1)}, bf16[1,64,896]{2,1,0:T(8,128)(2,1)S(1)}, u32[]{:S(2)}, u32[]{:S(2)}) collective-permute-start(bf16[1,64,896]{2,1,0:T(8,128)(2,1)S(1)} %get-tuple-element.101), channel_id=1, source_target_pairs={{0,8},{1,9},{2,10},{3,11},{4,12},{5,13},{6,14},{7,15},{8,0},{9,1},... | collective-permute-start | bytes 344072 | tf_op jit(solution)/shard_map/ppermute | solution.py:18
  70.9 0.7 multiply_bitcast_fusion
  71.7 3.2 %collective-permute-done.20 = bf16[1,64,416]{2,1,0:T(8,128)(2,1)S(1)} collective-permute-done((bf16[1,64,416]{2,1,0:T(8,128)(2,1)S(1)}, bf16[1,64,416]{2,1,0:T(8,128)(2,1)S(1)}, u32[]{:S(2)}, u32[]{:S(2)}) %collective-permute-start.20) | collective-permute-done | bytes 53280 | tf_op jit(solution)/shard_map/ppermute | solution.py:18
  75.0 1.3 %last.1 = (f32[64,1024]{1,0:T(8,128)}, f32[64,288]{1,0:T(8,128)}) custom-call(s32[4]{0:T(128)S(1)} %shift-right-arithmetic_and_fusion.refs_0_.place_ref, f32[64,416]{1,0:T(8,128)S(1)} %bitcast.41, bf16[64,416]{1,0:T(8,128)(2,1)S(1)} %bitcast.44, f32[64,896]{1,0:T(8,128)S(1)} %bitcast.40, bf16[64,896]{1,0:T(8,128)(2,1)S(1)} %bitcast.43), custom_call_target="tpu_custom_call" | custom-call | tf_op jit(solution)/shard_map/last/pallas_call | solution.py:45
  (40 shorter events, 6.9 us)
Async XLA Ops:
  4.2 3.3 %collective-permute-start = (bf16[512,1024]{1,0:T(8,128)(2,1)S(1)}, bf16[512,1024]{1,0:T(8,128)(2,1)S(1)}, u32[]{:S(2)}, u32[]{:S(2)}) collective-permute-start(bf16[512,1024]{1,0:T(8,128)(2,1)S(1)} %get-tuple-element.61), channel_id=1, source_target_pairs={{0,1},{1,0},{2,3},{3,2},{4,5},{5,4},{6,7},{7,6},{8,9},{9,8},{10,11... | collective-permute-start | bytes 3145736 | tf_op jit(solution)/shard_map/ppermute | solution.py:18
  4.7 22.7 %collective-permute-start.5 = (bf16[2,4,128,256]{3,2,1,0:T(8,128)(2,1)S(1)}, bf16[2,4,128,256]{3,2,1,0:T(8,128)(2,1)S(1)}, u32[]{:S(2)}, u32[]{:S(2)}) collective-permute-start(bf16[2,4,128,256]{3,2,1,0:T(8,128)(2,1)S(1)} %get-tuple-element.81), channel_id=1, source_target_pairs={{0,2},{1,3},{2,0},{3,1},{4,6},{5,7},{6,4},{7,5},{8,10},{9,11},{10,... | collective-permute-start | bytes 1572872 | tf_op jit(solution)/shard_map/ppermute | solution.py:18
  7.3 11.2 %collective-permute-start.2 = (bf16[4,128,256]{2,1,0:T(8,128)(2,1)S(1)}, bf16[4,128,256]{2,1,0:T(8,128)(2,1)S(1)}, u32[]{:S(2)}, u32[]{:S(2)}) collective-permute-start(bf16[4,128,256]{2,1,0:T(8,128)(2,1)S(1)} %get-tuple-element.72), channel_id=1, source_target_pairs={{0,1},{1,0},{2,3},{3,2},{4,5},{5,4},{6,7},{7,6},{8,9},{9,8},{10,11... | collective-permute-start | bytes 786440 | tf_op jit(solution)/shard_map/ppermute | solution.py:18
  8.2 14.1 %collective-permute-start.9 = (bf16[1,128,1024]{2,1,0:T(8,128)(2,1)S(1)}, bf16[1,128,1024]{2,1,0:T(8,128)(2,1)S(1)}, u32[]{:S(2)}, u32[]{:S(2)}) collective-permute-start(bf16[1,128,1024]{2,1,0:T(8,128)(2,1)S(1)} %get-tuple-element.86), channel_id=1, source_target_pairs={{0,4},{1,5},{2,6},{3,7},{4,0},{5,1},{6,2},{7,3},{8,12},{9,13},{10,... | collective-permute-start | bytes 786440 | tf_op jit(solution)/shard_map/ppermute | solution.py:18
  10.8 12.5 %collective-permute-start.8 = (bf16[1,128,1024]{2,1,0:T(8,128)(2,1)S(1)}, bf16[1,128,1024]{2,1,0:T(8,128)(2,1)S(1)}, u32[]{:S(2)}, u32[]{:S(2)}) collective-permute-start(bf16[1,128,1024]{2,1,0:T(8,128)(2,1)S(1)} %get-tuple-element.62), channel_id=1, source_target_pairs={{0,4},{1,5},{2,6},{3,7},{4,0},{5,1},{6,2},{7,3},{8,12},{9,13},{10,... | collective-permute-start | bytes 786440 | tf_op jit(solution)/shard_map/ppermute | solution.py:18
  10.9 1.2 %collective-permute-start.1 = (bf16[16,1024]{1,0:T(8,128)(2,1)S(1)}, bf16[16,1024]{1,0:T(8,128)(2,1)S(1)}, u32[]{:S(2)}, u32[]{:S(2)}) collective-permute-start(bf16[16,1024]{1,0:T(8,128)(2,1)S(1)} %get-tuple-element.67), channel_id=1, source_target_pairs={{0,1},{1,0},{2,3},{3,2},{4,5},{5,4},{6,7},{7,6},{8,9},{9,8},{10,11... | collective-permute-start | bytes 98312 | tf_op jit(solution)/shard_map/ppermute | solution.py:18
  12.1 4.4 %copy-start.1 = (bf16[1,4,128,1024]{3,2,1,0:T(8,128)(2,1)S(1)}, bf16[1,4,128,1024]{3,2,1,0:T(8,128)(2,1)}, u32[]{:S(2)}) copy-start(bf16[1,4,128,1024]{3,2,1,0:T(8,128)(2,1)} %param.8) | copy-start | bytes 3145732
  12.1 4.4 %copy-start.2 = (bf16[1024,288]{0,1:T(8,128)(2,1)S(1)}, bf16[1024,288]{0,1:T(8,128)(2,1)}, u32[]{:S(2)}) copy-start(bf16[1024,288]{0,1:T(8,128)(2,1)} %param.12) | copy-start | bytes 1769476
  14.6 17.5 %collective-permute-start.3 = (bf16[144,1024]{1,0:T(8,128)(2,1)S(1)}, bf16[144,1024]{1,0:T(8,128)(2,1)S(1)}, u32[]{:S(2)}, u32[]{:S(2)}) collective-permute-start(bf16[144,1024]{1,0:T(8,128)(2,1)S(1)} %get-tuple-element.75), channel_id=1, source_target_pairs={{0,2},{1,3},{2,0},{3,1},{4,6},{5,7},{6,4},{7,5},{8,10},{9,11},{10,... | collective-permute-start | bytes 884744 | tf_op jit(solution)/shard_map/ppermute | solution.py:18
  18.5 13.5 %collective-permute-start.4 = (bf16[144,1024]{1,0:T(8,128)(2,1)S(1)}, bf16[144,1024]{1,0:T(8,128)(2,1)S(1)}, u32[]{:S(2)}, u32[]{:S(2)}) collective-permute-start(bf16[144,1024]{1,0:T(8,128)(2,1)S(1)} %get-tuple-element.76), channel_id=1, source_target_pairs={{2,4},{4,2},{3,5},{5,3},{6,8},{8,6},{7,9},{9,7},{10,12},{12,10},{1... | collective-permute-start | bytes 884744 | tf_op jit(solution)/shard_map/ppermute | solution.py:28
  23.9 17.5 %collective-permute-start.10 = (bf16[1,128,1024]{2,1,0:T(8,128)(2,1)S(1)}, bf16[1,128,1024]{2,1,0:T(8,128)(2,1)S(1)}, u32[]{:S(2)}, u32[]{:S(2)}) collective-permute-start(bf16[1,128,1024]{2,1,0:T(8,128)(2,1)S(1)} %get-tuple-element.88), channel_id=1, source_target_pairs={{0,8},{1,9},{2,10},{3,11},{4,12},{5,13},{6,14},{7,15},{8,0},{9,1},... | collective-permute-start | bytes 786440 | tf_op jit(solution)/shard_map/ppermute | solution.py:18
  27.4 1.4 %collective-permute-start.7 = (bf16[2,128,256]{2,1,0:T(8,128)(2,1)S(1)}, bf16[2,128,256]{2,1,0:T(8,128)(2,1)S(1)}, u32[]{:S(2)}, u32[]{:S(2)}) collective-permute-start(bf16[2,128,256]{2,1,0:T(8,128)(2,1)S(1)} %get-tuple-element.116), channel_id=1, source_target_pairs={{0,1},{1,0},{2,3},{3,2},{4,5},{5,4},{6,7},{7,6},{8,9},{9,8},{10,11... | collective-permute-start | bytes 393224 | tf_op jit(solution)/shard_map/ppermute | solution.py:18
  27.5 1.5 %collective-permute-start.6 = (bf16[2,128,256]{2,1,0:T(8,128)(2,1)S(1)}, bf16[2,128,256]{2,1,0:T(8,128)(2,1)S(1)}, u32[]{:S(2)}, u32[]{:S(2)}) collective-permute-start(bf16[2,128,256]{2,1,0:T(8,128)(2,1)S(1)} %get-tuple-element.117), channel_id=1, source_target_pairs={{0,1},{1,0},{2,3},{3,2},{4,5},{5,4},{6,7},{7,6},{8,9},{9,8},{10,11... | collective-permute-start | bytes 393224 | tf_op jit(solution)/shard_map/ppermute | solution.py:18
  34.1 8.1 %collective-permute-start.13 = (bf16[512,512]{1,0:T(8,128)(2,1)S(1)}, bf16[512,512]{1,0:T(8,128)(2,1)S(1)}, u32[]{:S(2)}, u32[]{:S(2)}) collective-permute-start(bf16[512,512]{1,0:T(8,128)(2,1)S(1)} %get-tuple-element.96), channel_id=1, source_target_pairs={{0,1},{1,0},{2,3},{3,2},{4,5},{5,4},{6,7},{7,6},{8,9},{9,8},{10,11... | collective-permute-start | bytes 1572872 | tf_op jit(solution)/shard_map/ppermute | solution.py:18
  42.1 2.0 %collective-permute-start.12 = (bf16[512,512]{1,0:T(8,128)(2,1)S(1)}, bf16[512,512]{1,0:T(8,128)(2,1)S(1)}, u32[]{:S(2)}, u32[]{:S(2)}) collective-permute-start(bf16[512,512]{1,0:T(8,128)(2,1)S(1)} %get-tuple-element.95), channel_id=1, source_target_pairs={{0,1},{1,0},{2,3},{3,2},{4,5},{5,4},{6,7},{7,6},{8,9},{9,8},{10,11... | collective-permute-start | bytes 1572872 | tf_op jit(solution)/shard_map/ppermute | solution.py:18
  45.0 12.6 %collective-permute-start.14 = (bf16[2,128,896]{2,1,0:T(8,128)(2,1)S(1)}, bf16[2,128,896]{2,1,0:T(8,128)(2,1)S(1)}, u32[]{:S(2)}, u32[]{:S(2)}) collective-permute-start(bf16[2,128,896]{2,1,0:T(8,128)(2,1)S(1)} %get-tuple-element.98), channel_id=1, source_target_pairs={{0,2},{1,3},{2,0},{3,1},{4,6},{5,7},{6,4},{7,5},{8,10},{9,11},{10,... | collective-permute-start | bytes 1376264 | tf_op jit(solution)/shard_map/ppermute | solution.py:18
  45.4 1.4 %collective-permute-start.17 = (bf16[256,288]{1,0:T(8,128)(2,1)S(1)}, bf16[256,288]{1,0:T(8,128)(2,1)S(1)}, u32[]{:S(2)}, u32[]{:S(2)}) collective-permute-start(bf16[256,288]{1,0:T(8,128)(2,1)S(1)} %get-tuple-element.106), channel_id=1, source_target_pairs={{0,1},{1,0},{2,3},{3,2},{4,5},{5,4},{6,7},{7,6},{8,9},{9,8},{10,11... | collective-permute-start | bytes 442376 | tf_op jit(solution)/shard_map/ppermute | solution.py:18
  45.4 1.7 %collective-permute-start.16 = (bf16[256,288]{1,0:T(8,128)(2,1)S(1)}, bf16[256,288]{1,0:T(8,128)(2,1)S(1)}, u32[]{:S(2)}, u32[]{:S(2)}) collective-permute-start(bf16[256,288]{1,0:T(8,128)(2,1)S(1)} %get-tuple-element.105), channel_id=1, source_target_pairs={{0,1},{1,0},{2,3},{3,2},{4,5},{5,4},{6,7},{7,6},{8,9},{9,8},{10,11... | collective-permute-start | bytes 442376 | tf_op jit(solution)/shard_map/ppermute | solution.py:18
  47.1 1.8 %copy-start = (bf16[1024,1024]{1,0:T(8,128)(2,1)S(1)}, bf16[1024,1024]{1,0:T(8,128)(2,1)}, u32[]{:S(2)}) copy-start(bf16[1024,1024]{1,0:T(8,128)(2,1)} %weight_ref.1) | copy-start | bytes 6291460
  47.9 11.6 %collective-permute-start.18 = (bf16[2,128,416]{2,1,0:T(8,128)(2,1)S(1)}, bf16[2,128,416]{2,1,0:T(8,128)(2,1)S(1)}, u32[]{:S(2)}, u32[]{:S(2)}) collective-permute-start(bf16[2,128,416]{2,1,0:T(8,128)(2,1)S(1)} %get-tuple-element.108), channel_id=1, source_target_pairs={{0,4},{1,5},{2,6},{3,7},{4,0},{5,1},{6,2},{7,3},{8,12},{9,13},{10,... | collective-permute-start | bytes 638984 | tf_op jit(solution)/shard_map/ppermute | solution.py:18
  58.3 9.7 %collective-permute-start.15 = (bf16[2,64,896]{2,1,0:T(8,128)(2,1)S(1)}, bf16[2,64,896]{2,1,0:T(8,128)(2,1)S(1)}, u32[]{:S(2)}, u32[]{:S(2)}) collective-permute-start(bf16[2,64,896]{2,1,0:T(8,128)(2,1)S(1)} %get-tuple-element.100), channel_id=1, source_target_pairs={{0,4},{1,5},{2,6},{3,7},{4,0},{5,1},{6,2},{7,3},{8,12},{9,13},{10,... | collective-permute-start | bytes 688136 | tf_op jit(solution)/shard_map/ppermute | solution.py:18
  58.4 12.5 %collective-permute-start.11 = (bf16[1,64,1024]{2,1,0:T(8,128)(2,1)S(1)}, bf16[1,64,1024]{2,1,0:T(8,128)(2,1)S(1)}, u32[]{:S(2)}, u32[]{:S(2)}) collective-permute-start(bf16[1,64,1024]{2,1,0:T(8,128)(2,1)S(1)} %get-tuple-element.90), channel_id=1, source_target_pairs={{0,2},{1,3},{2,0},{3,1},{4,6},{5,7},{6,4},{7,5},{8,10},{9,11},{10,... | collective-permute-start | bytes 393224 | tf_op jit(solution)/shard_map/ppermute | solution.py:18
  60.1 9.8 %collective-permute-start.19 = (bf16[1,128,416]{2,1,0:T(8,128)(2,1)S(1)}, bf16[1,128,416]{2,1,0:T(8,128)(2,1)S(1)}, u32[]{:S(2)}, u32[]{:S(2)}) collective-permute-start(bf16[1,128,416]{2,1,0:T(8,128)(2,1)S(1)} %get-tuple-element.110), channel_id=1, source_target_pairs={{0,8},{1,9},{2,10},{3,11},{4,12},{5,13},{6,14},{7,15},{8,0},{9,1},... | collective-permute-start | bytes 319496 | tf_op jit(solution)/shard_map/ppermute | solution.py:18
  68.6 6.4 %collective-permute-start.21 = (bf16[1,64,896]{2,1,0:T(8,128)(2,1)S(1)}, bf16[1,64,896]{2,1,0:T(8,128)(2,1)S(1)}, u32[]{:S(2)}, u32[]{:S(2)}) collective-permute-start(bf16[1,64,896]{2,1,0:T(8,128)(2,1)S(1)} %get-tuple-element.101), channel_id=1, source_target_pairs={{0,8},{1,9},{2,10},{3,11},{4,12},{5,13},{6,14},{7,15},{8,0},{9,1},... | collective-permute-start | bytes 344072 | tf_op jit(solution)/shard_map/ppermute | solution.py:18
  70.5 4.3 %collective-permute-start.20 = (bf16[1,64,416]{2,1,0:T(8,128)(2,1)S(1)}, bf16[1,64,416]{2,1,0:T(8,128)(2,1)S(1)}, u32[]{:S(2)}, u32[]{:S(2)}) collective-permute-start(bf16[1,64,416]{2,1,0:T(8,128)(2,1)S(1)} %get-tuple-element.112), channel_id=1, source_target_pairs={{0,2},{1,3},{2,0},{3,1},{4,6},{5,7},{6,4},{7,5},{8,10},{9,11},{10,... | collective-permute-start | bytes 159752 | tf_op jit(solution)/shard_map/ppermute | solution.py:18

commit v5 on v4

--- a/solution.py
+++ b/solution.py
@@ -400,22 +400,36 @@
         group_send_ref[here, :] = send.reshape(step // 2, TAPS * gw).astype(BF)
 
 
-def close_of(place, near, back, term, own, other, inside, outside, spread, keep_in, send_in, piece):
-    _, positions, shard = back.shape
-    rows = keep_in.shape[0]
-    gw = term.shape[1] // TAPS
-    return call(
-        lambda *refs: close_kernel(gw, piece, near, *refs),
-        "close_near" if near else "close_far",
-        place,
-        [back, term, inside, outside, spread, keep_in, send_in, own, *other],
-        [
-            ((positions, 2 * shard), BF),
-            ((rows, 2 * shard), F32),
-            ((rows, 2 * shard), BF),
-            ((shard, TAPS * gw), F32),
-            ((shard, TAPS * gw), BF),
-        ],
+def closes_kernel(
+    gw, piece, count, place_ref, near_back_ref, near_term_ref, far_back_ref, far_term_ref, *refs
+):
+    shared, refs = refs[:5], refs[5:]
+    slots, outs = refs[:-10], refs[-10:]
+    for near, terms, mine, results in (
+        (True, (near_back_ref, near_term_ref), slots[:count], outs[:5]),
+        (False, (far_back_ref, far_term_ref), slots[count:], outs[5:]),
+    ):
+        close_kernel(gw, piece, near, place_ref, *terms, *shared, *mine, *results)
+
+
+def closes_of(place, near, near_slots, far, far_slots, shared, piece):
+    _, positions, shard = near[0].shape
+    rows = shared[-1].shape[0]
+    taps_gw = near[1].shape[1]
+    outs = [
+        ((positions, 2 * shard), BF),
+        ((rows, 2 * shard), F32),
+        ((rows, 2 * shard), BF),
+        ((shard, taps_gw), F32),
+        ((shard, taps_gw), BF),
+    ]
+    return call(
+        lambda *refs: closes_kernel(taps_gw // TAPS, piece, len(near_slots), *refs),
+        "close",
+        place,
+        [*near, *far, *shared, *near_slots, *far_slots],
+        outs * 2,
+        megabytes=14,
     )
 
 
@@ -580,8 +594,8 @@
     inner, edge, inside, outside = inner_of(
         after(place, sent), grad_copy, weight_copy, third_copy, edge_got
     )
+    outside = exchange_across(outside)
     inside = exchange(inside, 1)
-    outside = exchange_across(outside)
 
     spread, keep_in, send_in = ready_of(
         after(place, sent), group_weight.T, input_rows, shard, gw, piece
@@ -602,14 +616,15 @@
     splitting = after(place, sent)
     left_after.remove(order[2])
 
-    near_first, near_kept, near_send, group_near_kept, group_near_send = close_of(
-        closing, True, *near, near_own, (near_other,), inside, outside, spread, keep_in, send_in, piece
+    (
+        near_first, near_kept, near_send, group_near_kept, group_near_send,
+        far_first, far_kept, far_send, group_far_kept, group_far_send,
+    ) = closes_of(
+        closing, near, (near_own, near_other), far, (far_own, *far_other),
+        (inside, outside, spread, keep_in, send_in), piece,
     )
     near_got = exchange(after(near_send, sent), 0)
     group_near_got = exchange(group_near_send, 0)
-    far_first, far_kept, far_send, group_far_kept, group_far_send = close_of(
-        closing, False, *far, far_own, far_other, inside, outside, spread, keep_in, send_in, piece
-    )
     far_got = exchange(far_send, 0)
     group_far_got = exchange(group_far_send, 0)
 

time: 76.5 us -> 76 us (level)
    pallas_call x17 -> x16, Pallas kernels: 25.6 us -> 25 us  [call(): pl.pallas_call(kernel, in_specs=specs, out_specs=[pl.BlockSpec(memory_spa...]
where the time goes in v5:
time: 76 us; the launch traced here: 75.8 us
  Pallas kernels  27.7 us (36%)
  waiting for transfers between devices  25.4 us (33%)
  starting transfers between devices  21.1 us (28%)
  between operations  0.84 us (1%)
    ppermute x21, waiting for transfers between devices, exchange(): lax.ppermute(array, 'space', [(i, i ^ 1 << bit) for i in range(count)])  25.4 us
    pallas_call x16, Pallas kernels, call(): pl.pallas_call(kernel, in_specs=specs, out_specs=[pl.BlockSpec(memory_spa...  25 us
    ppermute x21, starting transfers between devices, exchange(): lax.ppermute(array, 'space', [(i, i ^ 1 << bit) for i in range(count)])  20.3 us
    pallas_call x1, Pallas kernels, result_of(): pl.pallas_call(result_kernel, in_specs=[pl.BlockSpec(memory_space=pltpu.S...  2.7 us
  transfers between devices with their start and end apart: 22, of which 12 were waited for; matrix products, arithmetic and copies ran while one was open for 1% of the time, Pallas kernels for 29%

profile of v5, /device:TPU:0, one launch (start us, length us, event | category | flops | bytes accessed | tf_op | source)
XLA Modules:
  0.0 75.8 jit_solution(13724705536199415634)
XLA Ops:
  0.6 3.5 %front.1 = (f32[512,1024]{1,0:T(8,128)S(1)}, bf16[512,1024]{1,0:T(8,128)(2,1)S(1)}, bf16[512,1024]{1,0:T(8,128)(2,1)S(1)}, bf16[512,1024]{1,0:T(8,128)(2,1)S(1)}...) custom-call(s32[4]{0:T(128)S(1)} %shift-right-arithmetic_and_fusion., ...), custom_call_target="tpu_custom_call" | custom-call | tf_op jit(solution)/shard_map/front/pallas_call | solution.py:45
  4.7 2.6 %collective-permute-start.3 = (bf16[2,4,128,256]{3,2,1,0:T(8,128)(2,1)S(1)}, bf16[2,4,128,256]{3,2,1,0:T(8,128)(2,1)S(1)}, u32[]{:S(2)}, u32[]{:S(2)}) collective-permute-start(bf16[2,4,128,256]{3,2,1,0:T(8,128)(2,1)S(1)} %get-tuple-element.76), channel_id=1, source_target_pairs={{0,2},{1,3},{2,0},{3,1},{4,6},{5,7},{6,4},{7,5},{8,10},{9,11},{10,... | collective-permute-start | bytes 1572872 | tf_op jit(solution)/shard_map/ppermute | solution.py:18
  7.4 0.8 %fold.7 = (f32[2,128,1024]{2,1,0:T(8,128)S(1)}, bf16[1,128,1024]{2,1,0:T(8,128)(2,1)S(1)}, bf16[1,128,1024]{2,1,0:T(8,128)(2,1)S(1)}) custom-call(s32[4]{0:T(128)S(1)} %shift-right-arithmetic_and_fusion.refs_0_.place_ref, f32[2,2,128,1024]{3,2,1,0:T(8,128)S(1)} %bitcast.28, bf16[4,128,1024]{2,1,0:T(8,128)(2,1)S(1)} %bitcast.31), custom_call_target="tpu_custom_call" | custom-call | tf_op jit(solution)/shard_map/fold/pallas_call | solution.py:45
  8.2 2.6 %collective-permute-start.9 = (bf16[1,128,1024]{2,1,0:T(8,128)(2,1)S(1)}, bf16[1,128,1024]{2,1,0:T(8,128)(2,1)S(1)}, u32[]{:S(2)}, u32[]{:S(2)}) collective-permute-start(bf16[1,128,1024]{2,1,0:T(8,128)(2,1)S(1)} %get-tuple-element.86), channel_id=1, source_target_pairs={{0,4},{1,5},{2,6},{3,7},{4,0},{5,1},{6,2},{7,3},{8,12},{9,13},{10,... | collective-permute-start | bytes 786440 | tf_op jit(solution)/shard_map/ppermute | solution.py:18
  10.9 1.2 %collective-permute-done.1.edge_ref = bf16[16,1024]{1,0:T(8,128)(2,1)S(1)} collective-permute-done((bf16[16,1024]{1,0:T(8,128)(2,1)S(1)}, bf16[16,1024]{1,0:T(8,128)(2,1)S(1)}, u32[]{:S(2)}, u32[]{:S(2)}) %collective-permute-start.1) | collective-permute-done | bytes 32800 | tf_op jit(solution)/shard_map/ppermute | solution.py:18
  12.1 2.4 %inner.1 = (bf16[512,1024]{1,0:T(8,128)(2,1)S(1)}, bf16[16,1024]{1,0:T(8,128)(2,1)S(1)}, bf16[144,1024]{1,0:T(8,128)(2,1)S(1)}, bf16[144,1024]{1,0:T(8,128)(2,1)S(1)}) custom-call(s32[4]{0:T(128)S(1)} %shift-right-arithmetic_and_fusion.refs_0_.place_ref, bf16[512,1024]{1,0:T(8,128)(2,1)S(1)} %get-tuple-element.64.grad_ref, ...), custom_call_target="tpu_custom_call" | custom-call | tf_op jit(solution)/shard_map/inner/pallas_call | solution.py:45
  14.6 1.9 %collective-permute-start.6 = (bf16[144,1024]{1,0:T(8,128)(2,1)S(1)}, bf16[144,1024]{1,0:T(8,128)(2,1)S(1)}, u32[]{:S(2)}, u32[]{:S(2)}) collective-permute-start(bf16[144,1024]{1,0:T(8,128)(2,1)S(1)} %get-tuple-element.79), channel_id=1, source_target_pairs={{0,2},{1,3},{2,0},{3,1},{4,6},{5,7},{6,4},{7,5},{8,10},{9,11},{10,... | collective-permute-start | bytes 884744 | tf_op jit(solution)/shard_map/ppermute | solution.py:18
  16.5 2.0 %ready.1 = (bf16[4,3,768,256]{3,2,1,0:T(8,128)(2,1)S(1)}, bf16[512,512]{1,0:T(8,128)(2,1)S(1)}, bf16[512,512]{1,0:T(8,128)(2,1)S(1)}) custom-call(s32[4]{0:T(128)S(1)} %shift-right-arithmetic_and_fusion.refs_0_.place_ref, bf16[288,1024]{1,0:T(8,128)(2,1)S(1)} %bitcast.33, bf16[512,1024]{1,0:T(8,128)(2,1)S(1)} %bitcast.29), custom_call_target="tpu_custom_call" | custom-call | tf_op jit(solution)/shard_map/ready/pallas_call | solution.py:45
  18.5 0.9 %collective-permute-start.7 = (bf16[144,1024]{1,0:T(8,128)(2,1)S(1)}, bf16[144,1024]{1,0:T(8,128)(2,1)S(1)}, u32[]{:S(2)}, u32[]{:S(2)}) collective-permute-start(bf16[144,1024]{1,0:T(8,128)(2,1)S(1)} %get-tuple-element.80), channel_id=1, source_target_pairs={{2,4},{4,2},{3,5},{5,3},{6,8},{8,6},{7,9},{9,7},{10,12},{12,10},{1... | collective-permute-start | bytes 884744 | tf_op jit(solution)/shard_map/ppermute | solution.py:28
  19.4 3.0 %body_near.1 = (f32[2,512,256]{2,1,0:T(8,128)S(1)}, f32[2,288,256]{2,1,0:T(8,128)S(1)}) custom-call(s32[4]{0:T(128)S(1)} %shift-right-arithmetic_and_fusion.refs_0_.place_ref, bf16[512,1024]{1,0:T(8,128)(2,1)S(1)} %get-tuple-element.68.refs_1_, bf16[16,1024]{1,0:T(8,128)(2,1)S(1)} %get-tuple-element.69.refs_2_, ...), custom_call_target="tpu_custom_call" | custom-call | tf_op jit(solution)/shard_map/body_near/pallas_call | solution.py:45
  22.4 0.9 %collective-permute-done.8.refs_2_ = bf16[1,128,1024]{2,1,0:T(8,128)(2,1)S(1)} collective-permute-done((bf16[1,128,1024]{2,1,0:T(8,128)(2,1)S(1)}, bf16[1,128,1024]{2,1,0:T(8,128)(2,1)S(1)}, u32[]{:S(2)}, u32[]{:S(2)}) %collective-permute-start.8) | collective-permute-done | bytes 262176 | tf_op jit(solution)/shard_map/ppermute | solution.py:18
  23.3 0.7 fold.8
  23.9 3.4 %collective-permute-start.10 = (bf16[1,128,1024]{2,1,0:T(8,128)(2,1)S(1)}, bf16[1,128,1024]{2,1,0:T(8,128)(2,1)S(1)}, u32[]{:S(2)}, u32[]{:S(2)}) collective-permute-start(bf16[1,128,1024]{2,1,0:T(8,128)(2,1)S(1)} %get-tuple-element.88), channel_id=1, source_target_pairs={{0,8},{1,9},{2,10},{3,11},{4,12},{5,13},{6,14},{7,15},{8,0},{9,1},... | collective-permute-start | bytes 786440 | tf_op jit(solution)/shard_map/ppermute | solution.py:18
  28.0 0.8 %collective-permute-done.5.refs_6_.refs_14_ = bf16[2,128,256]{2,1,0:T(8,128)(2,1)S(1)} collective-permute-done((bf16[2,128,256]{2,1,0:T(8,128)(2,1)S(1)}, bf16[2,128,256]{2,1,0:T(8,128)(2,1)S(1)}, u32[]{:S(2)}, u32[]{:S(2)}) %collective-permute-start.5) | collective-permute-done | bytes 131104 | tf_op jit(solution)/shard_map/ppermute | solution.py:18
  29.0 3.0 %body_far.1 = (f32[2,512,256]{2,1,0:T(8,128)S(1)}, f32[2,288,256]{2,1,0:T(8,128)S(1)}) custom-call(s32[4]{0:T(128)S(1)} %shift-right-arithmetic_and_fusion.refs_0_.place_ref, bf16[512,1024]{1,0:T(8,128)(2,1)S(1)} %get-tuple-element.68.refs_1_, bf16[16,1024]{1,0:T(8,128)(2,1)S(1)} %get-tuple-element.69.refs_2_, ...), custom_call_target="tpu_custom_call" | custom-call | tf_op jit(solution)/shard_map/body_far/pallas_call | solution.py:45
  32.0 3.4 %close.1 = (bf16[512,512]{1,0:T(8,128)(2,1)S(1)}, f32[512,512]{1,0:T(8,128)S(1)}, bf16[512,512]{1,0:T(8,128)(2,1)S(1)}, f32[256,288]{1,0:T(8,128)S(1)}, bf16[256...) custom-call(s32[4]{0:T(128)S(1)} %shift-right-arithmetic_and_fusion., ...), custom_call_target="tpu_custom_call" | custom-call | tf_op jit(solution)/shard_map/close/pallas_call | solution.py:45
  35.8 5.6 %collective-permute-done.10 = bf16[1,128,1024]{2,1,0:T(8,128)(2,1)S(1)} collective-permute-done((bf16[1,128,1024]{2,1,0:T(8,128)(2,1)S(1)}, bf16[1,128,1024]{2,1,0:T(8,128)(2,1)S(1)}, u32[]{:S(2)}, u32[]{:S(2)}) %collective-permute-start.10) | collective-permute-done | bytes 262176 | tf_op jit(solution)/shard_map/ppermute | solution.py:18
  42.2 1.9 %collective-permute-done.12.refs_3_ = bf16[512,512]{1,0:T(8,128)(2,1)S(1)} collective-permute-done((bf16[512,512]{1,0:T(8,128)(2,1)S(1)}, bf16[512,512]{1,0:T(8,128)(2,1)S(1)}, u32[]{:S(2)}, u32[]{:S(2)}) %collective-permute-start.12) | collective-permute-done | bytes 524320 | tf_op jit(solution)/shard_map/ppermute | solution.py:18
  44.1 0.9 %split.1 = (f32[2,128,896]{2,1,0:T(8,128)S(1)}, bf16[2,128,896]{2,1,0:T(8,128)(2,1)S(1)}) custom-call(s32[4]{0:T(128)S(1)} %shift-right-arithmetic_and_fusion.refs_0_.place_ref, f32[512,512]{1,0:T(8,128)S(1)} %get-tuple-element.92.refs_1_, f32[512,512]{1,0:T(8,128)S(1)} %get-tuple-element.93.refs_2_, bf16[512,512]{1,0:T(8,128)(2,1)S(1)} %collective-permute-done.12.refs_3_, ...), custom_call_target="tpu_custom_call" | custom-call | tf_op jit(solution)/shard_map/split/pallas_call | solution.py:45
  45.9 0.9 %collective-permute-done.16.refs_7_ = bf16[256,288]{1,0:T(8,128)(2,1)S(1)} collective-permute-done((bf16[256,288]{1,0:T(8,128)(2,1)S(1)}, bf16[256,288]{1,0:T(8,128)(2,1)S(1)}, u32[]{:S(2)}, u32[]{:S(2)}) %collective-permute-start.16) | collective-permute-done | bytes 147488 | tf_op jit(solution)/shard_map/ppermute | solution.py:18
  47.1 0.8 %split_group.1 = (f32[2,128,416]{2,1,0:T(8,128)S(1)}, bf16[2,128,416]{2,1,0:T(8,128)(2,1)S(1)}) custom-call(s32[4]{0:T(128)S(1)} %shift-right-arithmetic_and_fusion.refs_0_.place_ref, f32[512,512]{1,0:T(8,128)S(1)} %get-tuple-element.92.refs_1_, f32[512,512]{1,0:T(8,128)S(1)} %get-tuple-element.93.refs_2_, ...), custom_call_target="tpu_custom_call" | custom-call | tf_op jit(solution)/shard_map/split_group/pallas_call | solution.py:45
  47.9 0.9 %collective-permute-start.18 = (bf16[2,128,416]{2,1,0:T(8,128)(2,1)S(1)}, bf16[2,128,416]{2,1,0:T(8,128)(2,1)S(1)}, u32[]{:S(2)}, u32[]{:S(2)}) collective-permute-start(bf16[2,128,416]{2,1,0:T(8,128)(2,1)S(1)} %get-tuple-element.108), channel_id=1, source_target_pairs={{0,4},{1,5},{2,6},{3,7},{4,0},{5,1},{6,2},{7,3},{8,12},{9,13},{10,... | collective-permute-start | bytes 638984 | tf_op jit(solution)/shard_map/ppermute | solution.py:18
  48.8 2.7 %result.1 = bf16[512,1024]{1,0:T(8,128)(2,1)} custom-call(s32[4]{0:T(128)S(1)} %shift-right-arithmetic_and_fusion.refs_0_.place_ref, bf16[512,512]{1,0:T(8,128)(2,1)S(1)} %get-tuple-element.83.near_ref, bf16[512,512]{1,0:T(8,128)(2,1)S(1)} %get-tuple-element.84.far_ref, bf16[512,1024]{1,0:T(8,128)(2,1)S(1)} %get-tuple-element.64.grad_ref, ...), custom_call_target="tpu_custom_call" | custom-call | tf_op jit(solution)/shard_map/result/pallas_call | solution.py:550
  51.6 6.1 %collective-permute-done.14 = bf16[2,128,896]{2,1,0:T(8,128)(2,1)S(1)} collective-permute-done((bf16[2,128,896]{2,1,0:T(8,128)(2,1)S(1)}, bf16[2,128,896]{2,1,0:T(8,128)(2,1)S(1)}, u32[]{:S(2)}, u32[]{:S(2)}) %collective-permute-start.14) | collective-permute-done | bytes 458784 | tf_op jit(solution)/shard_map/ppermute | solution.py:18
  58.4 1.1 %collective-permute-start.11 = (bf16[1,64,1024]{2,1,0:T(8,128)(2,1)S(1)}, bf16[1,64,1024]{2,1,0:T(8,128)(2,1)S(1)}, u32[]{:S(2)}, u32[]{:S(2)}) collective-permute-start(bf16[1,64,1024]{2,1,0:T(8,128)(2,1)S(1)} %get-tuple-element.90), channel_id=1, source_target_pairs={{0,2},{1,3},{2,0},{3,1},{4,6},{5,7},{6,4},{7,5},{8,10},{9,11},{10,... | collective-permute-start | bytes 393224 | tf_op jit(solution)/shard_map/ppermute | solution.py:18
  60.1 3.4 %collective-permute-start.19 = (bf16[1,128,416]{2,1,0:T(8,128)(2,1)S(1)}, bf16[1,128,416]{2,1,0:T(8,128)(2,1)S(1)}, u32[]{:S(2)}, u32[]{:S(2)}) collective-permute-start(bf16[1,128,416]{2,1,0:T(8,128)(2,1)S(1)} %get-tuple-element.110), channel_id=1, source_target_pairs={{0,8},{1,9},{2,10},{3,11},{4,12},{5,13},{6,14},{7,15},{8,0},{9,1},... | collective-permute-start | bytes 319496 | tf_op jit(solution)/shard_map/ppermute | solution.py:18
  63.6 4.4 %collective-permute-done.15.refs_2_ = bf16[2,64,896]{2,1,0:T(8,128)(2,1)S(1)} collective-permute-done((bf16[2,64,896]{2,1,0:T(8,128)(2,1)S(1)}, bf16[2,64,896]{2,1,0:T(8,128)(2,1)S(1)}, u32[]{:S(2)}, u32[]{:S(2)}) %collective-permute-start.15) | collective-permute-done | bytes 229408 | tf_op jit(solution)/shard_map/ppermute | solution.py:18
  68.6 0.7 collective-permute-start.21
  69.9 0.8 %collective-permute-start.20 = (bf16[1,64,416]{2,1,0:T(8,128)(2,1)S(1)}, bf16[1,64,416]{2,1,0:T(8,128)(2,1)S(1)}, u32[]{:S(2)}, u32[]{:S(2)}) collective-permute-start(bf16[1,64,416]{2,1,0:T(8,128)(2,1)S(1)} %get-tuple-element.112), channel_id=1, source_target_pairs={{0,2},{1,3},{2,0},{3,1},{4,6},{5,7},{6,4},{7,5},{8,10},{9,11},{10,... | collective-permute-start | bytes 159752 | tf_op jit(solution)/shard_map/ppermute | solution.py:18
  70.7 0.7 multiply_bitcast_fusion
  71.4 2.8 %collective-permute-done.20 = bf16[1,64,416]{2,1,0:T(8,128)(2,1)S(1)} collective-permute-done((bf16[1,64,416]{2,1,0:T(8,128)(2,1)S(1)}, bf16[1,64,416]{2,1,0:T(8,128)(2,1)S(1)}, u32[]{:S(2)}, u32[]{:S(2)}) %collective-permute-start.20) | collective-permute-done | bytes 53280 | tf_op jit(solution)/shard_map/ppermute | solution.py:18
  74.5 1.3 %last.1 = (f32[64,1024]{1,0:T(8,128)}, f32[64,288]{1,0:T(8,128)}) custom-call(s32[4]{0:T(128)S(1)} %shift-right-arithmetic_and_fusion.refs_0_.place_ref, f32[64,416]{1,0:T(8,128)S(1)} %bitcast.41, bf16[64,416]{1,0:T(8,128)(2,1)S(1)} %bitcast.44, f32[64,896]{1,0:T(8,128)S(1)} %bitcast.40, bf16[64,896]{1,0:T(8,128)(2,1)S(1)} %bitcast.43), custom_call_target="tpu_custom_call" | custom-call | tf_op jit(solution)/shard_map/last/pallas_call | solution.py:45
  (39 shorter events, 6.6 us)
Async XLA Ops:
  4.2 3.3 %collective-permute-start = (bf16[512,1024]{1,0:T(8,128)(2,1)S(1)}, bf16[512,1024]{1,0:T(8,128)(2,1)S(1)}, u32[]{:S(2)}, u32[]{:S(2)}) collective-permute-start(bf16[512,1024]{1,0:T(8,128)(2,1)S(1)} %get-tuple-element.61), channel_id=1, source_target_pairs={{0,1},{1,0},{2,3},{3,2},{4,5},{5,4},{6,7},{7,6},{8,9},{9,8},{10,11... | collective-permute-start | bytes 3145736 | tf_op jit(solution)/shard_map/ppermute | solution.py:18
  4.7 22.7 %collective-permute-start.3 = (bf16[2,4,128,256]{3,2,1,0:T(8,128)(2,1)S(1)}, bf16[2,4,128,256]{3,2,1,0:T(8,128)(2,1)S(1)}, u32[]{:S(2)}, u32[]{:S(2)}) collective-permute-start(bf16[2,4,128,256]{3,2,1,0:T(8,128)(2,1)S(1)} %get-tuple-element.76), channel_id=1, source_target_pairs={{0,2},{1,3},{2,0},{3,1},{4,6},{5,7},{6,4},{7,5},{8,10},{9,11},{10,... | collective-permute-start | bytes 1572872 | tf_op jit(solution)/shard_map/ppermute | solution.py:18
  7.3 11.2 %collective-permute-start.2 = (bf16[4,128,256]{2,1,0:T(8,128)(2,1)S(1)}, bf16[4,128,256]{2,1,0:T(8,128)(2,1)S(1)}, u32[]{:S(2)}, u32[]{:S(2)}) collective-permute-start(bf16[4,128,256]{2,1,0:T(8,128)(2,1)S(1)} %get-tuple-element.72), channel_id=1, source_target_pairs={{0,1},{1,0},{2,3},{3,2},{4,5},{5,4},{6,7},{7,6},{8,9},{9,8},{10,11... | collective-permute-start | bytes 786440 | tf_op jit(solution)/shard_map/ppermute | solution.py:18
  8.2 14.1 %collective-permute-start.9 = (bf16[1,128,1024]{2,1,0:T(8,128)(2,1)S(1)}, bf16[1,128,1024]{2,1,0:T(8,128)(2,1)S(1)}, u32[]{:S(2)}, u32[]{:S(2)}) collective-permute-start(bf16[1,128,1024]{2,1,0:T(8,128)(2,1)S(1)} %get-tuple-element.86), channel_id=1, source_target_pairs={{0,4},{1,5},{2,6},{3,7},{4,0},{5,1},{6,2},{7,3},{8,12},{9,13},{10,... | collective-permute-start | bytes 786440 | tf_op jit(solution)/shard_map/ppermute | solution.py:18
  10.8 12.5 %collective-permute-start.8 = (bf16[1,128,1024]{2,1,0:T(8,128)(2,1)S(1)}, bf16[1,128,1024]{2,1,0:T(8,128)(2,1)S(1)}, u32[]{:S(2)}, u32[]{:S(2)}) collective-permute-start(bf16[1,128,1024]{2,1,0:T(8,128)(2,1)S(1)} %get-tuple-element.62), channel_id=1, source_target_pairs={{0,4},{1,5},{2,6},{3,7},{4,0},{5,1},{6,2},{7,3},{8,12},{9,13},{10,... | collective-permute-start | bytes 786440 | tf_op jit(solution)/shard_map/ppermute | solution.py:18
  10.9 1.2 %collective-permute-start.1 = (bf16[16,1024]{1,0:T(8,128)(2,1)S(1)}, bf16[16,1024]{1,0:T(8,128)(2,1)S(1)}, u32[]{:S(2)}, u32[]{:S(2)}) collective-permute-start(bf16[16,1024]{1,0:T(8,128)(2,1)S(1)} %get-tuple-element.67), channel_id=1, source_target_pairs={{0,1},{1,0},{2,3},{3,2},{4,5},{5,4},{6,7},{7,6},{8,9},{9,8},{10,11... | collective-permute-start | bytes 98312 | tf_op jit(solution)/shard_map/ppermute | solution.py:18
  12.1 4.4 %copy-start.1 = (bf16[1,4,128,1024]{3,2,1,0:T(8,128)(2,1)S(1)}, bf16[1,4,128,1024]{3,2,1,0:T(8,128)(2,1)}, u32[]{:S(2)}) copy-start(bf16[1,4,128,1024]{3,2,1,0:T(8,128)(2,1)} %param.8) | copy-start | bytes 3145732
  12.1 4.4 %copy-start.2 = (bf16[1024,288]{0,1:T(8,128)(2,1)S(1)}, bf16[1024,288]{0,1:T(8,128)(2,1)}, u32[]{:S(2)}) copy-start(bf16[1024,288]{0,1:T(8,128)(2,1)} %param.12) | copy-start | bytes 1769476
  14.6 17.5 %collective-permute-start.6 = (bf16[144,1024]{1,0:T(8,128)(2,1)S(1)}, bf16[144,1024]{1,0:T(8,128)(2,1)S(1)}, u32[]{:S(2)}, u32[]{:S(2)}) collective-permute-start(bf16[144,1024]{1,0:T(8,128)(2,1)S(1)} %get-tuple-element.79), channel_id=1, source_target_pairs={{0,2},{1,3},{2,0},{3,1},{4,6},{5,7},{6,4},{7,5},{8,10},{9,11},{10,... | collective-permute-start | bytes 884744 | tf_op jit(solution)/shard_map/ppermute | solution.py:18
  18.5 13.5 %collective-permute-start.7 = (bf16[144,1024]{1,0:T(8,128)(2,1)S(1)}, bf16[144,1024]{1,0:T(8,128)(2,1)S(1)}, u32[]{:S(2)}, u32[]{:S(2)}) collective-permute-start(bf16[144,1024]{1,0:T(8,128)(2,1)S(1)} %get-tuple-element.80), channel_id=1, source_target_pairs={{2,4},{4,2},{3,5},{5,3},{6,8},{8,6},{7,9},{9,7},{10,12},{12,10},{1... | collective-permute-start | bytes 884744 | tf_op jit(solution)/shard_map/ppermute | solution.py:28
  23.9 17.5 %collective-permute-start.10 = (bf16[1,128,1024]{2,1,0:T(8,128)(2,1)S(1)}, bf16[1,128,1024]{2,1,0:T(8,128)(2,1)S(1)}, u32[]{:S(2)}, u32[]{:S(2)}) collective-permute-start(bf16[1,128,1024]{2,1,0:T(8,128)(2,1)S(1)} %get-tuple-element.88), channel_id=1, source_target_pairs={{0,8},{1,9},{2,10},{3,11},{4,12},{5,13},{6,14},{7,15},{8,0},{9,1},... | collective-permute-start | bytes 786440 | tf_op jit(solution)/shard_map/ppermute | solution.py:18
  27.4 1.4 %collective-permute-start.5 = (bf16[2,128,256]{2,1,0:T(8,128)(2,1)S(1)}, bf16[2,128,256]{2,1,0:T(8,128)(2,1)S(1)}, u32[]{:S(2)}, u32[]{:S(2)}) collective-permute-start(bf16[2,128,256]{2,1,0:T(8,128)(2,1)S(1)} %get-tuple-element.116), channel_id=1, source_target_pairs={{0,1},{1,0},{2,3},{3,2},{4,5},{5,4},{6,7},{7,6},{8,9},{9,8},{10,11... | collective-permute-start | bytes 393224 | tf_op jit(solution)/shard_map/ppermute | solution.py:18
  27.5 1.5 %collective-permute-start.4 = (bf16[2,128,256]{2,1,0:T(8,128)(2,1)S(1)}, bf16[2,128,256]{2,1,0:T(8,128)(2,1)S(1)}, u32[]{:S(2)}, u32[]{:S(2)}) collective-permute-start(bf16[2,128,256]{2,1,0:T(8,128)(2,1)S(1)} %get-tuple-element.117), channel_id=1, source_target_pairs={{0,1},{1,0},{2,3},{3,2},{4,5},{5,4},{6,7},{7,6},{8,9},{9,8},{10,11... | collective-permute-start | bytes 393224 | tf_op jit(solution)/shard_map/ppermute | solution.py:18
  35.4 6.7 %collective-permute-start.13 = (bf16[512,512]{1,0:T(8,128)(2,1)S(1)}, bf16[512,512]{1,0:T(8,128)(2,1)S(1)}, u32[]{:S(2)}, u32[]{:S(2)}) collective-permute-start(bf16[512,512]{1,0:T(8,128)(2,1)S(1)} %get-tuple-element.96), channel_id=1, source_target_pairs={{0,1},{1,0},{2,3},{3,2},{4,5},{5,4},{6,7},{7,6},{8,9},{9,8},{10,11... | collective-permute-start | bytes 1572872 | tf_op jit(solution)/shard_map/ppermute | solution.py:18
  42.1 2.0 %collective-permute-start.12 = (bf16[512,512]{1,0:T(8,128)(2,1)S(1)}, bf16[512,512]{1,0:T(8,128)(2,1)S(1)}, u32[]{:S(2)}, u32[]{:S(2)}) collective-permute-start(bf16[512,512]{1,0:T(8,128)(2,1)S(1)} %get-tuple-element.95), channel_id=1, source_target_pairs={{0,1},{1,0},{2,3},{3,2},{4,5},{5,4},{6,7},{7,6},{8,9},{9,8},{10,11... | collective-permute-start | bytes 1572872 | tf_op jit(solution)/shard_map/ppermute | solution.py:18
  45.0 12.6 %collective-permute-start.14 = (bf16[2,128,896]{2,1,0:T(8,128)(2,1)S(1)}, bf16[2,128,896]{2,1,0:T(8,128)(2,1)S(1)}, u32[]{:S(2)}, u32[]{:S(2)}) collective-permute-start(bf16[2,128,896]{2,1,0:T(8,128)(2,1)S(1)} %get-tuple-element.98), channel_id=1, source_target_pairs={{0,2},{1,3},{2,0},{3,1},{4,6},{5,7},{6,4},{7,5},{8,10},{9,11},{10,... | collective-permute-start | bytes 1376264 | tf_op jit(solution)/shard_map/ppermute | solution.py:18
  45.4 1.4 %collective-permute-start.16 = (bf16[256,288]{1,0:T(8,128)(2,1)S(1)}, bf16[256,288]{1,0:T(8,128)(2,1)S(1)}, u32[]{:S(2)}, u32[]{:S(2)}) collective-permute-start(bf16[256,288]{1,0:T(8,128)(2,1)S(1)} %get-tuple-element.105), channel_id=1, source_target_pairs={{0,1},{1,0},{2,3},{3,2},{4,5},{5,4},{6,7},{7,6},{8,9},{9,8},{10,11... | collective-permute-start | bytes 442376 | tf_op jit(solution)/shard_map/ppermute | solution.py:18
  45.4 1.7 %collective-permute-start.17 = (bf16[256,288]{1,0:T(8,128)(2,1)S(1)}, bf16[256,288]{1,0:T(8,128)(2,1)S(1)}, u32[]{:S(2)}, u32[]{:S(2)}) collective-permute-start(bf16[256,288]{1,0:T(8,128)(2,1)S(1)} %get-tuple-element.106), channel_id=1, source_target_pairs={{0,1},{1,0},{2,3},{3,2},{4,5},{5,4},{6,7},{7,6},{8,9},{9,8},{10,11... | collective-permute-start | bytes 442376 | tf_op jit(solution)/shard_map/ppermute | solution.py:18
  47.1 1.8 %copy-start = (bf16[1024,1024]{1,0:T(8,128)(2,1)S(1)}, bf16[1024,1024]{1,0:T(8,128)(2,1)}, u32[]{:S(2)}) copy-start(bf16[1024,1024]{1,0:T(8,128)(2,1)} %weight_ref.1) | copy-start | bytes 6291460
  47.9 11.6 %collective-permute-start.18 = (bf16[2,128,416]{2,1,0:T(8,128)(2,1)S(1)}, bf16[2,128,416]{2,1,0:T(8,128)(2,1)S(1)}, u32[]{:S(2)}, u32[]{:S(2)}) collective-permute-start(bf16[2,128,416]{2,1,0:T(8,128)(2,1)S(1)} %get-tuple-element.108), channel_id=1, source_target_pairs={{0,4},{1,5},{2,6},{3,7},{4,0},{5,1},{6,2},{7,3},{8,12},{9,13},{10,... | collective-permute-start | bytes 638984 | tf_op jit(solution)/shard_map/ppermute | solution.py:18
  58.3 9.7 %collective-permute-start.15 = (bf16[2,64,896]{2,1,0:T(8,128)(2,1)S(1)}, bf16[2,64,896]{2,1,0:T(8,128)(2,1)S(1)}, u32[]{:S(2)}, u32[]{:S(2)}) collective-permute-start(bf16[2,64,896]{2,1,0:T(8,128)(2,1)S(1)} %get-tuple-element.100), channel_id=1, source_target_pairs={{0,4},{1,5},{2,6},{3,7},{4,0},{5,1},{6,2},{7,3},{8,12},{9,13},{10,... | collective-permute-start | bytes 688136 | tf_op jit(solution)/shard_map/ppermute | solution.py:18
  58.4 12.3 %collective-permute-start.11 = (bf16[1,64,1024]{2,1,0:T(8,128)(2,1)S(1)}, bf16[1,64,1024]{2,1,0:T(8,128)(2,1)S(1)}, u32[]{:S(2)}, u32[]{:S(2)}) collective-permute-start(bf16[1,64,1024]{2,1,0:T(8,128)(2,1)S(1)} %get-tuple-element.90), channel_id=1, source_target_pairs={{0,2},{1,3},{2,0},{3,1},{4,6},{5,7},{6,4},{7,5},{8,10},{9,11},{10,... | collective-permute-start | bytes 393224 | tf_op jit(solution)/shard_map/ppermute | solution.py:18
  60.1 9.1 %collective-permute-start.19 = (bf16[1,128,416]{2,1,0:T(8,128)(2,1)S(1)}, bf16[1,128,416]{2,1,0:T(8,128)(2,1)S(1)}, u32[]{:S(2)}, u32[]{:S(2)}) collective-permute-start(bf16[1,128,416]{2,1,0:T(8,128)(2,1)S(1)} %get-tuple-element.110), channel_id=1, source_target_pairs={{0,8},{1,9},{2,10},{3,11},{4,12},{5,13},{6,14},{7,15},{8,0},{9,1},... | collective-permute-start | bytes 319496 | tf_op jit(solution)/shard_map/ppermute | solution.py:18
  68.6 5.9 %collective-permute-start.21 = (bf16[1,64,896]{2,1,0:T(8,128)(2,1)S(1)}, bf16[1,64,896]{2,1,0:T(8,128)(2,1)S(1)}, u32[]{:S(2)}, u32[]{:S(2)}) collective-permute-start(bf16[1,64,896]{2,1,0:T(8,128)(2,1)S(1)} %get-tuple-element.101), channel_id=1, source_target_pairs={{0,8},{1,9},{2,10},{3,11},{4,12},{5,13},{6,14},{7,15},{8,0},{9,1},... | collective-permute-start | bytes 344072 | tf_op jit(solution)/shard_map/ppermute | solution.py:18
  69.9 4.3 %collective-permute-start.20 = (bf16[1,64,416]{2,1,0:T(8,128)(2,1)S(1)}, bf16[1,64,416]{2,1,0:T(8,128)(2,1)S(1)}, u32[]{:S(2)}, u32[]{:S(2)}) collective-permute-start(bf16[1,64,416]{2,1,0:T(8,128)(2,1)S(1)} %get-tuple-element.112), channel_id=1, source_target_pairs={{0,2},{1,3},{2,0},{3,1},{4,6},{5,7},{6,4},{7,5},{8,10},{9,11},{10,... | collective-permute-start | bytes 159752 | tf_op jit(solution)/shard_map/ppermute | solution.py:18

commit v6 on v5

--- a/solution.py
+++ b/solution.py
@@ -54,6 +54,10 @@
     )(place, *inputs)
 
 
+def bit_of(place_ref, bit):
+    return (place_ref[0] >> bit) & 1
+
+
 def nt_dot(a, b):
     return lax.dot_general(a, b, (((1,), (1,)), ((), ())), preferred_element_type=F32)
 
@@ -70,7 +74,7 @@
     channels = weight_ref.shape[0]
     step = channels // 2
     width = grad_ref.shape[0] // ROWS
-    half = place_ref[1]
+    half = bit_of(place_ref, 1)
     for part in range(2):
         here = slice(part * step, (part + 1) * step)
         weight = weight_ref[here, :]
@@ -112,7 +116,7 @@
     near_own_ref, near_core_ref, far_ref, edge_ref, sems,
 ):
     rows, width, _ = near_own_ref.shape
-    core, half = place_ref[0], place_ref[1]
+    core, half = bit_of(place_ref, 0), bit_of(place_ref, 1)
     copies = [(left_hbm, left_ref), (right_hbm, right_ref)]
     for target, row_at, column_at in (
         (far_ref.at[0], 1 - half, core),
@@ -188,9 +192,9 @@
             which, row = divmod(2 * at + side, 2 * pre // got)
             pair.append(total_ref[at, side] + received_refs[which][row].astype(F32))
         low, high = pair
-        keep_ref[at] = jnp.where(place_ref[bit] == 0, low, high)
+        keep_ref[at] = jnp.where(bit_of(place_ref, bit) == 0, low, high)
         which, row = divmod(at, pre // len(send_refs))
-        send_refs[which][row] = jnp.where(place_ref[bit] == 0, high, low).astype(BF)
+        send_refs[which][row] = jnp.where(bit_of(place_ref, bit) == 0, high, low).astype(BF)
 
 
 def fold_of(place, total, received, left, bit, piece, parts=1):
@@ -248,7 +252,7 @@
         if piece % 16:
             turned = turned.astype(F32)
         turned = turned.T.reshape(step // (2 * piece), 2, piece, positions)
-        keep, send = halves(turned, place_ref[0])
+        keep, send = halves(turned, bit_of(place_ref, 0))
         here = slice(shard * step // 2, (shard + 1) * step // 2)
         keep_ref[here, :] = keep.reshape(step // 2, positions).astype(BF)
         send_ref[here, :] = send.reshape(step // 2, positions).astype(BF)
@@ -297,8 +301,8 @@
     slots = slots[:1], slots[1:]
     positions, step = back_ref.shape[1:]
     width = positions // ROWS
-    core = place_ref[0]
-    side = place_ref[1] if near else 1 - place_ref[1]
+    core = bit_of(place_ref, 0)
+    side = bit_of(place_ref, 1) if near else 1 - bit_of(place_ref, 1)
     for slot, second_refs in enumerate(slots):
         shard = 2 * side + (core if slot == 0 else 1 - core)
         columns = pl.ds(pl.multiple_of(shard * step, step), step)
@@ -352,7 +356,7 @@
     slots = slots[:1], slots[1:]
     _, positions, step = back_ref.shape
     width = positions // ROWS
-    core, half = place_ref[0], place_ref[1]
+    core, half = bit_of(place_ref, 0), bit_of(place_ref, 1)
     side = half if near else 1 - half
     for slot, second_refs in enumerate(slots):
         turn = core if slot == 0 else 1 - core
@@ -446,11 +450,11 @@
     for at in range(keep_ref.shape[0]):
         here = slice(at * size, (at + 1) * size)
         low, high = both_halves(
-            place_ref[1], near_ref, far_ref, near_got_ref, far_got_ref, here
+            bit_of(place_ref, 1), near_ref, far_ref, near_got_ref, far_got_ref, here
         )
         edge = low.shape[1] - cut
         for columns, value in ((slice(0, edge), low[:, cut:]), (slice(edge, None), high)):
-            keep, send = halves(value.reshape(2, 2, piece, value.shape[1]), place_ref[1])
+            keep, send = halves(value.reshape(2, 2, piece, value.shape[1]), bit_of(place_ref, 1))
             rows = (size // 2, value.shape[1])
             keep_ref[at, :, columns] = keep.reshape(rows)
             send_ref[at, :, columns] = send.reshape(rows).astype(BF)
@@ -458,7 +462,7 @@
 
 def split_group_kernel(cut, piece, place_ref, *refs):
     *wide, near_ref, far_ref, near_got_ref, far_got_ref, keep_ref, send_ref = refs
-    half = place_ref[1]
+    half = bit_of(place_ref, 1)
     pre = keep_ref.shape[0]
     size = 4 * piece
     for at in range(pre):
@@ -473,7 +477,7 @@
             low, _ = both_halves(half, *wide, slice(at * size, (at + 1) * size))
             parts.append((slice(0, cut), low[:, :cut]))
         for columns, value in parts:
-            keep, send = halves(value.reshape(1, 2, size // 2, value.shape[1]), place_ref[2])
+            keep, send = halves(value.reshape(1, 2, size // 2, value.shape[1]), bit_of(place_ref, 2))
             keep_ref[at, :, columns] = keep[0]
             send_ref[at, :, columns] = send[0].astype(BF)
 
@@ -527,8 +531,8 @@
     channels = grad_ref.shape[1]
     step = channels // 4
     halfway = channels // 2
-    near = pl.ds(pl.multiple_of(place_ref[1] * halfway, halfway), halfway)
-    far = pl.ds(pl.multiple_of((1 - place_ref[1]) * halfway, halfway), halfway)
+    near = pl.ds(pl.multiple_of(bit_of(place_ref, 1) * halfway, halfway), halfway)
+    far = pl.ds(pl.multiple_of((1 - bit_of(place_ref, 1)) * halfway, halfway), halfway)
     outs = []
     for part in range(4):
         here = slice(part * step, (part + 1) * step)
@@ -565,8 +569,7 @@
     devices = lax.axis_size("space")
     position = lax.axis_index("space")
     n_bits = devices.bit_length() - 1
-    place = (position >> jnp.arange(n_bits, dtype=jnp.int32)) & 1
-    place = place.astype(jnp.int32)
+    place = position.astype(jnp.int32).reshape(1)
     _, tile_rows, width, channels = outer_grad.shape
     positions = tile_rows * width
     shard = channels // 4

time: 76 us -> 71.3 us (0.938)
  Pallas kernels: 27.7 us -> 18.5 us
  waiting for transfers between devices: 25.4 us -> 29.7 us
    pallas_call x16, Pallas kernels: 25 us -> 16.3 us  [call(): pl.pallas_call(kernel, in_specs=specs, out_specs=[pl.BlockSpec(memory_spa...]
    ppermute x21, waiting for transfers between devices: 25.4 us -> 29.7 us  [exchange(): lax.ppermute(array, 'space', [(i, i ^ 1 << bit) for i in range(count)])]
  transfers between devices with their start and end apart: 22 -> 22, of which waited for: 12 -> 13; matrix products, arithmetic and copies ran while one was open for 1% -> 1% of each run, Pallas kernels for 29% -> 20%
where the time goes in v6:
time: 71.3 us; the launch traced here: 71.1 us
  waiting for transfers between devices  29.7 us (42%)
  starting transfers between devices  21.2 us (30%)
  Pallas kernels  18.5 us (26%)
  between operations  0.83 us (1%)
  other arithmetic  0.73 us (1%)
    ppermute x21, waiting for transfers between devices, exchange(): lax.ppermute(array, 'space', [(i, i ^ 1 << bit) for i in range(count)])  29.7 us
    ppermute x21, starting transfers between devices, exchange(): lax.ppermute(array, 'space', [(i, i ^ 1 << bit) for i in range(count)])  20.3 us
    pallas_call x16, Pallas kernels, call(): pl.pallas_call(kernel, in_specs=specs, out_specs=[pl.BlockSpec(memory_spa...  16.3 us
    pallas_call x1, Pallas kernels, result_of(): pl.pallas_call(result_kernel, in_specs=[pl.BlockSpec(memory_space=pltpu.S...  2.16 us
  transfers between devices with their start and end apart: 22, of which 13 were waited for; matrix products, arithmetic and copies ran while one was open for 1% of the time, Pallas kernels for 20%

profile of v6, /device:TPU:0, one launch (start us, length us, event | category | flops | bytes accessed | tf_op | source)
XLA Modules:
  0.0 71.1 jit_solution(6638230233131874945)
XLA Ops:
  0.6 3.0 %front.1 = (f32[512,1024]{1,0:T(8,128)S(1)}, bf16[512,1024]{1,0:T(8,128)(2,1)S(1)}, bf16[512,1024]{1,0:T(8,128)(2,1)S(1)}, bf16[512,1024]{1,0:T(8,128)(2,1)S(1)}...) custom-call(s32[1]{0:T(128)} %bitcast.refs_0_.place_ref, ...), custom_call_target="tpu_custom_call" | custom-call | tf_op jit(solution)/shard_map/front/pallas_call | solution.py:45
  3.6 0.5 collective-permute-start
  4.1 2.6 %collective-permute-start.3 = (bf16[2,4,128,256]{3,2,1,0:T(8,128)(2,1)S(1)}, bf16[2,4,128,256]{3,2,1,0:T(8,128)(2,1)S(1)}, u32[]{:S(2)}, u32[]{:S(2)}) collective-permute-start(bf16[2,4,128,256]{3,2,1,0:T(8,128)(2,1)S(1)} %get-tuple-element.76), channel_id=1, source_target_pairs={{0,2},{1,3},{2,0},{3,1},{4,6},{5,7},{6,4},{7,5},{8,10},{9,11},{10,... | collective-permute-start | bytes 1572872 | tf_op jit(solution)/shard_map/ppermute | solution.py:18
  7.1 2.6 %collective-permute-start.9 = (bf16[1,128,1024]{2,1,0:T(8,128)(2,1)S(1)}, bf16[1,128,1024]{2,1,0:T(8,128)(2,1)S(1)}, u32[]{:S(2)}, u32[]{:S(2)}) collective-permute-start(bf16[1,128,1024]{2,1,0:T(8,128)(2,1)S(1)} %get-tuple-element.86), channel_id=1, source_target_pairs={{0,4},{1,5},{2,6},{3,7},{4,0},{5,1},{6,2},{7,3},{8,12},{9,13},{10,... | collective-permute-start | bytes 786440 | tf_op jit(solution)/shard_map/ppermute | solution.py:18
  9.8 1.2 %collective-permute-done.1.edge_ref = bf16[16,1024]{1,0:T(8,128)(2,1)S(1)} collective-permute-done((bf16[16,1024]{1,0:T(8,128)(2,1)S(1)}, bf16[16,1024]{1,0:T(8,128)(2,1)S(1)}, u32[]{:S(2)}, u32[]{:S(2)}) %collective-permute-start.1) | collective-permute-done | bytes 32800 | tf_op jit(solution)/shard_map/ppermute | solution.py:18
  11.0 1.9 %inner.1 = (bf16[512,1024]{1,0:T(8,128)(2,1)S(1)}, bf16[16,1024]{1,0:T(8,128)(2,1)S(1)}, bf16[144,1024]{1,0:T(8,128)(2,1)S(1)}, bf16[144,1024]{1,0:T(8,128)(2,1)S(1)}) custom-call(s32[1]{0:T(128)} %bitcast.refs_0_.place_ref, bf16[512,1024]{1,0:T(8,128)(2,1)S(1)} %get-tuple-element.64.grad_ref, bf16[1024,1024]{1,0:T(8,128)(2,1)S(1)} %get-tuple-element.65.weight_ref, ...), custom_call_target="tpu_custom_call" | custom-call | tf_op jit(solution)/shard_map/inner/pallas_call | solution.py:45
  12.9 1.9 %collective-permute-start.6 = (bf16[144,1024]{1,0:T(8,128)(2,1)S(1)}, bf16[144,1024]{1,0:T(8,128)(2,1)S(1)}, u32[]{:S(2)}, u32[]{:S(2)}) collective-permute-start(bf16[144,1024]{1,0:T(8,128)(2,1)S(1)} %get-tuple-element.79), channel_id=1, source_target_pairs={{0,2},{1,3},{2,0},{3,1},{4,6},{5,7},{6,4},{7,5},{8,10},{9,11},{10,... | collective-permute-start | bytes 884744 | tf_op jit(solution)/shard_map/ppermute | solution.py:18
  14.9 1.5 %ready.1 = (bf16[4,3,768,256]{3,2,1,0:T(8,128)(2,1)S(1)}, bf16[512,512]{1,0:T(8,128)(2,1)S(1)}, bf16[512,512]{1,0:T(8,128)(2,1)S(1)}) custom-call(s32[1]{0:T(128)} %bitcast.refs_0_.place_ref, bf16[288,1024]{1,0:T(8,128)(2,1)S(1)} %bitcast.34, bf16[512,1024]{1,0:T(8,128)(2,1)S(1)} %bitcast.30), custom_call_target="tpu_custom_call" | custom-call | tf_op jit(solution)/shard_map/ready/pallas_call | solution.py:45
  16.3 0.9 %collective-permute-start.7 = (bf16[144,1024]{1,0:T(8,128)(2,1)S(1)}, bf16[144,1024]{1,0:T(8,128)(2,1)S(1)}, u32[]{:S(2)}, u32[]{:S(2)}) collective-permute-start(bf16[144,1024]{1,0:T(8,128)(2,1)S(1)} %get-tuple-element.80), channel_id=1, source_target_pairs={{2,4},{4,2},{3,5},{5,3},{6,8},{8,6},{7,9},{9,7},{10,12},{12,10},{1... | collective-permute-start | bytes 884744 | tf_op jit(solution)/shard_map/ppermute | solution.py:28
  17.2 2.4 %body_near.1 = (f32[2,512,256]{2,1,0:T(8,128)S(1)}, f32[2,288,256]{2,1,0:T(8,128)S(1)}) custom-call(s32[1]{0:T(128)} %bitcast.refs_0_.place_ref, bf16[512,1024]{1,0:T(8,128)(2,1)S(1)} %get-tuple-element.68.refs_1_, bf16[16,1024]{1,0:T(8,128)(2,1)S(1)} %get-tuple-element.69.refs_2_, bf16[4,3,768,256]{3,2,1,0:T(8,128)(2,1)S(1)} %get-tuple-element.70.refs_3_.refs_7_, ...), custom_call_target="tpu_custom_call" | custom-call | tf_op jit(solution)/shard_map/body_near/pallas_call | solution.py:45
  19.7 2.7 %collective-permute-done.8.refs_2_ = bf16[1,128,1024]{2,1,0:T(8,128)(2,1)S(1)} collective-permute-done((bf16[1,128,1024]{2,1,0:T(8,128)(2,1)S(1)}, bf16[1,128,1024]{2,1,0:T(8,128)(2,1)S(1)}, u32[]{:S(2)}, u32[]{:S(2)}) %collective-permute-start.8) | collective-permute-done | bytes 262176 | tf_op jit(solution)/shard_map/ppermute | solution.py:18
  22.6 3.1 %collective-permute-start.10 = (bf16[1,128,1024]{2,1,0:T(8,128)(2,1)S(1)}, bf16[1,128,1024]{2,1,0:T(8,128)(2,1)S(1)}, u32[]{:S(2)}, u32[]{:S(2)}) collective-permute-start(bf16[1,128,1024]{2,1,0:T(8,128)(2,1)S(1)} %get-tuple-element.88), channel_id=1, source_target_pairs={{0,8},{1,9},{2,10},{3,11},{4,12},{5,13},{6,14},{7,15},{8,0},{9,1},... | collective-permute-start | bytes 786440 | tf_op jit(solution)/shard_map/ppermute | solution.py:18
  25.8 0.5 collective-permute-start.4
  26.3 0.8 %collective-permute-done.5.refs_6_.refs_14_ = bf16[2,128,256]{2,1,0:T(8,128)(2,1)S(1)} collective-permute-done((bf16[2,128,256]{2,1,0:T(8,128)(2,1)S(1)}, bf16[2,128,256]{2,1,0:T(8,128)(2,1)S(1)}, u32[]{:S(2)}, u32[]{:S(2)}) %collective-permute-start.5) | collective-permute-done | bytes 131104 | tf_op jit(solution)/shard_map/ppermute | solution.py:18
  27.3 2.5 %body_far.1 = (f32[2,512,256]{2,1,0:T(8,128)S(1)}, f32[2,288,256]{2,1,0:T(8,128)S(1)}) custom-call(s32[1]{0:T(128)} %bitcast.refs_0_.place_ref, bf16[512,1024]{1,0:T(8,128)(2,1)S(1)} %get-tuple-element.68.refs_1_, bf16[16,1024]{1,0:T(8,128)(2,1)S(1)} %get-tuple-element.69.refs_2_, bf16[4,3,768,256]{3,2,1,0:T(8,128)(2,1)S(1)} %get-tuple-element.70.refs_3_.refs_7_, ...), custom_call_target="tpu_custom_call" | custom-call | tf_op jit(solution)/shard_map/body_far/pallas_call | solution.py:45
  29.8 1.3 %collective-permute-done.6.refs_5_ = bf16[144,1024]{1,0:T(8,128)(2,1)S(1)} collective-permute-done((bf16[144,1024]{1,0:T(8,128)(2,1)S(1)}, bf16[144,1024]{1,0:T(8,128)(2,1)S(1)}, u32[]{:S(2)}, u32[]{:S(2)}) %collective-permute-start.6) | collective-permute-done | bytes 294944 | tf_op jit(solution)/shard_map/ppermute | solution.py:18
  31.1 2.9 %close.1 = (bf16[512,512]{1,0:T(8,128)(2,1)S(1)}, f32[512,512]{1,0:T(8,128)S(1)}, bf16[512,512]{1,0:T(8,128)(2,1)S(1)}, f32[256,288]{1,0:T(8,128)S(1)}, bf16[256...) custom-call(s32[1]{0:T(128)} %bitcast.refs_0_.place_ref, ...), custom_call_target="tpu_custom_call" | custom-call | tf_op jit(solution)/shard_map/close/pallas_call | solution.py:45
  34.1 5.2 %collective-permute-done.10 = bf16[1,128,1024]{2,1,0:T(8,128)(2,1)S(1)} collective-permute-done((bf16[1,128,1024]{2,1,0:T(8,128)(2,1)S(1)}, bf16[1,128,1024]{2,1,0:T(8,128)(2,1)S(1)}, u32[]{:S(2)}, u32[]{:S(2)}) %collective-permute-start.10) | collective-permute-done | bytes 262176 | tf_op jit(solution)/shard_map/ppermute | solution.py:18
  39.5 1.9 %collective-permute-done.12.refs_3_ = bf16[512,512]{1,0:T(8,128)(2,1)S(1)} collective-permute-done((bf16[512,512]{1,0:T(8,128)(2,1)S(1)}, bf16[512,512]{1,0:T(8,128)(2,1)S(1)}, u32[]{:S(2)}, u32[]{:S(2)}) %collective-permute-start.12) | collective-permute-done | bytes 524320 | tf_op jit(solution)/shard_map/ppermute | solution.py:18
  41.3 0.4 split.1
  42.4 0.9 %collective-permute-done.16.refs_7_ = bf16[256,288]{1,0:T(8,128)(2,1)S(1)} collective-permute-done((bf16[256,288]{1,0:T(8,128)(2,1)S(1)}, bf16[256,288]{1,0:T(8,128)(2,1)S(1)}, u32[]{:S(2)}, u32[]{:S(2)}) %collective-permute-start.16) | collective-permute-done | bytes 147488 | tf_op jit(solution)/shard_map/ppermute | solution.py:18
  43.9 1.1 %collective-permute-start.18 = (bf16[2,128,416]{2,1,0:T(8,128)(2,1)S(1)}, bf16[2,128,416]{2,1,0:T(8,128)(2,1)S(1)}, u32[]{:S(2)}, u32[]{:S(2)}) collective-permute-start(bf16[2,128,416]{2,1,0:T(8,128)(2,1)S(1)} %get-tuple-element.108), channel_id=1, source_target_pairs={{0,4},{1,5},{2,6},{3,7},{4,0},{5,1},{6,2},{7,3},{8,12},{9,13},{10,... | collective-permute-start | bytes 638984 | tf_op jit(solution)/shard_map/ppermute | solution.py:18
  45.2 2.2 %result.1 = bf16[512,1024]{1,0:T(8,128)(2,1)} custom-call(s32[1]{0:T(128)} %bitcast.refs_0_.place_ref, bf16[512,512]{1,0:T(8,128)(2,1)S(1)} %get-tuple-element.83.near_ref, bf16[512,512]{1,0:T(8,128)(2,1)S(1)} %get-tuple-element.84.far_ref, bf16[512,1024]{1,0:T(8,128)(2,1)S(1)} %get-tuple-element.64.grad_ref, bf16[1024,1024]{1,0:T(8,128)(2,1)S(1)} %copy-done), custom_call_target="tpu_custom_call" | custom-call | tf_op jit(solution)/shard_map/result/pallas_call | solution.py:554
  47.4 7.0 %collective-permute-done.14 = bf16[2,128,896]{2,1,0:T(8,128)(2,1)S(1)} collective-permute-done((bf16[2,128,896]{2,1,0:T(8,128)(2,1)S(1)}, bf16[2,128,896]{2,1,0:T(8,128)(2,1)S(1)}, u32[]{:S(2)}, u32[]{:S(2)}) %collective-permute-start.14) | collective-permute-done | bytes 458784 | tf_op jit(solution)/shard_map/ppermute | solution.py:18
  54.6 1.1 %collective-permute-start.11 = (bf16[1,64,1024]{2,1,0:T(8,128)(2,1)S(1)}, bf16[1,64,1024]{2,1,0:T(8,128)(2,1)S(1)}, u32[]{:S(2)}, u32[]{:S(2)}) collective-permute-start(bf16[1,64,1024]{2,1,0:T(8,128)(2,1)S(1)} %get-tuple-element.90), channel_id=1, source_target_pairs={{0,2},{1,3},{2,0},{3,1},{4,6},{5,7},{6,4},{7,5},{8,10},{9,11},{10,... | collective-permute-start | bytes 393224 | tf_op jit(solution)/shard_map/ppermute | solution.py:18
  55.8 3.4 %collective-permute-start.19 = (bf16[1,128,416]{2,1,0:T(8,128)(2,1)S(1)}, bf16[1,128,416]{2,1,0:T(8,128)(2,1)S(1)}, u32[]{:S(2)}, u32[]{:S(2)}) collective-permute-start(bf16[1,128,416]{2,1,0:T(8,128)(2,1)S(1)} %get-tuple-element.110), channel_id=1, source_target_pairs={{0,8},{1,9},{2,10},{3,11},{4,12},{5,13},{6,14},{7,15},{8,0},{9,1},... | collective-permute-start | bytes 319496 | tf_op jit(solution)/shard_map/ppermute | solution.py:18
  59.2 5.0 %collective-permute-done.15.refs_2_ = bf16[2,64,896]{2,1,0:T(8,128)(2,1)S(1)} collective-permute-done((bf16[2,64,896]{2,1,0:T(8,128)(2,1)S(1)}, bf16[2,64,896]{2,1,0:T(8,128)(2,1)S(1)}, u32[]{:S(2)}, u32[]{:S(2)}) %collective-permute-start.15) | collective-permute-done | bytes 229408 | tf_op jit(solution)/shard_map/ppermute | solution.py:18
  64.4 2.1 %collective-permute-start.20 = (bf16[1,64,416]{2,1,0:T(8,128)(2,1)S(1)}, bf16[1,64,416]{2,1,0:T(8,128)(2,1)S(1)}, u32[]{:S(2)}, u32[]{:S(2)}) collective-permute-start(bf16[1,64,416]{2,1,0:T(8,128)(2,1)S(1)} %get-tuple-element.112), channel_id=1, source_target_pairs={{0,2},{1,3},{2,0},{3,1},{4,6},{5,7},{6,4},{7,5},{8,10},{9,11},{10,... | collective-permute-start | bytes 159752 | tf_op jit(solution)/shard_map/ppermute | solution.py:18
  66.5 0.7 %multiply_bitcast_fusion = f32[64,1024]{1,0:T(8,128)} fusion(f32[1,64,1024]{2,1,0:T(8,128)S(1)} %get-tuple-element.89, bf16[1,64,1024]{2,1,0:T(8,128)(2,1)S(1)} %collective-permute-done.11), kind=kLoop, calls=%fused_computation.1 | loop fusion | flops 196608 | bytes 655360 | tf_op jit(solution)/shard_map/mul | solution.py:642
  67.2 1.5 %collective-permute-done.20 = bf16[1,64,416]{2,1,0:T(8,128)(2,1)S(1)} collective-permute-done((bf16[1,64,416]{2,1,0:T(8,128)(2,1)S(1)}, bf16[1,64,416]{2,1,0:T(8,128)(2,1)S(1)}, u32[]{:S(2)}, u32[]{:S(2)}) %collective-permute-start.20) | collective-permute-done | bytes 53280 | tf_op jit(solution)/shard_map/ppermute | solution.py:18
  68.8 1.6 %collective-permute-done.21 = bf16[1,64,896]{2,1,0:T(8,128)(2,1)S(1)} collective-permute-done((bf16[1,64,896]{2,1,0:T(8,128)(2,1)S(1)}, bf16[1,64,896]{2,1,0:T(8,128)(2,1)S(1)}, u32[]{:S(2)}, u32[]{:S(2)}) %collective-permute-start.21) | collective-permute-done | bytes 114720 | tf_op jit(solution)/shard_map/ppermute | solution.py:18
  70.3 0.8 %last.1 = (f32[64,1024]{1,0:T(8,128)}, f32[64,288]{1,0:T(8,128)}) custom-call(s32[1]{0:T(128)} %bitcast.refs_0_.place_ref, f32[64,416]{1,0:T(8,128)S(1)} %bitcast.42, bf16[64,416]{1,0:T(8,128)(2,1)S(1)} %bitcast.45, f32[64,896]{1,0:T(8,128)S(1)} %bitcast.41, bf16[64,896]{1,0:T(8,128)(2,1)S(1)} %bitcast.44), custom_call_target="tpu_custom_call" | custom-call | tf_op jit(solution)/shard_map/last/pallas_call | solution.py:45
  (38 shorter events, 3.0 us)
Async XLA Ops:
  3.6 3.3 %collective-permute-start = (bf16[512,1024]{1,0:T(8,128)(2,1)S(1)}, bf16[512,1024]{1,0:T(8,128)(2,1)S(1)}, u32[]{:S(2)}, u32[]{:S(2)}) collective-permute-start(bf16[512,1024]{1,0:T(8,128)(2,1)S(1)} %get-tuple-element.61), channel_id=1, source_target_pairs={{0,1},{1,0},{2,3},{3,2},{4,5},{5,4},{6,7},{7,6},{8,9},{9,8},{10,11... | collective-permute-start | bytes 3145736 | tf_op jit(solution)/shard_map/ppermute | solution.py:18
  4.1 21.6 %collective-permute-start.3 = (bf16[2,4,128,256]{3,2,1,0:T(8,128)(2,1)S(1)}, bf16[2,4,128,256]{3,2,1,0:T(8,128)(2,1)S(1)}, u32[]{:S(2)}, u32[]{:S(2)}) collective-permute-start(bf16[2,4,128,256]{3,2,1,0:T(8,128)(2,1)S(1)} %get-tuple-element.76), channel_id=1, source_target_pairs={{0,2},{1,3},{2,0},{3,1},{4,6},{5,7},{6,4},{7,5},{8,10},{9,11},{10,... | collective-permute-start | bytes 1572872 | tf_op jit(solution)/shard_map/ppermute | solution.py:18
  6.7 9.6 %collective-permute-start.2 = (bf16[4,128,256]{2,1,0:T(8,128)(2,1)S(1)}, bf16[4,128,256]{2,1,0:T(8,128)(2,1)S(1)}, u32[]{:S(2)}, u32[]{:S(2)}) collective-permute-start(bf16[4,128,256]{2,1,0:T(8,128)(2,1)S(1)} %get-tuple-element.72), channel_id=1, source_target_pairs={{0,1},{1,0},{2,3},{3,2},{4,5},{5,4},{6,7},{7,6},{8,9},{9,8},{10,11... | collective-permute-start | bytes 786440 | tf_op jit(solution)/shard_map/ppermute | solution.py:18
  7.1 12.5 %collective-permute-start.9 = (bf16[1,128,1024]{2,1,0:T(8,128)(2,1)S(1)}, bf16[1,128,1024]{2,1,0:T(8,128)(2,1)S(1)}, u32[]{:S(2)}, u32[]{:S(2)}) collective-permute-start(bf16[1,128,1024]{2,1,0:T(8,128)(2,1)S(1)} %get-tuple-element.86), channel_id=1, source_target_pairs={{0,4},{1,5},{2,6},{3,7},{4,0},{5,1},{6,2},{7,3},{8,12},{9,13},{10,... | collective-permute-start | bytes 786440 | tf_op jit(solution)/shard_map/ppermute | solution.py:18
  9.7 12.7 %collective-permute-start.8 = (bf16[1,128,1024]{2,1,0:T(8,128)(2,1)S(1)}, bf16[1,128,1024]{2,1,0:T(8,128)(2,1)S(1)}, u32[]{:S(2)}, u32[]{:S(2)}) collective-permute-start(bf16[1,128,1024]{2,1,0:T(8,128)(2,1)S(1)} %get-tuple-element.62), channel_id=1, source_target_pairs={{0,4},{1,5},{2,6},{3,7},{4,0},{5,1},{6,2},{7,3},{8,12},{9,13},{10,... | collective-permute-start | bytes 786440 | tf_op jit(solution)/shard_map/ppermute | solution.py:18
  9.8 1.2 %collective-permute-start.1 = (bf16[16,1024]{1,0:T(8,128)(2,1)S(1)}, bf16[16,1024]{1,0:T(8,128)(2,1)S(1)}, u32[]{:S(2)}, u32[]{:S(2)}) collective-permute-start(bf16[16,1024]{1,0:T(8,128)(2,1)S(1)} %get-tuple-element.67), channel_id=1, source_target_pairs={{0,1},{1,0},{2,3},{3,2},{4,5},{5,4},{6,7},{7,6},{8,9},{9,8},{10,11... | collective-permute-start | bytes 98312 | tf_op jit(solution)/shard_map/ppermute | solution.py:18
  11.0 3.9 %copy-start.1 = (bf16[1,4,128,1024]{3,2,1,0:T(8,128)(2,1)S(1)}, bf16[1,4,128,1024]{3,2,1,0:T(8,128)(2,1)}, u32[]{:S(2)}) copy-start(bf16[1,4,128,1024]{3,2,1,0:T(8,128)(2,1)} %param.8) | copy-start | bytes 3145732
  11.0 3.9 %copy-start.2 = (bf16[1024,288]{0,1:T(8,128)(2,1)S(1)}, bf16[1024,288]{0,1:T(8,128)(2,1)}, u32[]{:S(2)}) copy-start(bf16[1024,288]{0,1:T(8,128)(2,1)} %param.12) | copy-start | bytes 1769476
  12.9 18.2 %collective-permute-start.6 = (bf16[144,1024]{1,0:T(8,128)(2,1)S(1)}, bf16[144,1024]{1,0:T(8,128)(2,1)S(1)}, u32[]{:S(2)}, u32[]{:S(2)}) collective-permute-start(bf16[144,1024]{1,0:T(8,128)(2,1)S(1)} %get-tuple-element.79), channel_id=1, source_target_pairs={{0,2},{1,3},{2,0},{3,1},{4,6},{5,7},{6,4},{7,5},{8,10},{9,11},{10,... | collective-permute-start | bytes 884744 | tf_op jit(solution)/shard_map/ppermute | solution.py:18
  16.3 14.8 %collective-permute-start.7 = (bf16[144,1024]{1,0:T(8,128)(2,1)S(1)}, bf16[144,1024]{1,0:T(8,128)(2,1)S(1)}, u32[]{:S(2)}, u32[]{:S(2)}) collective-permute-start(bf16[144,1024]{1,0:T(8,128)(2,1)S(1)} %get-tuple-element.80), channel_id=1, source_target_pairs={{2,4},{4,2},{3,5},{5,3},{6,8},{8,6},{7,9},{9,7},{10,12},{12,10},{1... | collective-permute-start | bytes 884744 | tf_op jit(solution)/shard_map/ppermute | solution.py:28
  22.6 16.7 %collective-permute-start.10 = (bf16[1,128,1024]{2,1,0:T(8,128)(2,1)S(1)}, bf16[1,128,1024]{2,1,0:T(8,128)(2,1)S(1)}, u32[]{:S(2)}, u32[]{:S(2)}) collective-permute-start(bf16[1,128,1024]{2,1,0:T(8,128)(2,1)S(1)} %get-tuple-element.88), channel_id=1, source_target_pairs={{0,8},{1,9},{2,10},{3,11},{4,12},{5,13},{6,14},{7,15},{8,0},{9,1},... | collective-permute-start | bytes 786440 | tf_op jit(solution)/shard_map/ppermute | solution.py:18
  25.7 1.4 %collective-permute-start.5 = (bf16[2,128,256]{2,1,0:T(8,128)(2,1)S(1)}, bf16[2,128,256]{2,1,0:T(8,128)(2,1)S(1)}, u32[]{:S(2)}, u32[]{:S(2)}) collective-permute-start(bf16[2,128,256]{2,1,0:T(8,128)(2,1)S(1)} %get-tuple-element.116), channel_id=1, source_target_pairs={{0,1},{1,0},{2,3},{3,2},{4,5},{5,4},{6,7},{7,6},{8,9},{9,8},{10,11... | collective-permute-start | bytes 393224 | tf_op jit(solution)/shard_map/ppermute | solution.py:18
  25.8 1.5 %collective-permute-start.4 = (bf16[2,128,256]{2,1,0:T(8,128)(2,1)S(1)}, bf16[2,128,256]{2,1,0:T(8,128)(2,1)S(1)}, u32[]{:S(2)}, u32[]{:S(2)}) collective-permute-start(bf16[2,128,256]{2,1,0:T(8,128)(2,1)S(1)} %get-tuple-element.117), channel_id=1, source_target_pairs={{0,1},{1,0},{2,3},{3,2},{4,5},{5,4},{6,7},{7,6},{8,9},{9,8},{10,11... | collective-permute-start | bytes 393224 | tf_op jit(solution)/shard_map/ppermute | solution.py:18
  34.0 5.4 %collective-permute-start.13 = (bf16[512,512]{1,0:T(8,128)(2,1)S(1)}, bf16[512,512]{1,0:T(8,128)(2,1)S(1)}, u32[]{:S(2)}, u32[]{:S(2)}) collective-permute-start(bf16[512,512]{1,0:T(8,128)(2,1)S(1)} %get-tuple-element.96), channel_id=1, source_target_pairs={{0,1},{1,0},{2,3},{3,2},{4,5},{5,4},{6,7},{7,6},{8,9},{9,8},{10,11... | collective-permute-start | bytes 1572872 | tf_op jit(solution)/shard_map/ppermute | solution.py:18
  39.4 2.0 %collective-permute-start.12 = (bf16[512,512]{1,0:T(8,128)(2,1)S(1)}, bf16[512,512]{1,0:T(8,128)(2,1)S(1)}, u32[]{:S(2)}, u32[]{:S(2)}) collective-permute-start(bf16[512,512]{1,0:T(8,128)(2,1)S(1)} %get-tuple-element.95), channel_id=1, source_target_pairs={{0,1},{1,0},{2,3},{3,2},{4,5},{5,4},{6,7},{7,6},{8,9},{9,8},{10,11... | collective-permute-start | bytes 1572872 | tf_op jit(solution)/shard_map/ppermute | solution.py:18
  41.8 12.6 %collective-permute-start.14 = (bf16[2,128,896]{2,1,0:T(8,128)(2,1)S(1)}, bf16[2,128,896]{2,1,0:T(8,128)(2,1)S(1)}, u32[]{:S(2)}, u32[]{:S(2)}) collective-permute-start(bf16[2,128,896]{2,1,0:T(8,128)(2,1)S(1)} %get-tuple-element.98), channel_id=1, source_target_pairs={{0,2},{1,3},{2,0},{3,1},{4,6},{5,7},{6,4},{7,5},{8,10},{9,11},{10,... | collective-permute-start | bytes 1376264 | tf_op jit(solution)/shard_map/ppermute | solution.py:18
  41.8 1.5 %collective-permute-start.16 = (bf16[256,288]{1,0:T(8,128)(2,1)S(1)}, bf16[256,288]{1,0:T(8,128)(2,1)S(1)}, u32[]{:S(2)}, u32[]{:S(2)}) collective-permute-start(bf16[256,288]{1,0:T(8,128)(2,1)S(1)} %get-tuple-element.105), channel_id=1, source_target_pairs={{0,1},{1,0},{2,3},{3,2},{4,5},{5,4},{6,7},{7,6},{8,9},{9,8},{10,11... | collective-permute-start | bytes 442376 | tf_op jit(solution)/shard_map/ppermute | solution.py:18
  42.0 1.6 %collective-permute-start.17 = (bf16[256,288]{1,0:T(8,128)(2,1)S(1)}, bf16[256,288]{1,0:T(8,128)(2,1)S(1)}, u32[]{:S(2)}, u32[]{:S(2)}) collective-permute-start(bf16[256,288]{1,0:T(8,128)(2,1)S(1)} %get-tuple-element.106), channel_id=1, source_target_pairs={{0,1},{1,0},{2,3},{3,2},{4,5},{5,4},{6,7},{7,6},{8,9},{9,8},{10,11... | collective-permute-start | bytes 442376 | tf_op jit(solution)/shard_map/ppermute | solution.py:18
  43.6 1.6 %copy-start = (bf16[1024,1024]{1,0:T(8,128)(2,1)S(1)}, bf16[1024,1024]{1,0:T(8,128)(2,1)}, u32[]{:S(2)}) copy-start(bf16[1024,1024]{1,0:T(8,128)(2,1)} %weight_ref.1) | copy-start | bytes 6291460
  43.9 11.8 %collective-permute-start.18 = (bf16[2,128,416]{2,1,0:T(8,128)(2,1)S(1)}, bf16[2,128,416]{2,1,0:T(8,128)(2,1)S(1)}, u32[]{:S(2)}, u32[]{:S(2)}) collective-permute-start(bf16[2,128,416]{2,1,0:T(8,128)(2,1)S(1)} %get-tuple-element.108), channel_id=1, source_target_pairs={{0,4},{1,5},{2,6},{3,7},{4,0},{5,1},{6,2},{7,3},{8,12},{9,13},{10,... | collective-permute-start | bytes 638984 | tf_op jit(solution)/shard_map/ppermute | solution.py:18
  54.5 9.7 %collective-permute-start.15 = (bf16[2,64,896]{2,1,0:T(8,128)(2,1)S(1)}, bf16[2,64,896]{2,1,0:T(8,128)(2,1)S(1)}, u32[]{:S(2)}, u32[]{:S(2)}) collective-permute-start(bf16[2,64,896]{2,1,0:T(8,128)(2,1)S(1)} %get-tuple-element.100), channel_id=1, source_target_pairs={{0,4},{1,5},{2,6},{3,7},{4,0},{5,1},{6,2},{7,3},{8,12},{9,13},{10,... | collective-permute-start | bytes 688136 | tf_op jit(solution)/shard_map/ppermute | solution.py:18
  54.6 11.9 %collective-permute-start.11 = (bf16[1,64,1024]{2,1,0:T(8,128)(2,1)S(1)}, bf16[1,64,1024]{2,1,0:T(8,128)(2,1)S(1)}, u32[]{:S(2)}, u32[]{:S(2)}) collective-permute-start(bf16[1,64,1024]{2,1,0:T(8,128)(2,1)S(1)} %get-tuple-element.90), channel_id=1, source_target_pairs={{0,2},{1,3},{2,0},{3,1},{4,6},{5,7},{6,4},{7,5},{8,10},{9,11},{10,... | collective-permute-start | bytes 393224 | tf_op jit(solution)/shard_map/ppermute | solution.py:18
  55.8 8.5 %collective-permute-start.19 = (bf16[1,128,416]{2,1,0:T(8,128)(2,1)S(1)}, bf16[1,128,416]{2,1,0:T(8,128)(2,1)S(1)}, u32[]{:S(2)}, u32[]{:S(2)}) collective-permute-start(bf16[1,128,416]{2,1,0:T(8,128)(2,1)S(1)} %get-tuple-element.110), channel_id=1, source_target_pairs={{0,8},{1,9},{2,10},{3,11},{4,12},{5,13},{6,14},{7,15},{8,0},{9,1},... | collective-permute-start | bytes 319496 | tf_op jit(solution)/shard_map/ppermute | solution.py:18
  64.3 6.1 %collective-permute-start.21 = (bf16[1,64,896]{2,1,0:T(8,128)(2,1)S(1)}, bf16[1,64,896]{2,1,0:T(8,128)(2,1)S(1)}, u32[]{:S(2)}, u32[]{:S(2)}) collective-permute-start(bf16[1,64,896]{2,1,0:T(8,128)(2,1)S(1)} %get-tuple-element.101), channel_id=1, source_target_pairs={{0,8},{1,9},{2,10},{3,11},{4,12},{5,13},{6,14},{7,15},{8,0},{9,1},... | collective-permute-start | bytes 344072 | tf_op jit(solution)/shard_map/ppermute | solution.py:18
  64.4 4.4 %collective-permute-start.20 = (bf16[1,64,416]{2,1,0:T(8,128)(2,1)S(1)}, bf16[1,64,416]{2,1,0:T(8,128)(2,1)S(1)}, u32[]{:S(2)}, u32[]{:S(2)}) collective-permute-start(bf16[1,64,416]{2,1,0:T(8,128)(2,1)S(1)} %get-tuple-element.112), channel_id=1, source_target_pairs={{0,2},{1,3},{2,0},{3,1},{4,6},{5,7},{6,4},{7,5},{8,10},{9,11},{10,... | collective-permute-start | bytes 159752 | tf_op jit(solution)/shard_map/ppermute | solution.py:18

commit v7 on v6

--- a/solution.py
+++ b/solution.py
@@ -626,9 +626,9 @@
         closing, near, (near_own, near_other), far, (far_own, *far_other),
         (inside, outside, spread, keep_in, send_in), piece,
     )
-    near_got = exchange(after(near_send, sent), 0)
+    near_got = exchange(near_send, 0)
     group_near_got = exchange(group_near_send, 0)
-    far_got = exchange(far_send, 0)
+    far_got = exchange(after(far_send, sent), 0)
     group_far_got = exchange(group_far_send, 0)
 
     cut = shard // 2

time: 71.3 us -> 71.3 us (level)
  no operation moved by 1% of the time
where the time goes in v7:
time: 71.3 us; the launch traced here: 71.1 us
  waiting for transfers between devices  29.7 us (42%)
  starting transfers between devices  21.2 us (30%)
  Pallas kernels  18.5 us (26%)
  between operations  0.83 us (1%)
  other arithmetic  0.73 us (1%)
    ppermute x21, waiting for transfers between devices, exchange(): lax.ppermute(array, 'space', [(i, i ^ 1 << bit) for i in range(count)])  29.7 us
    ppermute x21, starting transfers between devices, exchange(): lax.ppermute(array, 'space', [(i, i ^ 1 << bit) for i in range(count)])  20.3 us
    pallas_call x16, Pallas kernels, call(): pl.pallas_call(kernel, in_specs=specs, out_specs=[pl.BlockSpec(memory_spa...  16.3 us
    pallas_call x1, Pallas kernels, result_of(): pl.pallas_call(result_kernel, in_specs=[pl.BlockSpec(memory_space=pltpu.S...  2.16 us
  transfers between devices with their start and end apart: 22, of which 13 were waited for; matrix products, arithmetic and copies ran while one was open for 1% of the time, Pallas kernels for 20%

profile of v7, /device:TPU:0, one launch (start us, length us, event | category | flops | bytes accessed | tf_op | source)
XLA Modules:
  0.0 71.1 jit_solution(15696535037944376904)
XLA Ops:
  0.6 3.0 %front.1 = (f32[512,1024]{1,0:T(8,128)S(1)}, bf16[512,1024]{1,0:T(8,128)(2,1)S(1)}, bf16[512,1024]{1,0:T(8,128)(2,1)S(1)}, bf16[512,1024]{1,0:T(8,128)(2,1)S(1)}...) custom-call(s32[1]{0:T(128)} %bitcast.refs_0_.place_ref, ...), custom_call_target="tpu_custom_call" | custom-call | tf_op jit(solution)/shard_map/front/pallas_call | solution.py:45
  3.6 0.5 collective-permute-start
  4.1 2.6 %collective-permute-start.3 = (bf16[2,4,128,256]{3,2,1,0:T(8,128)(2,1)S(1)}, bf16[2,4,128,256]{3,2,1,0:T(8,128)(2,1)S(1)}, u32[]{:S(2)}, u32[]{:S(2)}) collective-permute-start(bf16[2,4,128,256]{3,2,1,0:T(8,128)(2,1)S(1)} %get-tuple-element.76), channel_id=1, source_target_pairs={{0,2},{1,3},{2,0},{3,1},{4,6},{5,7},{6,4},{7,5},{8,10},{9,11},{10,... | collective-permute-start | bytes 1572872 | tf_op jit(solution)/shard_map/ppermute | solution.py:18
  7.1 2.6 %collective-permute-start.9 = (bf16[1,128,1024]{2,1,0:T(8,128)(2,1)S(1)}, bf16[1,128,1024]{2,1,0:T(8,128)(2,1)S(1)}, u32[]{:S(2)}, u32[]{:S(2)}) collective-permute-start(bf16[1,128,1024]{2,1,0:T(8,128)(2,1)S(1)} %get-tuple-element.86), channel_id=1, source_target_pairs={{0,4},{1,5},{2,6},{3,7},{4,0},{5,1},{6,2},{7,3},{8,12},{9,13},{10,... | collective-permute-start | bytes 786440 | tf_op jit(solution)/shard_map/ppermute | solution.py:18
  9.8 1.2 %collective-permute-done.1.edge_ref = bf16[16,1024]{1,0:T(8,128)(2,1)S(1)} collective-permute-done((bf16[16,1024]{1,0:T(8,128)(2,1)S(1)}, bf16[16,1024]{1,0:T(8,128)(2,1)S(1)}, u32[]{:S(2)}, u32[]{:S(2)}) %collective-permute-start.1) | collective-permute-done | bytes 32800 | tf_op jit(solution)/shard_map/ppermute | solution.py:18
  11.0 1.9 %inner.1 = (bf16[512,1024]{1,0:T(8,128)(2,1)S(1)}, bf16[16,1024]{1,0:T(8,128)(2,1)S(1)}, bf16[144,1024]{1,0:T(8,128)(2,1)S(1)}, bf16[144,1024]{1,0:T(8,128)(2,1)S(1)}) custom-call(s32[1]{0:T(128)} %bitcast.refs_0_.place_ref, bf16[512,1024]{1,0:T(8,128)(2,1)S(1)} %get-tuple-element.64.grad_ref, bf16[1024,1024]{1,0:T(8,128)(2,1)S(1)} %get-tuple-element.65.weight_ref, ...), custom_call_target="tpu_custom_call" | custom-call | tf_op jit(solution)/shard_map/inner/pallas_call | solution.py:45
  12.9 1.9 %collective-permute-start.6 = (bf16[144,1024]{1,0:T(8,128)(2,1)S(1)}, bf16[144,1024]{1,0:T(8,128)(2,1)S(1)}, u32[]{:S(2)}, u32[]{:S(2)}) collective-permute-start(bf16[144,1024]{1,0:T(8,128)(2,1)S(1)} %get-tuple-element.79), channel_id=1, source_target_pairs={{0,2},{1,3},{2,0},{3,1},{4,6},{5,7},{6,4},{7,5},{8,10},{9,11},{10,... | collective-permute-start | bytes 884744 | tf_op jit(solution)/shard_map/ppermute | solution.py:18
  14.9 1.5 %ready.1 = (bf16[4,3,768,256]{3,2,1,0:T(8,128)(2,1)S(1)}, bf16[512,512]{1,0:T(8,128)(2,1)S(1)}, bf16[512,512]{1,0:T(8,128)(2,1)S(1)}) custom-call(s32[1]{0:T(128)} %bitcast.refs_0_.place_ref, bf16[288,1024]{1,0:T(8,128)(2,1)S(1)} %bitcast.34, bf16[512,1024]{1,0:T(8,128)(2,1)S(1)} %bitcast.30), custom_call_target="tpu_custom_call" | custom-call | tf_op jit(solution)/shard_map/ready/pallas_call | solution.py:45
  16.3 0.9 %collective-permute-start.7 = (bf16[144,1024]{1,0:T(8,128)(2,1)S(1)}, bf16[144,1024]{1,0:T(8,128)(2,1)S(1)}, u32[]{:S(2)}, u32[]{:S(2)}) collective-permute-start(bf16[144,1024]{1,0:T(8,128)(2,1)S(1)} %get-tuple-element.80), channel_id=1, source_target_pairs={{2,4},{4,2},{3,5},{5,3},{6,8},{8,6},{7,9},{9,7},{10,12},{12,10},{1... | collective-permute-start | bytes 884744 | tf_op jit(solution)/shard_map/ppermute | solution.py:28
  17.2 2.4 %body_near.1 = (f32[2,512,256]{2,1,0:T(8,128)S(1)}, f32[2,288,256]{2,1,0:T(8,128)S(1)}) custom-call(s32[1]{0:T(128)} %bitcast.refs_0_.place_ref, bf16[512,1024]{1,0:T(8,128)(2,1)S(1)} %get-tuple-element.68.refs_1_, bf16[16,1024]{1,0:T(8,128)(2,1)S(1)} %get-tuple-element.69.refs_2_, bf16[4,3,768,256]{3,2,1,0:T(8,128)(2,1)S(1)} %get-tuple-element.70.refs_3_.refs_7_, ...), custom_call_target="tpu_custom_call" | custom-call | tf_op jit(solution)/shard_map/body_near/pallas_call | solution.py:45
  19.7 2.7 %collective-permute-done.8.refs_2_ = bf16[1,128,1024]{2,1,0:T(8,128)(2,1)S(1)} collective-permute-done((bf16[1,128,1024]{2,1,0:T(8,128)(2,1)S(1)}, bf16[1,128,1024]{2,1,0:T(8,128)(2,1)S(1)}, u32[]{:S(2)}, u32[]{:S(2)}) %collective-permute-start.8) | collective-permute-done | bytes 262176 | tf_op jit(solution)/shard_map/ppermute | solution.py:18
  22.6 3.1 %collective-permute-start.10 = (bf16[1,128,1024]{2,1,0:T(8,128)(2,1)S(1)}, bf16[1,128,1024]{2,1,0:T(8,128)(2,1)S(1)}, u32[]{:S(2)}, u32[]{:S(2)}) collective-permute-start(bf16[1,128,1024]{2,1,0:T(8,128)(2,1)S(1)} %get-tuple-element.88), channel_id=1, source_target_pairs={{0,8},{1,9},{2,10},{3,11},{4,12},{5,13},{6,14},{7,15},{8,0},{9,1},... | collective-permute-start | bytes 786440 | tf_op jit(solution)/shard_map/ppermute | solution.py:18
  25.8 0.5 collective-permute-start.4
  26.3 0.8 %collective-permute-done.5.refs_6_.refs_14_ = bf16[2,128,256]{2,1,0:T(8,128)(2,1)S(1)} collective-permute-done((bf16[2,128,256]{2,1,0:T(8,128)(2,1)S(1)}, bf16[2,128,256]{2,1,0:T(8,128)(2,1)S(1)}, u32[]{:S(2)}, u32[]{:S(2)}) %collective-permute-start.5) | collective-permute-done | bytes 131104 | tf_op jit(solution)/shard_map/ppermute | solution.py:18
  27.3 2.5 %body_far.1 = (f32[2,512,256]{2,1,0:T(8,128)S(1)}, f32[2,288,256]{2,1,0:T(8,128)S(1)}) custom-call(s32[1]{0:T(128)} %bitcast.refs_0_.place_ref, bf16[512,1024]{1,0:T(8,128)(2,1)S(1)} %get-tuple-element.68.refs_1_, bf16[16,1024]{1,0:T(8,128)(2,1)S(1)} %get-tuple-element.69.refs_2_, bf16[4,3,768,256]{3,2,1,0:T(8,128)(2,1)S(1)} %get-tuple-element.70.refs_3_.refs_7_, ...), custom_call_target="tpu_custom_call" | custom-call | tf_op jit(solution)/shard_map/body_far/pallas_call | solution.py:45
  29.8 1.3 %collective-permute-done.6.refs_5_ = bf16[144,1024]{1,0:T(8,128)(2,1)S(1)} collective-permute-done((bf16[144,1024]{1,0:T(8,128)(2,1)S(1)}, bf16[144,1024]{1,0:T(8,128)(2,1)S(1)}, u32[]{:S(2)}, u32[]{:S(2)}) %collective-permute-start.6) | collective-permute-done | bytes 294944 | tf_op jit(solution)/shard_map/ppermute | solution.py:18
  31.1 2.9 %close.1 = (bf16[512,512]{1,0:T(8,128)(2,1)S(1)}, f32[512,512]{1,0:T(8,128)S(1)}, bf16[512,512]{1,0:T(8,128)(2,1)S(1)}, f32[256,288]{1,0:T(8,128)S(1)}, bf16[256...) custom-call(s32[1]{0:T(128)} %bitcast.refs_0_.place_ref, ...), custom_call_target="tpu_custom_call" | custom-call | tf_op jit(solution)/shard_map/close/pallas_call | solution.py:45
  34.1 5.2 %collective-permute-done.10 = bf16[1,128,1024]{2,1,0:T(8,128)(2,1)S(1)} collective-permute-done((bf16[1,128,1024]{2,1,0:T(8,128)(2,1)S(1)}, bf16[1,128,1024]{2,1,0:T(8,128)(2,1)S(1)}, u32[]{:S(2)}, u32[]{:S(2)}) %collective-permute-start.10) | collective-permute-done | bytes 262176 | tf_op jit(solution)/shard_map/ppermute | solution.py:18
  39.5 1.9 %collective-permute-done.13.refs_4_ = bf16[512,512]{1,0:T(8,128)(2,1)S(1)} collective-permute-done((bf16[512,512]{1,0:T(8,128)(2,1)S(1)}, bf16[512,512]{1,0:T(8,128)(2,1)S(1)}, u32[]{:S(2)}, u32[]{:S(2)}) %collective-permute-start.13) | collective-permute-done | bytes 524320 | tf_op jit(solution)/shard_map/ppermute | solution.py:18
  41.3 0.4 split.1
  42.4 0.9 %collective-permute-done.16.refs_7_ = bf16[256,288]{1,0:T(8,128)(2,1)S(1)} collective-permute-done((bf16[256,288]{1,0:T(8,128)(2,1)S(1)}, bf16[256,288]{1,0:T(8,128)(2,1)S(1)}, u32[]{:S(2)}, u32[]{:S(2)}) %collective-permute-start.16) | collective-permute-done | bytes 147488 | tf_op jit(solution)/shard_map/ppermute | solution.py:18
  43.9 1.1 %collective-permute-start.18 = (bf16[2,128,416]{2,1,0:T(8,128)(2,1)S(1)}, bf16[2,128,416]{2,1,0:T(8,128)(2,1)S(1)}, u32[]{:S(2)}, u32[]{:S(2)}) collective-permute-start(bf16[2,128,416]{2,1,0:T(8,128)(2,1)S(1)} %get-tuple-element.108), channel_id=1, source_target_pairs={{0,4},{1,5},{2,6},{3,7},{4,0},{5,1},{6,2},{7,3},{8,12},{9,13},{10,... | collective-permute-start | bytes 638984 | tf_op jit(solution)/shard_map/ppermute | solution.py:18
  45.2 2.2 %result.1 = bf16[512,1024]{1,0:T(8,128)(2,1)} custom-call(s32[1]{0:T(128)} %bitcast.refs_0_.place_ref, bf16[512,512]{1,0:T(8,128)(2,1)S(1)} %get-tuple-element.83.near_ref, bf16[512,512]{1,0:T(8,128)(2,1)S(1)} %get-tuple-element.84.far_ref, bf16[512,1024]{1,0:T(8,128)(2,1)S(1)} %get-tuple-element.64.grad_ref, bf16[1024,1024]{1,0:T(8,128)(2,1)S(1)} %copy-done), custom_call_target="tpu_custom_call" | custom-call | tf_op jit(solution)/shard_map/result/pallas_call | solution.py:554
  47.4 7.0 %collective-permute-done.14 = bf16[2,128,896]{2,1,0:T(8,128)(2,1)S(1)} collective-permute-done((bf16[2,128,896]{2,1,0:T(8,128)(2,1)S(1)}, bf16[2,128,896]{2,1,0:T(8,128)(2,1)S(1)}, u32[]{:S(2)}, u32[]{:S(2)}) %collective-permute-start.14) | collective-permute-done | bytes 458784 | tf_op jit(solution)/shard_map/ppermute | solution.py:18
  54.6 1.1 %collective-permute-start.11 = (bf16[1,64,1024]{2,1,0:T(8,128)(2,1)S(1)}, bf16[1,64,1024]{2,1,0:T(8,128)(2,1)S(1)}, u32[]{:S(2)}, u32[]{:S(2)}) collective-permute-start(bf16[1,64,1024]{2,1,0:T(8,128)(2,1)S(1)} %get-tuple-element.90), channel_id=1, source_target_pairs={{0,2},{1,3},{2,0},{3,1},{4,6},{5,7},{6,4},{7,5},{8,10},{9,11},{10,... | collective-permute-start | bytes 393224 | tf_op jit(solution)/shard_map/ppermute | solution.py:18
  55.8 3.4 %collective-permute-start.19 = (bf16[1,128,416]{2,1,0:T(8,128)(2,1)S(1)}, bf16[1,128,416]{2,1,0:T(8,128)(2,1)S(1)}, u32[]{:S(2)}, u32[]{:S(2)}) collective-permute-start(bf16[1,128,416]{2,1,0:T(8,128)(2,1)S(1)} %get-tuple-element.110), channel_id=1, source_target_pairs={{0,8},{1,9},{2,10},{3,11},{4,12},{5,13},{6,14},{7,15},{8,0},{9,1},... | collective-permute-start | bytes 319496 | tf_op jit(solution)/shard_map/ppermute | solution.py:18
  59.2 5.0 %collective-permute-done.15.refs_2_ = bf16[2,64,896]{2,1,0:T(8,128)(2,1)S(1)} collective-permute-done((bf16[2,64,896]{2,1,0:T(8,128)(2,1)S(1)}, bf16[2,64,896]{2,1,0:T(8,128)(2,1)S(1)}, u32[]{:S(2)}, u32[]{:S(2)}) %collective-permute-start.15) | collective-permute-done | bytes 229408 | tf_op jit(solution)/shard_map/ppermute | solution.py:18
  64.4 2.1 %collective-permute-start.20 = (bf16[1,64,416]{2,1,0:T(8,128)(2,1)S(1)}, bf16[1,64,416]{2,1,0:T(8,128)(2,1)S(1)}, u32[]{:S(2)}, u32[]{:S(2)}) collective-permute-start(bf16[1,64,416]{2,1,0:T(8,128)(2,1)S(1)} %get-tuple-element.112), channel_id=1, source_target_pairs={{0,2},{1,3},{2,0},{3,1},{4,6},{5,7},{6,4},{7,5},{8,10},{9,11},{10,... | collective-permute-start | bytes 159752 | tf_op jit(solution)/shard_map/ppermute | solution.py:18
  66.5 0.7 %multiply_bitcast_fusion = f32[64,1024]{1,0:T(8,128)} fusion(f32[1,64,1024]{2,1,0:T(8,128)S(1)} %get-tuple-element.89, bf16[1,64,1024]{2,1,0:T(8,128)(2,1)S(1)} %collective-permute-done.11), kind=kLoop, calls=%fused_computation.1 | loop fusion | flops 196608 | bytes 655360 | tf_op jit(solution)/shard_map/mul | solution.py:642
  67.2 1.5 %collective-permute-done.20 = bf16[1,64,416]{2,1,0:T(8,128)(2,1)S(1)} collective-permute-done((bf16[1,64,416]{2,1,0:T(8,128)(2,1)S(1)}, bf16[1,64,416]{2,1,0:T(8,128)(2,1)S(1)}, u32[]{:S(2)}, u32[]{:S(2)}) %collective-permute-start.20) | collective-permute-done | bytes 53280 | tf_op jit(solution)/shard_map/ppermute | solution.py:18
  68.8 1.6 %collective-permute-done.21 = bf16[1,64,896]{2,1,0:T(8,128)(2,1)S(1)} collective-permute-done((bf16[1,64,896]{2,1,0:T(8,128)(2,1)S(1)}, bf16[1,64,896]{2,1,0:T(8,128)(2,1)S(1)}, u32[]{:S(2)}, u32[]{:S(2)}) %collective-permute-start.21) | collective-permute-done | bytes 114720 | tf_op jit(solution)/shard_map/ppermute | solution.py:18
  70.3 0.8 %last.1 = (f32[64,1024]{1,0:T(8,128)}, f32[64,288]{1,0:T(8,128)}) custom-call(s32[1]{0:T(128)} %bitcast.refs_0_.place_ref, f32[64,416]{1,0:T(8,128)S(1)} %bitcast.42, bf16[64,416]{1,0:T(8,128)(2,1)S(1)} %bitcast.45, f32[64,896]{1,0:T(8,128)S(1)} %bitcast.41, bf16[64,896]{1,0:T(8,128)(2,1)S(1)} %bitcast.44), custom_call_target="tpu_custom_call" | custom-call | tf_op jit(solution)/shard_map/last/pallas_call | solution.py:45
  (38 shorter events, 3.0 us)
Async XLA Ops:
  3.6 3.3 %collective-permute-start = (bf16[512,1024]{1,0:T(8,128)(2,1)S(1)}, bf16[512,1024]{1,0:T(8,128)(2,1)S(1)}, u32[]{:S(2)}, u32[]{:S(2)}) collective-permute-start(bf16[512,1024]{1,0:T(8,128)(2,1)S(1)} %get-tuple-element.61), channel_id=1, source_target_pairs={{0,1},{1,0},{2,3},{3,2},{4,5},{5,4},{6,7},{7,6},{8,9},{9,8},{10,11... | collective-permute-start | bytes 3145736 | tf_op jit(solution)/shard_map/ppermute | solution.py:18
  4.1 21.6 %collective-permute-start.3 = (bf16[2,4,128,256]{3,2,1,0:T(8,128)(2,1)S(1)}, bf16[2,4,128,256]{3,2,1,0:T(8,128)(2,1)S(1)}, u32[]{:S(2)}, u32[]{:S(2)}) collective-permute-start(bf16[2,4,128,256]{3,2,1,0:T(8,128)(2,1)S(1)} %get-tuple-element.76), channel_id=1, source_target_pairs={{0,2},{1,3},{2,0},{3,1},{4,6},{5,7},{6,4},{7,5},{8,10},{9,11},{10,... | collective-permute-start | bytes 1572872 | tf_op jit(solution)/shard_map/ppermute | solution.py:18
  6.7 9.6 %collective-permute-start.2 = (bf16[4,128,256]{2,1,0:T(8,128)(2,1)S(1)}, bf16[4,128,256]{2,1,0:T(8,128)(2,1)S(1)}, u32[]{:S(2)}, u32[]{:S(2)}) collective-permute-start(bf16[4,128,256]{2,1,0:T(8,128)(2,1)S(1)} %get-tuple-element.72), channel_id=1, source_target_pairs={{0,1},{1,0},{2,3},{3,2},{4,5},{5,4},{6,7},{7,6},{8,9},{9,8},{10,11... | collective-permute-start | bytes 786440 | tf_op jit(solution)/shard_map/ppermute | solution.py:18
  7.1 12.5 %collective-permute-start.9 = (bf16[1,128,1024]{2,1,0:T(8,128)(2,1)S(1)}, bf16[1,128,1024]{2,1,0:T(8,128)(2,1)S(1)}, u32[]{:S(2)}, u32[]{:S(2)}) collective-permute-start(bf16[1,128,1024]{2,1,0:T(8,128)(2,1)S(1)} %get-tuple-element.86), channel_id=1, source_target_pairs={{0,4},{1,5},{2,6},{3,7},{4,0},{5,1},{6,2},{7,3},{8,12},{9,13},{10,... | collective-permute-start | bytes 786440 | tf_op jit(solution)/shard_map/ppermute | solution.py:18
  9.7 12.7 %collective-permute-start.8 = (bf16[1,128,1024]{2,1,0:T(8,128)(2,1)S(1)}, bf16[1,128,1024]{2,1,0:T(8,128)(2,1)S(1)}, u32[]{:S(2)}, u32[]{:S(2)}) collective-permute-start(bf16[1,128,1024]{2,1,0:T(8,128)(2,1)S(1)} %get-tuple-element.62), channel_id=1, source_target_pairs={{0,4},{1,5},{2,6},{3,7},{4,0},{5,1},{6,2},{7,3},{8,12},{9,13},{10,... | collective-permute-start | bytes 786440 | tf_op jit(solution)/shard_map/ppermute | solution.py:18
  9.8 1.2 %collective-permute-start.1 = (bf16[16,1024]{1,0:T(8,128)(2,1)S(1)}, bf16[16,1024]{1,0:T(8,128)(2,1)S(1)}, u32[]{:S(2)}, u32[]{:S(2)}) collective-permute-start(bf16[16,1024]{1,0:T(8,128)(2,1)S(1)} %get-tuple-element.67), channel_id=1, source_target_pairs={{0,1},{1,0},{2,3},{3,2},{4,5},{5,4},{6,7},{7,6},{8,9},{9,8},{10,11... | collective-permute-start | bytes 98312 | tf_op jit(solution)/shard_map/ppermute | solution.py:18
  11.0 3.9 %copy-start.1 = (bf16[1,4,128,1024]{3,2,1,0:T(8,128)(2,1)S(1)}, bf16[1,4,128,1024]{3,2,1,0:T(8,128)(2,1)}, u32[]{:S(2)}) copy-start(bf16[1,4,128,1024]{3,2,1,0:T(8,128)(2,1)} %param.8) | copy-start | bytes 3145732
  11.0 3.9 %copy-start.2 = (bf16[1024,288]{0,1:T(8,128)(2,1)S(1)}, bf16[1024,288]{0,1:T(8,128)(2,1)}, u32[]{:S(2)}) copy-start(bf16[1024,288]{0,1:T(8,128)(2,1)} %param.12) | copy-start | bytes 1769476
  12.9 18.2 %collective-permute-start.6 = (bf16[144,1024]{1,0:T(8,128)(2,1)S(1)}, bf16[144,1024]{1,0:T(8,128)(2,1)S(1)}, u32[]{:S(2)}, u32[]{:S(2)}) collective-permute-start(bf16[144,1024]{1,0:T(8,128)(2,1)S(1)} %get-tuple-element.79), channel_id=1, source_target_pairs={{0,2},{1,3},{2,0},{3,1},{4,6},{5,7},{6,4},{7,5},{8,10},{9,11},{10,... | collective-permute-start | bytes 884744 | tf_op jit(solution)/shard_map/ppermute | solution.py:18
  16.3 14.8 %collective-permute-start.7 = (bf16[144,1024]{1,0:T(8,128)(2,1)S(1)}, bf16[144,1024]{1,0:T(8,128)(2,1)S(1)}, u32[]{:S(2)}, u32[]{:S(2)}) collective-permute-start(bf16[144,1024]{1,0:T(8,128)(2,1)S(1)} %get-tuple-element.80), channel_id=1, source_target_pairs={{2,4},{4,2},{3,5},{5,3},{6,8},{8,6},{7,9},{9,7},{10,12},{12,10},{1... | collective-permute-start | bytes 884744 | tf_op jit(solution)/shard_map/ppermute | solution.py:28
  22.6 16.7 %collective-permute-start.10 = (bf16[1,128,1024]{2,1,0:T(8,128)(2,1)S(1)}, bf16[1,128,1024]{2,1,0:T(8,128)(2,1)S(1)}, u32[]{:S(2)}, u32[]{:S(2)}) collective-permute-start(bf16[1,128,1024]{2,1,0:T(8,128)(2,1)S(1)} %get-tuple-element.88), channel_id=1, source_target_pairs={{0,8},{1,9},{2,10},{3,11},{4,12},{5,13},{6,14},{7,15},{8,0},{9,1},... | collective-permute-start | bytes 786440 | tf_op jit(solution)/shard_map/ppermute | solution.py:18
  25.7 1.4 %collective-permute-start.5 = (bf16[2,128,256]{2,1,0:T(8,128)(2,1)S(1)}, bf16[2,128,256]{2,1,0:T(8,128)(2,1)S(1)}, u32[]{:S(2)}, u32[]{:S(2)}) collective-permute-start(bf16[2,128,256]{2,1,0:T(8,128)(2,1)S(1)} %get-tuple-element.116), channel_id=1, source_target_pairs={{0,1},{1,0},{2,3},{3,2},{4,5},{5,4},{6,7},{7,6},{8,9},{9,8},{10,11... | collective-permute-start | bytes 393224 | tf_op jit(solution)/shard_map/ppermute | solution.py:18
  25.8 1.5 %collective-permute-start.4 = (bf16[2,128,256]{2,1,0:T(8,128)(2,1)S(1)}, bf16[2,128,256]{2,1,0:T(8,128)(2,1)S(1)}, u32[]{:S(2)}, u32[]{:S(2)}) collective-permute-start(bf16[2,128,256]{2,1,0:T(8,128)(2,1)S(1)} %get-tuple-element.117), channel_id=1, source_target_pairs={{0,1},{1,0},{2,3},{3,2},{4,5},{5,4},{6,7},{7,6},{8,9},{9,8},{10,11... | collective-permute-start | bytes 393224 | tf_op jit(solution)/shard_map/ppermute | solution.py:18
  34.0 5.4 %collective-permute-start.12 = (bf16[512,512]{1,0:T(8,128)(2,1)S(1)}, bf16[512,512]{1,0:T(8,128)(2,1)S(1)}, u32[]{:S(2)}, u32[]{:S(2)}) collective-permute-start(bf16[512,512]{1,0:T(8,128)(2,1)S(1)} %get-tuple-element.94), channel_id=1, source_target_pairs={{0,1},{1,0},{2,3},{3,2},{4,5},{5,4},{6,7},{7,6},{8,9},{9,8},{10,11... | collective-permute-start | bytes 1572872 | tf_op jit(solution)/shard_map/ppermute | solution.py:18
  39.4 2.0 %collective-permute-start.13 = (bf16[512,512]{1,0:T(8,128)(2,1)S(1)}, bf16[512,512]{1,0:T(8,128)(2,1)S(1)}, u32[]{:S(2)}, u32[]{:S(2)}) collective-permute-start(bf16[512,512]{1,0:T(8,128)(2,1)S(1)} %get-tuple-element.96), channel_id=1, source_target_pairs={{0,1},{1,0},{2,3},{3,2},{4,5},{5,4},{6,7},{7,6},{8,9},{9,8},{10,11... | collective-permute-start | bytes 1572872 | tf_op jit(solution)/shard_map/ppermute | solution.py:18
  41.8 12.6 %collective-permute-start.14 = (bf16[2,128,896]{2,1,0:T(8,128)(2,1)S(1)}, bf16[2,128,896]{2,1,0:T(8,128)(2,1)S(1)}, u32[]{:S(2)}, u32[]{:S(2)}) collective-permute-start(bf16[2,128,896]{2,1,0:T(8,128)(2,1)S(1)} %get-tuple-element.98), channel_id=1, source_target_pairs={{0,2},{1,3},{2,0},{3,1},{4,6},{5,7},{6,4},{7,5},{8,10},{9,11},{10,... | collective-permute-start | bytes 1376264 | tf_op jit(solution)/shard_map/ppermute | solution.py:18
  41.8 1.5 %collective-permute-start.16 = (bf16[256,288]{1,0:T(8,128)(2,1)S(1)}, bf16[256,288]{1,0:T(8,128)(2,1)S(1)}, u32[]{:S(2)}, u32[]{:S(2)}) collective-permute-start(bf16[256,288]{1,0:T(8,128)(2,1)S(1)} %get-tuple-element.105), channel_id=1, source_target_pairs={{0,1},{1,0},{2,3},{3,2},{4,5},{5,4},{6,7},{7,6},{8,9},{9,8},{10,11... | collective-permute-start | bytes 442376 | tf_op jit(solution)/shard_map/ppermute | solution.py:18
  42.0 1.6 %collective-permute-start.17 = (bf16[256,288]{1,0:T(8,128)(2,1)S(1)}, bf16[256,288]{1,0:T(8,128)(2,1)S(1)}, u32[]{:S(2)}, u32[]{:S(2)}) collective-permute-start(bf16[256,288]{1,0:T(8,128)(2,1)S(1)} %get-tuple-element.106), channel_id=1, source_target_pairs={{0,1},{1,0},{2,3},{3,2},{4,5},{5,4},{6,7},{7,6},{8,9},{9,8},{10,11... | collective-permute-start | bytes 442376 | tf_op jit(solution)/shard_map/ppermute | solution.py:18
  43.6 1.6 %copy-start = (bf16[1024,1024]{1,0:T(8,128)(2,1)S(1)}, bf16[1024,1024]{1,0:T(8,128)(2,1)}, u32[]{:S(2)}) copy-start(bf16[1024,1024]{1,0:T(8,128)(2,1)} %weight_ref.1) | copy-start | bytes 6291460
  43.9 11.8 %collective-permute-start.18 = (bf16[2,128,416]{2,1,0:T(8,128)(2,1)S(1)}, bf16[2,128,416]{2,1,0:T(8,128)(2,1)S(1)}, u32[]{:S(2)}, u32[]{:S(2)}) collective-permute-start(bf16[2,128,416]{2,1,0:T(8,128)(2,1)S(1)} %get-tuple-element.108), channel_id=1, source_target_pairs={{0,4},{1,5},{2,6},{3,7},{4,0},{5,1},{6,2},{7,3},{8,12},{9,13},{10,... | collective-permute-start | bytes 638984 | tf_op jit(solution)/shard_map/ppermute | solution.py:18
  54.5 9.7 %collective-permute-start.15 = (bf16[2,64,896]{2,1,0:T(8,128)(2,1)S(1)}, bf16[2,64,896]{2,1,0:T(8,128)(2,1)S(1)}, u32[]{:S(2)}, u32[]{:S(2)}) collective-permute-start(bf16[2,64,896]{2,1,0:T(8,128)(2,1)S(1)} %get-tuple-element.100), channel_id=1, source_target_pairs={{0,4},{1,5},{2,6},{3,7},{4,0},{5,1},{6,2},{7,3},{8,12},{9,13},{10,... | collective-permute-start | bytes 688136 | tf_op jit(solution)/shard_map/ppermute | solution.py:18
  54.6 11.9 %collective-permute-start.11 = (bf16[1,64,1024]{2,1,0:T(8,128)(2,1)S(1)}, bf16[1,64,1024]{2,1,0:T(8,128)(2,1)S(1)}, u32[]{:S(2)}, u32[]{:S(2)}) collective-permute-start(bf16[1,64,1024]{2,1,0:T(8,128)(2,1)S(1)} %get-tuple-element.90), channel_id=1, source_target_pairs={{0,2},{1,3},{2,0},{3,1},{4,6},{5,7},{6,4},{7,5},{8,10},{9,11},{10,... | collective-permute-start | bytes 393224 | tf_op jit(solution)/shard_map/ppermute | solution.py:18
  55.8 8.5 %collective-permute-start.19 = (bf16[1,128,416]{2,1,0:T(8,128)(2,1)S(1)}, bf16[1,128,416]{2,1,0:T(8,128)(2,1)S(1)}, u32[]{:S(2)}, u32[]{:S(2)}) collective-permute-start(bf16[1,128,416]{2,1,0:T(8,128)(2,1)S(1)} %get-tuple-element.110), channel_id=1, source_target_pairs={{0,8},{1,9},{2,10},{3,11},{4,12},{5,13},{6,14},{7,15},{8,0},{9,1},... | collective-permute-start | bytes 319496 | tf_op jit(solution)/shard_map/ppermute | solution.py:18
  64.3 6.1 %collective-permute-start.21 = (bf16[1,64,896]{2,1,0:T(8,128)(2,1)S(1)}, bf16[1,64,896]{2,1,0:T(8,128)(2,1)S(1)}, u32[]{:S(2)}, u32[]{:S(2)}) collective-permute-start(bf16[1,64,896]{2,1,0:T(8,128)(2,1)S(1)} %get-tuple-element.101), channel_id=1, source_target_pairs={{0,8},{1,9},{2,10},{3,11},{4,12},{5,13},{6,14},{7,15},{8,0},{9,1},... | collective-permute-start | bytes 344072 | tf_op jit(solution)/shard_map/ppermute | solution.py:18
  64.4 4.4 %collective-permute-start.20 = (bf16[1,64,416]{2,1,0:T(8,128)(2,1)S(1)}, bf16[1,64,416]{2,1,0:T(8,128)(2,1)S(1)}, u32[]{:S(2)}, u32[]{:S(2)}) collective-permute-start(bf16[1,64,416]{2,1,0:T(8,128)(2,1)S(1)} %get-tuple-element.112), channel_id=1, source_target_pairs={{0,2},{1,3},{2,0},{3,1},{4,6},{5,7},{6,4},{7,5},{8,10},{9,11},{10,... | collective-permute-start | bytes 159752 | tf_op jit(solution)/shard_map/ppermute | solution.py:18
